TPU v7x, 128 devices: a whole 4x4x4 slice. The times are simulated.
128 devices in a mesh: key: 16 (over y_lo, x, core), limb: 8 (over z, y_hi).
Axes of the slice: x: 4, y: 4 (y_hi: 2, y_lo: 2; y = y_hi * 2 + y_lo), z: 4, core: 2. Of those that a mesh axis runs over, the one named last changes fastest.
Arguments:
- cipher: float32 [16, 2, 24, 32768], P('key', None, 'limb'), may hold values from -6 to 6
- key_main: bfloat16 [16, 2, 3, 24, 32768], P('key', None, None, 'limb'), may hold values from -4 to 4
- key_special: bfloat16 [16, 2, 3, 8, 32768], P('key', None, None, 'limb'), may hold values from -4 to 4
- diag_main: bfloat16 [16, 24, 32768], P('key', 'limb'), may hold values from -5 to 5
- diag_special: bfloat16 [16, 8, 32768], P('key', 'limb'), may hold values from -5 to 5
- perms: int32 [16, 32768], P('key'), may hold values from 0 to 32767, each once within a row
- tw_exp: int32 [32], replicated, may hold values from 1 to 32767
- up_conv: float32 [24, 32], replicated, may hold values from -2 to 2
- down_conv: float32 [8, 24], replicated, may hold values from -2 to 2
Outputs:
- rotated: float32 [16, 2, 24, 32768], P('key', None, 'limb')
Inputs may be any that keep to these rules, and one draw needn't show every extreme that they name: Each row of perms holds every coefficient position once.
All inputs are finite; a program needn't handle non-finite values.
Results may differ from a plain program's by a relative error of at most 0.0003.
Values may be sent and summed in bfloat16 or wider, within the bound.
No kernel may reach another device: no remote copies, remote signals or barrier semaphores. Data moves between devices by JAX's collectives and lax.ppermute only.
A program may use at most 640 MiB of HBM per device.

v0:
```python
import math

import jax
import jax.numpy as jnp
from jax import lax
from jax.sharding import PartitionSpec as P

A = 128
DNUM = 3
ROTS = 2


HIGHEST_PRECISION = lax.Precision.HIGHEST


def from_behind(value, axis, steps):
    count = lax.axis_size(axis)
    pairs = [(source, (source + steps) % count) for source in range(count)]
    return lax.ppermute(value, axis, pairs)


def hartley(extent):
    indices = jnp.arange(extent, dtype=jnp.int32)
    phases = indices[:, None] * indices[None, :] % extent
    angles = phases.astype(jnp.float32) * (2.0 * math.pi / extent)
    return (jnp.cos(angles) + jnp.sin(angles)) / math.sqrt(extent)


def twiddle(exponents, row_count, col_count, length):
    row_index = jnp.arange(row_count, dtype=jnp.int32)
    col_index = jnp.arange(col_count, dtype=jnp.int32)
    product = row_index[:, None] * col_index[None, :] % length
    phases = product[None, :, :] * exponents[:, None, None] % length
    angles = phases.astype(jnp.float32) * (2.0 * math.pi / length)
    return 1.0 + 0.5 * jnp.cos(angles)


def forward(values, exponents, row_count):
    layout = values.shape
    length = layout[-1]
    col_count = length // row_count
    blocks = values.reshape(layout[:-1] + (row_count, col_count)) * twiddle(
        exponents, row_count, col_count, length
    )
    halfway = jnp.einsum("ia,...ab->...ib", hartley(row_count), blocks, precision=HIGHEST_PRECISION)
    finished = jnp.einsum(
        "...ib,bj->...ij", halfway, hartley(col_count), precision=HIGHEST_PRECISION
    )
    return finished.reshape(layout)


def inverse(values, exponents, row_count):
    layout = values.shape
    length = layout[-1]
    col_count = length // row_count
    blocks = values.reshape(layout[:-1] + (row_count, col_count))
    halfway = jnp.einsum("ia,...ab->...ib", hartley(row_count), blocks, precision=HIGHEST_PRECISION)
    finished = jnp.einsum(
        "...ib,bj->...ij", halfway, hartley(col_count), precision=HIGHEST_PRECISION
    )
    finished = finished / twiddle(exponents, row_count, col_count, length)
    return finished.reshape(layout)


def digit_weights(up_conv, digit_count):
    limb_count = up_conv.shape[0]
    group_of = jnp.arange(limb_count, dtype=jnp.int32) * digit_count // limb_count
    members = (group_of[:, None] == jnp.arange(digit_count, dtype=jnp.int32)[None, :]).astype(
        jnp.float32
    )
    return members[:, :, None] * up_conv[:, None, :]


def lower_once(main_part, special_part, exps_main, exps_spec, down_conv):
    lowered = inverse(special_part, exps_spec, A)
    columns = lax.all_to_all(lowered, "limb", split_axis=2, concat_axis=1, tiled=True)
    returned = jnp.einsum("pkn,kl->pln", columns, down_conv, precision=HIGHEST_PRECISION)
    returned = lax.all_to_all(returned, "limb", split_axis=1, concat_axis=2, tiled=True)
    return main_part - forward(returned, exps_main, A)


def switch(first_poly, ext_main, ext_spec, key_main, key_spec, diag_main, diag_spec, mapping):
    perm_main = jnp.take(ext_main, mapping, axis=2)
    perm_spec = jnp.take(ext_spec, mapping, axis=2)
    base_part = jnp.take(first_poly, mapping, axis=1)
    sum_main = jnp.sum(key_main.astype(jnp.float32) * perm_main[None], axis=1)
    sum_spec = jnp.sum(key_spec.astype(jnp.float32) * perm_spec[None], axis=1)
    sum_main = sum_main + jnp.stack([base_part, jnp.zeros_like(base_part)])
    return (
        diag_main.astype(jnp.float32)[None] * sum_main,
        diag_spec.astype(jnp.float32)[None] * sum_spec,
    )


def on_device(
    cipher, key_main, key_special, diag_main, diag_special, perms, tw_exp, up_conv, down_conv
):
    limb_dev = cipher.shape[2]
    spec_dev = key_special.shape[3]
    main_count = up_conv.shape[0]
    length = cipher.shape[3]
    lead = lax.axis_index("limb")
    exps_main = lax.dynamic_slice_in_dim(tw_exp, lead * limb_dev, limb_dev)
    exps_spec = lax.dynamic_slice_in_dim(tw_exp, main_count + lead * spec_dev, spec_dev)
    first_poly = cipher[0, 0]
    coefficients = inverse(cipher[0, 1], exps_main, A)
    columns = lax.all_to_all(coefficients, "limb", split_axis=1, concat_axis=0, tiled=True)
    raised = jnp.einsum(
        "ln,ldm->dmn", columns, digit_weights(up_conv, DNUM), precision=HIGHEST_PRECISION
    )
    rise_main, rise_spec = (
        lax.all_to_all(raised[:, :main_count], "limb", split_axis=1, concat_axis=2, tiled=True),
        lax.all_to_all(raised[:, main_count:], "limb", split_axis=1, concat_axis=2, tiled=True),
    )
    ext_main = forward(rise_main, exps_main, A)
    ext_spec = forward(rise_spec, exps_spec, A)
    summed = jnp.zeros((2, limb_dev + spec_dev, length), jnp.float32)
    for rotation in range(ROTS):
        if rotation > 0:
            first_poly, ext_main, ext_spec, summed = from_behind(
                (first_poly, ext_main, ext_spec, summed), "key", 1
            )
        part_main, part_spec = switch(
            first_poly,
            ext_main,
            ext_spec,
            key_main[0],
            key_special[0],
            diag_main[0],
            diag_special[0],
            perms[0],
        )
        result_sum = summed + jnp.concatenate([part_main, part_spec], axis=1)
        summed = result_sum
    summed = from_behind(summed, "key", 1 - ROTS)
    result = lower_once(summed[:, :limb_dev], summed[:, limb_dev:], exps_main, exps_spec, down_conv)
    return result[None]


def solution(mesh):
    placed = (
        P("key", None, "limb", None),
        P("key", None, None, "limb", None),
        P("key", None, None, "limb", None),
        P("key", "limb", None),
        P("key", "limb", None),
        P("key", None),
        P(),
        P(),
        P(),
    )
    return jax.shard_map(
        on_device,
        mesh=mesh,
        in_specs=placed,
        out_specs=P("key", None, "limb", None),
        check_vma=False,
    )
```

profile of v0, /device:TPU:0, one launch (start us, length us, event | category | flops | bytes accessed | tf_op | source)
XLA Modules:
  0.0 2257.5 jit_solution(11000643237898477479)
XLA Ops:
  0.1 3.1 fusion.116
  4.7 2.8 convolution_divide_fusion
  7.6 1.1 copy.124
  8.7 8.0 all-to-all-start
  16.7 8.8 copy.178
  25.5 9.8 copy.144
  37.7 114.8 %gather_fusion.1 = f32[32768,3]{1,0:T(8,128)} fusion(f32[3,32768]{0,1:T(8,128)} %bitcast.136, s32[32768]{0:T(1024)S(1)} %fusion.48), kind=kCustom, calls=%fused_computation.1.clone | custom fusion | bytes 917504 | tf_op jit(solution)/shard_map/jit(_take)/gather | solution.py:85
  152.5 9.5 copy.133
  162.2 1.5 fusion.60
  163.8 1.1 copy.134
  164.8 7.7 all-to-all-start.2
  172.6 1.2 fusion.44
  173.8 1.5 fusion.16
  175.4 1.9 copy.125
  177.4 9.1 copy.145
  186.4 114.8 %gather_fusion.4 = f32[32768,3]{1,0:T(8,128)} fusion(f32[3,32768]{0,1:T(8,128)} %copy.145, s32[32768]{0:T(1024)S(1)} %fusion.48), kind=kCustom, calls=%fused_computation.4.clone | custom fusion | bytes 917504 | tf_op jit(solution)/shard_map/jit(_take)/gather | solution.py:85
  301.2 9.8 copy.146
  311.0 7.2 all-to-all-start.1
  318.2 1.0 copy.135
  319.2 1.1 reshape.354
  321.2 2.5 fusion.31
  323.7 1.2 reshape.356
  325.0 1.2 copy.147
  327.0 1.4 select_bitcast_fusion.2
  328.4 1.0 stack.14
  329.4 1.0 stack.12
  330.5 8.5 copy.138
  339.0 114.8 %gather_fusion.2 = f32[32768,3]{1,0:T(8,128)} fusion(f32[3,32768]{0,1:T(8,128)} %bitcast.139, s32[32768]{0:T(1024)S(1)} %fusion.48), kind=kCustom, calls=%fused_computation.2.clone | custom fusion | bytes 917504 | tf_op jit(solution)/shard_map/jit(_take)/gather | solution.py:84
  453.8 9.3 copy.148
  463.0 114.8 %gather_fusion.5 = f32[32768,3]{1,0:T(8,128)} fusion(f32[3,32768]{0,1:T(8,128)} %bitcast.140, s32[32768]{0:T(1024)S(1)} %fusion.48), kind=kCustom, calls=%fused_computation.5.clone | custom fusion | bytes 917504 | tf_op jit(solution)/shard_map/jit(_take)/gather | solution.py:84
  577.8 22.8 %fusion.1 = (f32[3,32768]{0,1:T(8,128)}, f32[3,32768]{0,1:T(8,128)}) fusion(f32[32768,3]{1,0:T(8,128)} %gather_fusion.2, pred[32768]{0:T(1024)(128)(4,1)S(1)} %compare_and_fusion, f32[32768,3]{1,0:T(8,128)} %gather_fusion.5), kind=kLoop, calls=%fused_computation.11 | loop fusion | flops 196608 | bytes 1605632 | tf_op jit(solution)/shard_map/mul | solution.py:87
  600.6 9.5 copy.149
  610.1 9.5 copy.139
  619.6 2.9 fusion.6
  623.3 2.2 convolution_bitcast_fusion.1
  625.5 3.0 fusion.27
  629.2 1.1 collective-permute-start.1
  630.4 2.0 bitcast_multiply_fusion
  632.4 1.0 copy.141
  633.4 39.8 %copy.130 = f32[3,3,32768]{1,0,2:T(4,128)} copy(f32[3,3,32768]{2,1,0:T(4,128)S(1)} %reshape.353) | data formatting | bytes 2359296 | tf_op jit(solution)/shard_map/reshape | solution.py:49
  673.2 521.5 %gather_fusion = f32[32768,3,3]{2,1,0:T(4,128)} fusion(f32[3,3,32768]{1,0,2:T(4,128)} %copy.130, s32[32768]{0:T(1024)S(1)} %fusion.48), kind=kCustom, calls=%fused_computation.clone | custom fusion | bytes 2490368 | tf_op jit(solution)/shard_map/jit(_take)/gather | solution.py:83
  1194.7 39.8 %copy.142 = f32[3,3,32768]{1,0,2:T(4,128)} copy(f32[3,3,32768]{2,1,0:T(4,128)S(1)} %collective-permute-done.1) | data formatting | bytes 2359296 | tf_op jit(solution)/shard_map/ppermute | solution.py:19
  1234.5 521.5 %gather_fusion.3 = f32[32768,3,3]{2,1,0:T(4,128)} fusion(f32[3,3,32768]{1,0,2:T(4,128)} %copy.142, s32[32768]{0:T(1024)S(1)} %fusion.48), kind=kCustom, calls=%fused_computation.3.clone | custom fusion | bytes 2490368 | tf_op jit(solution)/shard_map/jit(_take)/gather | solution.py:83
  1756.1 117.0 %select_bitcast_fusion.1 = (f32[3,3,32768]{1,0,2:T(4,128)}, f32[3,3,32768]{1,0,2:T(4,128)}) fusion(f32[32768,3,3]{2,1,0:T(4,128)} %gather_fusion, pred[32768]{0:T(1024)(128)(4,1)S(1)} %copy-done.5, f32[32768,3,3]{2,1,0:T(4,128)} %gather_fusion.3), kind=kLoop, calls=%fused_computation.7 | loop fusion | flops 589824 | bytes 4751360 | tf_op jit(solution)/shard_map/jit(_take)/select_n | solution.py:83
  1873.0 45.2 %copy.143 = f32[3,3,32768]{2,1,0:T(4,128)S(1)} copy(f32[3,3,32768]{1,0,2:T(4,128)} %get-tuple-element.21) | data formatting | bytes 2359296 | tf_op jit(solution)/shard_map/jit(_take)/select_n | solution.py:83
  1918.3 45.3 %copy.131 = f32[3,3,32768]{2,1,0:T(4,128)S(1)} copy(f32[3,3,32768]{1,0,2:T(4,128)} %get-tuple-element.20) | data formatting | bytes 2359296 | tf_op jit(solution)/shard_map/jit(_take)/select_n | solution.py:83
  1963.5 4.9 fusion.3
  1968.4 2.2 add_multiply_fusion
  1971.2 1.4 pad_maximum_fusion
  1973.3 1.2 copy.151
  1975.1 13.9 collective-permute-done
  1990.1 12.3 collective-permute-done.4
  2004.0 1.6 convolution_divide_fusion.1
  2005.6 8.6 copy.175
  2014.6 146.5 %reduce.6 = f32[32768,2]{1,0:T(8,128)} reduce(f32[32768,1,2]{2,1,0:T(1,128)} %bitcast.137, f32[]{:T(128)} %broadcast.542), dimensions={1}, to_apply=%bitcast.126.reduce_sub_computation | reduce | bytes 524292
  2161.2 13.7 reshape.449
  2174.9 15.8 all_to_all.70
  2190.7 1.3 reduce.7
  2192.0 31.5 %reshape.450 = f32[32768,1,2]{2,1,0:T(1,128)} reshape(f32[8,8192]{1,0:T(8,128)S(1)} %reduce.7) | data formatting | bytes 524288
  2223.5 9.7 copy.176
  2234.7 15.6 all_to_all.71
  2250.9 1.6 convolution_bitcast_fusion.2
  2252.5 2.4 fusion.8
  2255.4 1.7 fusion.7
  (65 shorter events, 15.3 us)
Async XLA Ops:
  0.0 2233.2 %copy-start = (f32[8,24]{1,0:T(8,128)S(1)}, f32[8,24]{1,0:T(8,128)}, u32[]{:S(2)}) copy-start(f32[8,24]{1,0:T(8,128)} %param.23) | copy-start | bytes 2308
  8.7 153.3 %all-to-all-start = ((f32[3,8,4096]{2,0,1:T(4,128)}), f32[3,8,4096]{2,0,1:T(4,128)S(1)}, u32[]{:S(2)}, u32[]{:S(2)}) async-start(f32[3,8,4096]{2,0,1:T(4,128)} %copy.124), calls=%async_computation | async-start | bytes 1048576 | tf_op jit(solution)/shard_map/all_to_all | solution.py:107
  16.7 18.7 copy-start.8
  16.7 18.7 copy-start.9
  16.7 19.6 copy-start.12
  16.7 20.2 copy-start.10
  25.5 136.7 %copy-start.11 = (f32[24,32]{1,0:T(8,128)S(1)}, f32[24,32]{1,0:T(8,128)}, u32[]{:S(2)}) copy-start(f32[24,32]{1,0:T(8,128)} %param.22) | copy-start | bytes 9220
  35.3 142.0 %collective-permute-start.2 = (f32[3,32768]{1,0:T(4,128)}, f32[3,32768]{1,0:T(4,128)}, u32[]{:S(2)}, u32[]{:S(2)}) collective-permute-start(f32[3,32768]{1,0:T(4,128)} %copy.144), channel_id=1, source_target_pairs={{0,8},{8,16},{16,24},{24,32},{32,40},{40,48},{48,56},{56,64},{64,7... | collective-permute-start | bytes 1179656 | tf_op jit(solution)/shard_map/ppermute | solution.py:19
  36.3 541.5 %copy-start.4 = (pred[32768]{0:T(1024)(128)(4,1)}, pred[32768]{0:T(1024)(128)(4,1)S(1)}, u32[]{:S(2)}) copy-start(pred[32768]{0:T(1024)(128)(4,1)S(1)} %compare_and_fusion) | copy-start | bytes 98308
  164.8 146.2 %all-to-all-start.2 = ((f32[3,8,4096]{2,0,1:T(4,128)}), f32[3,8,4096]{2,0,1:T(4,128)S(1)}, u32[]{:S(2)}, u32[]{:S(2)}) async-start(f32[3,8,4096]{2,0,1:T(4,128)} %copy.134), calls=%async_computation.2 | async-start | bytes 1048576 | tf_op jit(solution)/shard_map/all_to_all | solution.py:113
  173.8 146.5 %copy-start.6 = (f32[128,256]{1,0:T(8,128)}, f32[128,256]{1,0:T(8,128)S(1)}, u32[]{:S(2)}) copy-start(f32[128,256]{1,0:T(8,128)S(1)} %fusion.44) | copy-start | bytes 393220
  175.3 448.0 %copy-start.1 = (f32[3,128,256]{2,1,0:T(8,128)}, f32[3,128,256]{2,1,0:T(8,128)S(1)}, u32[]{:S(2)}) copy-start(f32[3,128,256]{2,1,0:T(8,128)S(1)} %fusion.16) | copy-start | bytes 1179652
  311.0 311.4 %all-to-all-start.1 = ((f32[3,24,4096]{2,0,1:T(4,128)}), f32[3,24,4096]{2,0,1:T(4,128)S(1)}, u32[]{:S(2)}, u32[]{:S(2)}) async-start(f32[3,24,4096]{2,0,1:T(4,128)} %copy.125), calls=%async_computation.1 | async-start | bytes 3145728 | tf_op jit(solution)/shard_map/all_to_all | solution.py:112
  326.1 127.6 %collective-permute-start.3 = (f32[3,1,32768]{2,1,0:T(1,128)}, f32[3,1,32768]{2,1,0:T(1,128)}, u32[]{:S(2)}, u32[]{:S(2)}) collective-permute-start(f32[3,1,32768]{2,1,0:T(1,128)} %copy.147), channel_id=1, source_target_pairs={{0,8},{8,16},{16,24},{24,32},{32,40},{40,48},{48,56},{56,64},{64,7... | collective-permute-start | bytes 1179656 | tf_op jit(solution)/shard_map/ppermute | solution.py:19
  629.2 565.5 %collective-permute-start.1 = (f32[3,3,32768]{2,1,0:T(4,128)S(1)}, f32[3,3,32768]{2,1,0:T(4,128)S(1)}, u32[]{:S(2)}, u32[]{:S(2)}) collective-permute-start(f32[3,3,32768]{2,1,0:T(4,128)S(1)} %reshape.353), channel_id=1, source_target_pairs={{0,8},{8,16},{16,24},{24,32},{32,40},{40,48},{48,56},{56,64},{64,7... | collective-permute-start | bytes 3538952 | tf_op jit(solution)/shard_map/ppermute | solution.py:19
  1194.7 561.4 %copy-start.5 = (pred[32768]{0:T(1024)(128)(4,1)S(1)}, pred[32768]{0:T(1024)(128)(4,1)}, u32[]{:S(2)}) copy-start(pred[32768]{0:T(1024)(128)(4,1)} %copy-done.4) | copy-start | bytes 98308
  1918.3 50.2 %copy-start.3 = (f32[1,3,32768]{2,0,1:T(1,128)S(1)}, f32[1,3,32768]{2,0,1:T(1,128)}, u32[]{:S(2)}) copy-start(f32[1,3,32768]{2,0,1:T(1,128)} %stack.14) | copy-start | bytes 1179652
  1963.5 40.5 %copy-start.7 = (f32[128,256]{1,0:T(8,128)S(1)}, f32[128,256]{1,0:T(8,128)}, u32[]{:S(2)}) copy-start(f32[128,256]{1,0:T(8,128)} %copy-done.6) | copy-start | bytes 393220
  1972.6 16.4 collective-permute-start
  1989.6 12.8 collective-permute-start.4
  2192.0 58.9 %copy-start.2 = (f32[3,128,256]{2,1,0:T(8,128)S(1)}, f32[3,128,256]{2,1,0:T(8,128)}, u32[]{:S(2)}) copy-start(f32[3,128,256]{2,1,0:T(8,128)} %copy-done.1) | copy-start | bytes 1179652
where the time goes:
time: 2290 us; the launch traced here: 2260 us
  local copies, waits for them, and re-layouts  1840 us (80%)
  other arithmetic  309 us (13%)
  blocking collectives  31.4 us (1%)
  waiting for transfers between devices  26.3 us (1%)
  starting transfers between devices  26.2 us (1%)
    gather x2, local copies, waits for them, and re-layouts, switch(): perm_main = jnp.take(ext_main, mapping, axis=2)  1040 us
    gather x4, local copies, waits for them, and re-layouts, switch(): base_part = jnp.take(first_poly, mapping, axis=1)  249 us
    gather x2, local copies, waits for them, and re-layouts, switch(): perm_spec = jnp.take(ext_spec, mapping, axis=2)  230 us
    unnamed x1, other arithmetic  147 us
    select_n x1, other arithmetic, switch(): perm_main = jnp.take(ext_main, mapping, axis=2)  117 us
    select_n x2, local copies, waits for them, and re-layouts, switch(): perm_main = jnp.take(ext_main, mapping, axis=2)  90.5 us
    ppermute x3, local copies, waits for them, and re-layouts, from_behind(): return lax.ppermute(value, axis, pairs)  58.2 us
    unnamed x30, local copies, waits for them, and re-layouts  54.6 us
  transfers between devices with their start and end apart: 8, of which 2 were waited for; matrix products, arithmetic and copies ran while one was open for 51% of the time, Pallas kernels for 0%

commit v1 on v0

v1 whole, which is shorter than its diff:
```python
import functools
import math

import jax
import jax.numpy as jnp
import numpy as np
from jax import lax
from jax.experimental import pallas as pl
from jax.experimental.pallas import tpu as pltpu
from jax.sharding import PartitionSpec as P

A = 128
B = 256
NRING = A * B
DNUM = 3
LIMBS = 8
JS = 4
CHUNK = A // LIMBS
HIGHEST = lax.Precision.HIGHEST
MIB = 1 << 20

VMEM = pl.BlockSpec(memory_space=pltpu.VMEM)
SMEM = pl.BlockSpec(memory_space=pltpu.SMEM)


def hartley(extent):
    indices = np.arange(extent)
    angles = (indices[:, None] * indices[None, :] % extent) * (2.0 * math.pi / extent)
    return ((np.cos(angles) + np.sin(angles)) / math.sqrt(extent)).astype(np.float32)


def twiddle(exponents):
    product = jnp.arange(A, dtype=jnp.int32)[:, None] * jnp.arange(B, dtype=jnp.int32)[None, :] % NRING
    phases = product[None, :, :] * exponents[:, None, None] % NRING
    return 1.0 + 0.5 * jnp.cos(phases.astype(jnp.float32) * (2.0 * math.pi / NRING))


def params(mib):
    return pltpu.CompilerParams(vmem_limit_bytes=mib * MIB)


def both_sides(h_a, block, h_b):
    half = jnp.dot(h_a, block, precision=HIGHEST, preferred_element_type=jnp.float32)
    return jnp.dot(half, h_b, precision=HIGHEST, preferred_element_type=jnp.float32)


def inverse_kernel(cipher_ref, tw_ref, ha_ref, hb_ref, out_ref, x_ref):
    def spread(step, _):
        rows = [cipher_ref[0, 0, :, pl.ds(pl.multiple_of((step * 8 + k) * B, B), B)] for k in range(8)]
        for limb in range(JS - 1):
            x_ref[limb, pl.ds(pl.multiple_of(step * 8, 8), 8), :] = jnp.concatenate([row[limb : limb + 1] for row in rows], axis=0)
        return 0

    lax.fori_loop(0, A // 8, spread, 0)
    for limb in range(JS - 1):
        done = both_sides(ha_ref[...], x_ref[limb], hb_ref[...]) / tw_ref[limb]
        for to in range(LIMBS):
            out_ref[to, limb * CHUNK : (limb + 1) * CHUNK, :] = done[to * CHUNK : (to + 1) * CHUNK]


def raise_kernel(up_ref, x_ref, out_ref):
    def body(to, _):
        for digit in range(DNUM):
            for j in range(JS):
                m = to * (JS - 1) + j if j < JS - 1 else LIMBS * (JS - 1) + to
                total = None
                for limb in range(digit * LIMBS, (digit + 1) * LIMBS):
                    at = limb % (JS - 1) * CHUNK
                    term = up_ref[limb, m] * x_ref[limb // (JS - 1), at : at + CHUNK, :]
                    total = term if total is None else total + term
                at = (digit * JS + j) * CHUNK
                out_ref[to, at : at + CHUNK, :] = total
        return 0

    lax.fori_loop(0, LIMBS, body, 0)


def pack_kernel(km_ref, ks_ref, dm_ref, ds_ref, out_ref, rows_ref):
    for p in range(2):
        for digit in range(DNUM):
            at = p * 16 + digit * JS
            rows_ref[at : at + JS - 1, :] = km_ref[0, p, digit].astype(jnp.float32)
            rows_ref[at + JS - 1 : at + JS, :] = ks_ref[0, p, digit].astype(jnp.float32)
        at = p * 16 + DNUM * JS
        rows_ref[at : at + JS - 1, :] = dm_ref[0].astype(jnp.float32)
        rows_ref[at + JS - 1 : at + JS, :] = ds_ref[0].astype(jnp.float32)
    out_ref[...] = rows_ref[...].astype(jnp.bfloat16)


def switch_kernel(
    idx0_ref, idx1_ref, x_ref, base_ref, tw_ref, ha_ref, hb_ref, k0_ref, k1_ref,
    sum_ref, low_ref, rows_ref, ext_ref, got0_ref, got1_ref, spec_ref,
):
    channels = DNUM * JS
    for ch in range(channels):
        at = ch * CHUNK
        block = jnp.concatenate([x_ref[src, at : at + CHUNK, :] for src in range(LIMBS)], axis=0)
        done = both_sides(ha_ref[...], block * tw_ref[ch % JS], hb_ref[...])
        rows_ref[0, pl.ds(ch, A, stride=16), :] = done[:, :128]
        rows_ref[1, pl.ds(ch, A, stride=16), :] = done[:, 128:]

    def first(i, _):
        for half in range(2):
            lanes = pl.ds(pl.multiple_of(i * B + half * 128, 128), 128)
            rows_ref[half, pl.ds(pl.multiple_of(i * 16 + 8, 8) + 4, 3), :] = base_ref[0, 0, :, lanes]
            rows_ref[half, pl.ds(pl.multiple_of(i * 16 + 8, 8) + 7, 1), :] = jnp.zeros((1, 128), jnp.float32)
        return 0

    lax.fori_loop(0, A, first, 0)

    def turn(step, _):
        for k in range(4):
            i = step * 4 + k
            for half in range(2):
                part = rows_ref[half, pl.ds(pl.multiple_of(i * 16, 16), 16), :]
                ext_ref[pl.ds(pl.multiple_of(i * B + half * 128, 128), 128), :] = jnp.concatenate([part] * 8, axis=0).T
        return 0

    lax.fori_loop(0, A // 4, turn, 0)

    group = lax.broadcasted_iota(jnp.int32, (1, 128), 1) // 16

    def gather(idx_ref, got_ref):
        def body(step, _):
            blk = step // 8
            r0 = step % 8 * 16
            for r in range(16):
                row = None
                for g in range(8):
                    one = ext_ref[pl.ds(idx_ref[blk * 1024 + r0 + (g * 128 + r)], 1), :]
                    row = one if row is None else jnp.where(group == g, one, row)
                got_ref[step, r : r + 1, :] = row
            return 0

        lax.fori_loop(0, NRING // 128, body, 0)

    gather(idx0_ref, got0_ref)
    gather(idx1_ref, got1_ref)

    sub = lax.broadcasted_iota(jnp.int32, (8, 128), 0)
    low_half = sub < JS
    base_gain = jnp.where((sub >= JS) & (sub < 2 * JS - 1), 1.0, 0.0).astype(jnp.float32)

    def combine(step, _):
        lines = [[[], []], [[], []]]
        for k in range(16):
            blk, g = step * 2 + k // 8, k % 8
            if g == 0:
                at8 = pl.ds(blk * 8, 8)
                turned = [ref[at8].reshape(128, 128).T for ref in (got0_ref, got1_ref)]
            lanes = pl.ds(pl.multiple_of(step * 2048 + k * 128, 128), 128)
            sums = [None, None]
            for s, k_ref in enumerate((k0_ref, k1_ref)):
                keys = k_ref[:, lanes].astype(jnp.float32)
                upper = turned[s][g * 16 : g * 16 + 8]
                lower = turned[s][g * 16 + 8 : g * 16 + 16]
                tail = keys[8:16]
                diag = jnp.where(low_half, jnp.roll(tail, JS, axis=0), tail)
                for p in range(2):
                    gain = jnp.where(low_half, keys[p * 16 + 8 : p * 16 + 16], base_gain if p == 0 else 0.0)
                    part = diag * (keys[p * 16 : p * 16 + 8] * upper + gain * lower)
                    sums[p] = part if sums[p] is None else sums[p] + part
            folded = [value + jnp.roll(value, JS, axis=0) for value in sums]
            both = jnp.where(low_half, folded[0], folded[1])
            sum_ref[:, lanes] = both
            for p in range(2):
                lines[p][k % 2].append(both[p * JS + JS - 1 : p * JS + JS])
        at = pl.ds(pl.multiple_of(step * 8, 8), 8)
        for p in range(2):
            for half in range(2):
                spec_ref[p, at, half * 128 : (half + 1) * 128] = jnp.concatenate(lines[p][half], axis=0)
        return 0

    lax.fori_loop(0, NRING // 2048, combine, 0)

    for p in range(2):
        done = both_sides(ha_ref[...], spec_ref[p], hb_ref[...]) / tw_ref[JS - 1]
        for to in range(LIMBS):
            low_ref[to, p * CHUNK : (p + 1) * CHUNK, :] = done[to * CHUNK : (to + 1) * CHUNK]


def lower_kernel(down_ref, x_ref, out_ref):
    def body(to, _):
        for p in range(2):
            for j in range(JS - 1):
                total = None
                for k in range(LIMBS):
                    term = down_ref[k, to * (JS - 1) + j] * x_ref[k, p * CHUNK : (p + 1) * CHUNK, :]
                    total = term if total is None else total + term
                at = (p * (JS - 1) + j) * CHUNK
                out_ref[to, at : at + CHUNK, :] = total
        return 0

    lax.fori_loop(0, LIMBS, body, 0)


def finish_kernel(x_ref, sum_ref, tw_ref, ha_ref, hb_ref, out_ref, rows_ref):
    for p in range(2):
        for j in range(JS - 1):
            at = (p * (JS - 1) + j) * CHUNK
            block = jnp.concatenate([x_ref[src, at : at + CHUNK, :] for src in range(LIMBS)], axis=0)
            done = both_sides(ha_ref[...], block * tw_ref[j], hb_ref[...])
            rows_ref[0, pl.ds(p * JS + j, A, stride=8), :] = done[:, :128]
            rows_ref[1, pl.ds(p * JS + j, A, stride=8), :] = done[:, 128:]

    def body(i, _):
        for half in range(2):
            lanes = pl.ds(pl.multiple_of(i * B + half * 128, 128), 128)
            rest = sum_ref[:, lanes] - rows_ref[half, pl.ds(pl.multiple_of(i * 8, 8), 8), :]
            for p in range(2):
                out_ref[0, p, :, lanes] = rest[p * JS : p * JS + JS - 1]
        return 0

    lax.fori_loop(0, A, body, 0)


def exchange(value):
    return lax.all_to_all(value, "limb", split_axis=0, concat_axis=0, tiled=True)


def f32(*shape):
    return jax.ShapeDtypeStruct(shape, jnp.float32)


def on_device(cipher, key_main, key_special, diag_main, diag_special, perms, tw_exp, up_conv, down_conv):
    lead = lax.axis_index("limb")
    main_count = up_conv.shape[0]
    exps = jnp.concatenate(
        [
            lax.dynamic_slice_in_dim(tw_exp, lead * (JS - 1), JS - 1),
            lax.dynamic_slice_in_dim(tw_exp, main_count + lead, 1),
        ]
    )
    tw = twiddle(exps)
    h_a, h_b = jnp.asarray(hartley(A)), jnp.asarray(hartley(B))
    poly = (1, 1, JS - 1, NRING)

    def whole(*shape):
        return pl.BlockSpec(shape, lambda step: (0,) * len(shape))

    coefs = pl.pallas_call(
        inverse_kernel,
        grid=(1,),
        out_shape=f32(LIMBS, (JS - 1) * CHUNK, B),
        in_specs=[
            pl.BlockSpec(poly, lambda step: (0, 1, 0, 0)),
            whole(JS, A, B),
            whole(A, A),
            whole(B, B),
        ],
        out_specs=whole(LIMBS, (JS - 1) * CHUNK, B),
        scratch_shapes=[pltpu.VMEM((JS - 1, A, B), jnp.float32)],
        compiler_params=params(32),
        name="coefficients",
    )(cipher, tw, h_a, h_b)
    columns = exchange(coefs)

    count = lax.axis_size("key")
    ahead = [((target + 1) % count, target) for target in range(count)]
    lanes = NRING // 4
    packed = pl.pallas_call(
        pack_kernel,
        grid=(4,),
        out_shape=jax.ShapeDtypeStruct((32, NRING), jnp.bfloat16),
        in_specs=[
            pl.BlockSpec((1, 2, DNUM, JS - 1, lanes), lambda step: (0, 0, 0, 0, step)),
            pl.BlockSpec((1, 2, DNUM, 1, lanes), lambda step: (0, 0, 0, 0, step)),
            pl.BlockSpec((1, JS - 1, lanes), lambda step: (0, 0, step)),
            pl.BlockSpec((1, 1, lanes), lambda step: (0, 0, step)),
        ],
        out_specs=pl.BlockSpec((32, lanes), lambda step: (0, step)),
        scratch_shapes=[pltpu.VMEM((32, lanes), jnp.float32)],
        compiler_params=params(32),
        name="pack_keys",
    )(key_main, key_special, diag_main, diag_special)
    packed_next = lax.ppermute(packed, "key", ahead)
    perm_own = perms[0]
    perm_next = lax.ppermute(perm_own, "key", ahead)

    raised = pl.pallas_call(
        raise_kernel,
        out_shape=f32(LIMBS, DNUM * JS * CHUNK, B),
        in_specs=[SMEM, VMEM],
        out_specs=VMEM,
        compiler_params=params(32),
        name="raise_digits",
    )(up_conv, columns)
    rise = exchange(raised)

    summed, lowered = pl.pallas_call(
        switch_kernel,
        grid=(1,),
        out_shape=(f32(2 * JS, NRING), f32(LIMBS, 2 * CHUNK, B)),
        in_specs=[
            SMEM,
            SMEM,
            whole(LIMBS, DNUM * JS * CHUNK, B),
            pl.BlockSpec(poly, lambda step: (0, 0, 0, 0)),
            whole(JS, A, B),
            whole(A, A),
            whole(B, B),
            whole(32, NRING),
            whole(32, NRING),
        ],
        out_specs=(whole(2 * JS, NRING), whole(LIMBS, 2 * CHUNK, B)),
        scratch_shapes=[
            pltpu.VMEM((2, A * 16, 128), jnp.float32),
            pltpu.VMEM((NRING, 128), jnp.float32),
            pltpu.VMEM((NRING // 128, 16, 128), jnp.float32),
            pltpu.VMEM((NRING // 128, 16, 128), jnp.float32),
            pltpu.VMEM((2, A, B), jnp.float32),
        ],
        compiler_params=params(56),
        name="switch_keys",
    )(perm_own, perm_next, rise, cipher, tw, h_a, h_b, packed, packed_next)
    special = exchange(lowered)

    returned = pl.pallas_call(
        lower_kernel,
        out_shape=f32(LIMBS, 2 * (JS - 1) * CHUNK, B),
        in_specs=[SMEM, VMEM],
        out_specs=VMEM,
        compiler_params=params(32),
        name="return_limbs",
    )(down_conv, special)
    back = exchange(returned)

    return pl.pallas_call(
        finish_kernel,
        grid=(1,),
        out_shape=f32(1, 2, JS - 1, NRING),
        in_specs=[
            whole(LIMBS, 2 * (JS - 1) * CHUNK, B),
            whole(2 * JS, NRING),
            whole(JS, A, B),
            whole(A, A),
            whole(B, B),
        ],
        out_specs=whole(1, 2, JS - 1, NRING),
        scratch_shapes=[pltpu.VMEM((2, A * 8, 128), jnp.float32)],
        compiler_params=params(32),
        name="finish",
    )(back, summed, tw, h_a, h_b)


def solution(mesh):
    placed = (
        P("key", None, "limb", None),
        P("key", None, None, "limb", None),
        P("key", None, None, "limb", None),
        P("key", "limb", None),
        P("key", "limb", None),
        P("key", None),
        P(),
        P(),
        P(),
    )
    return jax.shard_map(
        on_device,
        mesh=mesh,
        in_specs=placed,
        out_specs=P("key", None, "limb", None),
        check_vma=False,
    )
```

time: 2290 us -> 185 us (0.08)
  the two profiles are of different devices: /device:TPU:0 before, /device:TPU:6 now
where the time goes in v1:
time: 185 us
  Pallas kernels  85.9 us (46%)
  blocking collectives  58.7 us (32%)
  waiting for transfers between devices  24.6 us (13%)
  local copies, waits for them, and re-layouts  7.67 us (4%)
  starting transfers between devices  4.85 us (3%)
  other arithmetic  2.77 us (1%)
    pallas_call x1, Pallas kernels, on_device(): pl.pallas_call(switch_kernel, grid=(1,), out_shape=(f32(2 * JS, NRING), f...  77.6 us
    all_to_all x3, blocking collectives, exchange(): lax.all_to_all(value, 'limb', split_axis=0, concat_axis=0, tiled=True)  58.7 us
    all_to_all x1, waiting for transfers between devices, exchange(): lax.all_to_all(value, 'limb', split_axis=0, concat_axis=0, tiled=True)  22.1 us
    unnamed x41, local copies, waits for them, and re-layouts  5.29 us
    all_to_all x1, starting transfers between devices, exchange(): lax.all_to_all(value, 'limb', split_axis=0, concat_axis=0, tiled=True)  4.43 us
  transfers between devices with their start and end apart: 3, of which 2 were waited for; matrix products, arithmetic and copies ran while one was open for 2% of the time, Pallas kernels for 2%

profile of v1, /device:TPU:6, one launch (start us, length us, event | category | flops | bytes accessed | tf_op | source)
XLA Modules:
  0.0 184.7 jit_solution(15851890829096895027)
XLA Ops:
  0.0 0.0 copy-start.14
  0.0 1.7 copy.14.ks_ref
  1.7 0.0 copy-done.14
  1.7 0.0 copy-start.10
  1.7 0.0 copy-start.11
  1.7 1.0 copy.13.km_ref
  2.8 0.0 copy-done.10
  2.8 0.0 copy-done.11
  2.8 0.0 copy-start.18
  2.8 0.0 copy-start.15
  2.8 1.3 pack_keys.1.k0_ref
  4.1 0.0 copy-start.1
  4.1 0.0 copy-start.5
  4.2 0.0 copy-start.8
  4.2 0.3 collective-permute-start.1
  4.5 0.0 copy-done.18
  4.5 0.8 dynamic_slice.7
  5.3 0.1 dynamic_slice.6
  5.4 0.7 pad_add_fusion
  6.1 0.0 copy-done.15
  6.1 0.5 copy.12.cipher_ref.base_ref
  6.7 0.0 copy-start
  6.7 0.1 add_select_fusion.1
  6.8 2.0 %fusion.4.tw_ref = f32[4,128,256]{2,1,0:T(8,128)S(1)} fusion(s32[4]{0:T(128)S(1)} %pad_add_fusion, s32[128,256]{1,0:T(8,128)S(1)} %add_select_fusion.1), kind=kLoop, calls=%fused_computation.9 | loop fusion | flops 2097152 | bytes 655376 | tf_op jit(solution)/shard_map/add | solution.py:35
  8.8 0.0 copy-done.5
  8.8 0.0 copy-done.8
  8.8 0.0 copy-start.12
  8.8 1.3 coefficients.1
  10.1 0.0 copy-done.1
  10.1 0.0 copy-start.2
  10.1 0.8 copy-done.2
  10.9 31.1 %all_to_all.20.x_ref = f32[8,48,256]{2,1,0:T(8,128)S(1)} all-to-all(f32[8,48,256]{2,1,0:T(8,128)S(1)} %coefficients.1), channel_id=1, replica_groups=mesh['key'=16,'limb'=8] {'limb'}, dimensions={0} | all-to-all | bytes 786432 | tf_op jit(solution)/shard_map/all_to_all | solution.py:218
  42.0 0.0 copy-done
  42.0 0.0 copy-done.12
  42.0 1.7 raise_digits.1
  43.7 0.0 copy-start.4
  43.7 1.2 copy-done.4
  44.8 0.0 copy-start.16
  44.8 4.4 %all-to-all-start.1 = ((f32[8,192,256]{2,1,0:T(8,128)}), f32[8,192,256]{2,1,0:T(8,128)}, u32[]{:S(2)}, u32[]{:S(2)}) async-start(f32[8,192,256]{2,1,0:T(8,128)} %copy-done.4), calls=%async_computation.1 | async-start | bytes 3145728 | tf_op jit(solution)/shard_map/all_to_all | solution.py:218
  49.3 0.0 copy-done.16
  49.3 0.0 copy-start.13
  49.3 0.1 collective-permute-start
  49.4 2.5 %collective-permute-done.idx1_ref = s32[32768]{0:T(1024)S(1)} collective-permute-done((s32[32768]{0:T(1024)S(1)}, s32[32768]{0:T(1024)S(1)}, u32[]{:S(2)}, u32[]{:S(2)}) %collective-permute-start) | collective-permute-done | bytes 131104 | tf_op jit(solution)/shard_map/ppermute | solution.py:278
  51.9 0.0 copy-start.17
  51.9 22.1 %all-to-all-done.1.x_ref = f32[8,192,256]{2,1,0:T(8,128)} async-done(((f32[8,192,256]{2,1,0:T(8,128)}), f32[8,192,256]{2,1,0:T(8,128)}, u32[]{:S(2)}, u32[]{:S(2)}) %all-to-all-start.1) | async-done | bytes 1572896 | tf_op jit(solution)/shard_map/all_to_all | solution.py:218
  74.0 0.0 collective-permute-done.1.k1_ref
  74.0 0.0 copy-done.17
  74.0 77.6 %switch_keys.1 = (f32[8,32768]{1,0:T(8,128)}, f32[8,32,256]{2,1,0:T(8,128)}) custom-call(s32[32768]{0:T(1024)} %bitcast.1, s32[32768]{0:T(1024)} %copy-done.17, f32[8,192,256]{2,1,0:T(8,128)} %all-to-all-done.1.x_ref, f32[1,2,3,32768]{3,2,1,0:T(4,128)} %copy-done, f32[4,128,256]{2,1,0:T(8,128)} %copy-done.2, f32[128,128]{1,0:T(8,128)} %constant.46.clone.ha_ref, ...), custom_call_target="tpu_custom_call" | custom-call | tf_op jit(solution)/shard_map/switch_keys/pallas_call | solution.py:290
  151.7 0.0 copy-start.3
  151.7 0.0 copy-start.6
  151.7 0.0 copy-start.7
  151.7 0.0 copy-start.9
  151.7 12.2 %all_to_all.21.x_ref = f32[8,32,256]{2,1,0:T(8,128)S(1)} all-to-all(f32[8,32,256]{2,1,0:T(8,128)} %get-tuple-element.7), channel_id=1, replica_groups=mesh['key'=16,'limb'=8] {'limb'}, dimensions={0} | all-to-all | bytes 524288 | tf_op jit(solution)/shard_map/all_to_all | solution.py:218
  163.9 0.0 copy-done.13
  163.9 1.1 return_limbs.1
  165.1 15.4 %all_to_all.22.x_ref = f32[8,96,256]{2,1,0:T(8,128)S(1)} all-to-all(f32[8,96,256]{2,1,0:T(8,128)S(1)} %return_limbs.1), channel_id=1, replica_groups=mesh['key'=16,'limb'=8] {'limb'}, dimensions={0} | all-to-all | bytes 1572864 | tf_op jit(solution)/shard_map/all_to_all | solution.py:218
  180.4 0.0 copy-done.3
  180.4 0.0 copy-done.6
  180.4 0.0 copy-done.7
  180.4 0.0 copy-done.9
  180.4 2.8 %finish.1 = f32[1,2,3,32768]{3,2,1,0:T(4,128)S(1)} custom-call(f32[8,96,256]{2,1,0:T(8,128)S(1)} %all_to_all.22.x_ref, f32[8,32768]{1,0:T(8,128)S(1)} %copy-done.7, f32[4,128,256]{2,1,0:T(8,128)S(1)} %copy-done.3, f32[128,128]{1,0:T(8,128)S(1)} %copy-done.9, f32[256,256]{1,0:T(8,128)S(1)} %copy-done.6), custom_call_target="tpu_custom_call" | custom-call | tf_op jit(solution)/shard_map/finish/pallas_call | solution.py:328
  183.3 1.5 copy.16
Async XLA Ops:
  0.0 1.7 copy-start.14
  1.7 1.0 copy-start.10
  1.7 1.0 copy-start.11
  2.8 1.7 copy-start.18
  2.8 3.3 %copy-start.15 = (f32[1,2,3,32768]{3,1,2,0:T(2,128)S(1)}, f32[1,2,3,32768]{3,1,2,0:T(2,128)}, u32[]{:S(2)}) copy-start(f32[1,2,3,32768]{3,1,2,0:T(2,128)} %param.11) | copy-start | bytes 2359300
  4.1 6.0 %copy-start.1 = (bf16[32,32768]{1,0:T(8,128)(2,1)}, bf16[32,32768]{1,0:T(8,128)(2,1)S(1)}, u32[]{:S(2)}) copy-start(bf16[32,32768]{1,0:T(8,128)(2,1)S(1)} %pack_keys.1.k0_ref) | copy-start | bytes 6291460
  4.1 4.6 %copy-start.5 = (f32[256,256]{1,0:T(8,128)S(1)}, f32[256,256]{1,0:T(8,128)}, u32[]{:S(2)}) copy-start(f32[256,256]{1,0:T(8,128)} %constant.47.clone.hb_ref) | copy-start | bytes 786436
  4.2 4.6 %copy-start.8 = (f32[128,128]{1,0:T(8,128)S(1)}, f32[128,128]{1,0:T(8,128)}, u32[]{:S(2)}) copy-start(f32[128,128]{1,0:T(8,128)} %constant.46.clone.ha_ref) | copy-start | bytes 196612
  4.2 69.8 %collective-permute-start.1 = (bf16[32,32768]{1,0:T(8,128)(2,1)S(1)}, bf16[32,32768]{1,0:T(8,128)(2,1)}, u32[]{:S(2)}, u32[]{:S(2)}) collective-permute-start(bf16[32,32768]{1,0:T(8,128)(2,1)S(1)} %pack_keys.1.k0_ref), channel_id=1, source_target_pairs={{8,0},{16,8},{24,16},{32,24},{40,32},{48,40},{56,48},{64,56},{72,6... | collective-permute-start | bytes 6291464 | tf_op jit(solution)/shard_map/ppermute | solution.py:276
  6.7 35.3 %copy-start = (f32[1,2,3,32768]{3,2,1,0:T(4,128)}, f32[1,2,3,32768]{3,2,1,0:T(4,128)S(1)}, u32[]{:S(2)}) copy-start(f32[1,2,3,32768]{3,2,1,0:T(4,128)S(1)} %copy.12.cipher_ref.base_ref) | copy-start | bytes 2359300
  8.8 33.2 %copy-start.12 = (f32[24,32]{1,0:T(8,128)S(1)}, f32[24,32]{1,0:T(8,128)}, u32[]{:S(2)}) copy-start(f32[24,32]{1,0:T(8,128)} %up_ref.1) | copy-start | bytes 9220
  10.1 0.8 copy-start.2
  43.7 1.2 copy-start.4
  44.8 4.4 %copy-start.16 = (s32[1,32768]{1,0:T(1,128)S(1)}, s32[1,32768]{1,0:T(1,128)}, u32[]{:S(2)}) copy-start(s32[1,32768]{1,0:T(1,128)} %param.16) | copy-start | bytes 393220
  44.8 29.2 %all-to-all-start.1 = ((f32[8,192,256]{2,1,0:T(8,128)}), f32[8,192,256]{2,1,0:T(8,128)}, u32[]{:S(2)}, u32[]{:S(2)}) async-start(f32[8,192,256]{2,1,0:T(8,128)} %copy-done.4), calls=%async_computation.1 | async-start | bytes 3145728 | tf_op jit(solution)/shard_map/all_to_all | solution.py:218
  49.3 114.7 %copy-start.13 = (f32[8,24]{1,0:T(8,128)S(1)}, f32[8,24]{1,0:T(8,128)}, u32[]{:S(2)}) copy-start(f32[8,24]{1,0:T(8,128)} %down_ref.1) | copy-start | bytes 2308
  49.3 2.6 %collective-permute-start = (s32[32768]{0:T(1024)S(1)}, s32[32768]{0:T(1024)S(1)}, u32[]{:S(2)}, u32[]{:S(2)}) collective-permute-start(s32[32768]{0:T(1024)S(1)} %bitcast.2), channel_id=1, source_target_pairs={{8,0},{16,8},{24,16},{32,24},{40,32},{48,40},{56,48},{64,56},{72,6... | collective-permute-start | bytes 393224 | tf_op jit(solution)/shard_map/ppermute | solution.py:278
  51.9 22.1 %copy-start.17 = (s32[32768]{0:T(1024)}, s32[32768]{0:T(1024)S(1)}, u32[]{:S(2)}) copy-start(s32[32768]{0:T(1024)S(1)} %collective-permute-done.idx1_ref) | copy-start | bytes 393220
  151.7 28.8 %copy-start.3 = (f32[4,128,256]{2,1,0:T(8,128)S(1)}, f32[4,128,256]{2,1,0:T(8,128)}, u32[]{:S(2)}) copy-start(f32[4,128,256]{2,1,0:T(8,128)} %copy-done.2) | copy-start | bytes 1572868
  151.7 28.8 %copy-start.6 = (f32[256,256]{1,0:T(8,128)S(1)}, f32[256,256]{1,0:T(8,128)}, u32[]{:S(2)}) copy-start(f32[256,256]{1,0:T(8,128)} %constant.47.clone.hb_ref) | copy-start | bytes 786436
  151.7 28.8 %copy-start.7 = (f32[8,32768]{1,0:T(8,128)S(1)}, f32[8,32768]{1,0:T(8,128)}, u32[]{:S(2)}) copy-start(f32[8,32768]{1,0:T(8,128)} %get-tuple-element.8.sum_ref) | copy-start | bytes 3145732
  151.7 28.8 %copy-start.9 = (f32[128,128]{1,0:T(8,128)S(1)}, f32[128,128]{1,0:T(8,128)}, u32[]{:S(2)}) copy-start(f32[128,128]{1,0:T(8,128)} %constant.46.clone.ha_ref) | copy-start | bytes 196612

commit v2 on v1

v2 whole, which is shorter than its diff:
```python
import math

import jax
import jax.numpy as jnp
import numpy as np
from jax import lax
from jax.experimental import pallas as pl
from jax.experimental.pallas import tpu as pltpu
from jax.sharding import PartitionSpec as P

A = 128
B = 256
NRING = A * B
DNUM = 3
LIMBS = 8
JS = 4
CHUNK = A // LIMBS
HIGHEST = lax.Precision.HIGHEST
MIB = 1 << 20
LN2 = math.log(2.0)
LINE = 1024
SLOTS = 4
BLOCKS = 4
ROTS = 2
TAIL = 16
FINE = 16
CODES = 32767.0
STEPS = ((2, 1), (1, 1), (3, 1), (2, 0), (0, 1), (1, 0), (3, 0))

VMEM = pl.BlockSpec(memory_space=pltpu.VMEM)
SMEM = pl.BlockSpec(memory_space=pltpu.SMEM)


def hartley(extent):
    indices = np.arange(extent)
    angles = (indices[:, None] * indices[None, :] % extent) * (2.0 * math.pi / extent)
    return ((np.cos(angles) + np.sin(angles)) / math.sqrt(extent)).astype(np.float32)


def twiddle(exponent):
    product = lax.broadcasted_iota(jnp.int32, (A, B), 0) * lax.broadcasted_iota(jnp.int32, (A, B), 1)
    phase = ((product & (NRING - 1)) * exponent) & (NRING - 1)
    quarter = NRING // 4 - jnp.abs(phase - NRING // 2)
    x = quarter.astype(jnp.float32) * (2.0 * math.pi / NRING)
    y = x * x
    series = 0.0
    for power in (11, 9, 7, 5, 3):
        series = (series + (-1.0) ** (power // 2) / math.factorial(power)) * y
    return 1.0 - 0.5 * (x + x * series)


def params(mib):
    return pltpu.CompilerParams(vmem_limit_bytes=mib * MIB)


def both_sides(h_a, block, h_b):
    half = jnp.dot(h_a, block, precision=HIGHEST, preferred_element_type=jnp.float32)
    return jnp.dot(half, h_b, precision=HIGHEST, preferred_element_type=jnp.float32)


def send_coded(blocks, out_ref):
    top = jnp.max(jnp.abs(blocks[0]))
    for block in blocks[1:]:
        top = jnp.maximum(top, jnp.max(jnp.abs(block)))
    exponent = jnp.ceil(jnp.log(jnp.full((TAIL, B), jnp.maximum(top, 1e-36))) * (FINE / LN2) + 0.125)
    gain = jnp.exp(exponent[:1] * (-LN2 / FINE))
    for at, block in enumerate(blocks):
        root = jnp.sqrt(jnp.sqrt(jnp.abs(block) * gain)) * CODES
        code = jnp.round(jnp.where(block < 0, -root, root)).astype(jnp.int32)
        out_ref[at * A : (at + 1) * A, :] = code.astype(jnp.int16)
    out_ref[len(blocks) * A :, :] = exponent.astype(jnp.int32).astype(jnp.int16)


def received(ref, at):
    tail = ref[ref.shape[0] - TAIL :, :].astype(jnp.int32).astype(jnp.float32)[:1]
    gain = jnp.exp(tail * (LN2 / FINE))
    root = ref[at * A : (at + 1) * A, :].astype(jnp.int32).astype(jnp.float32) * (1.0 / CODES)
    return (root * jnp.abs(root)) * (root * root) * gain


def partner(lead, step, sign):
    z = (lead // 2 + LIMBS + sign * step[0]) % (LIMBS // 2)
    return z * 2 + (lead + step[1]) % 2


def inverse_kernel(lead_ref, exp_ref, cipher_ref, ha_ref, hb_ref, out_ref, x_ref):
    def spread(step, _):
        for limb in range(JS - 1):
            rows = [cipher_ref[0, limb, 1:2, pl.ds(pl.multiple_of((step * 8 + k) * B, B), B)] for k in range(8)]
            x_ref[limb, pl.ds(pl.multiple_of(step * 8, 8), 8), :] = jnp.concatenate(rows, axis=0)
        return 0

    lax.fori_loop(0, A // 8, spread, 0)
    done = []
    for limb in range(JS - 1):
        tw = twiddle(exp_ref[lead_ref[0] * (JS - 1) + limb])
        done.append(both_sides(ha_ref[...], x_ref[limb], hb_ref[...]) / tw)
    send_coded(done, out_ref)


def pack_kernel(km_ref, ks_ref, dm_ref, ds_ref, out_ref, rows_ref):
    for p in range(2):
        for digit in range(DNUM):
            at = p * 16 + digit * JS
            rows_ref[at : at + JS - 1, :] = km_ref[0, p, digit].astype(jnp.float32)
            rows_ref[at + JS - 1 : at + JS, :] = ks_ref[0, p, digit].astype(jnp.float32)
        at = p * 16 + DNUM * JS
        rows_ref[at : at + JS - 1, :] = dm_ref[0].astype(jnp.float32)
        rows_ref[at + JS - 1 : at + JS, :] = ds_ref[0].astype(jnp.float32)
    out_ref[...] = rows_ref[...].astype(jnp.bfloat16)


def gather_kernel(
    lead_ref, exp_ref, up_ref, idx_ref, base_ref, ha_ref, hb_ref, own_ref, *rest,
):
    arrived, (got_ref, coef_ref, raised_ref, rows_ref, ext_ref, *slots, arrive) = rest[: len(STEPS)], rest[len(STEPS) :]
    chunks = ROTS * NRING // LINE

    def fetch(chunk, slot):
        place = pl.ds(pl.multiple_of(chunk * LINE, LINE), LINE)
        return pltpu.make_async_copy(idx_ref.at[place], slots[slot], arrive.at[slot])

    for slot in range(SLOTS):
        fetch(slot, slot).start()
    lead = lead_ref[0]
    for step, ref in zip(((0, 0),) + STEPS, (own_ref,) + arrived):
        source = partner(lead, step, -1)
        for limb in range(JS - 1):
            coef_ref[source * (JS - 1) + limb] = received(ref, limb)

    def lift(step, _):
        rows = pl.ds(pl.multiple_of(step * CHUNK, CHUNK), CHUNK)
        for digit in range(DNUM):
            limbs = range(digit * LIMBS, (digit + 1) * LIMBS)
            parts = [coef_ref[limb, rows, :] for limb in limbs]
            for j in range(JS):
                m = lead * (JS - 1) + j if j < JS - 1 else LIMBS * (JS - 1) + lead
                total = None
                for limb, part in zip(limbs, parts):
                    term = up_ref[limb, m] * part
                    total = term if total is None else total + term
                raised_ref[digit * JS + j, rows, :] = total
        return 0

    lax.fori_loop(0, LIMBS, lift, 0)

    for j in range(JS):
        tw = twiddle(exp_ref[lead * (JS - 1) + j if j < JS - 1 else LIMBS * (JS - 1) + lead])
        for digit in range(DNUM):
            ch = digit * JS + j
            done = both_sides(ha_ref[...], raised_ref[ch] * tw, hb_ref[...])
            rows_ref[0, pl.ds(ch, A, stride=16), :] = done[:, :128]
            rows_ref[1, pl.ds(ch, A, stride=16), :] = done[:, 128:]

    def first(i, _):
        for half in range(2):
            lanes = pl.ds(pl.multiple_of(i * B + half * 128, 128), 128)
            lines = [base_ref[0, limb, 0:1, lanes] for limb in range(JS - 1)] + [jnp.zeros((1, 128), jnp.float32)]
            rows_ref[half, pl.ds(pl.multiple_of(i * 16 + 8, 8) + 4, 4), :] = jnp.concatenate(lines, axis=0)
        return 0

    lax.fori_loop(0, A, first, 0)

    def turn(step, _):
        for k in range(4):
            i = step * 4 + k
            for half in range(2):
                part = rows_ref[half, pl.ds(pl.multiple_of(i * 16, 16), 16), :]
                ext_ref[pl.ds(pl.multiple_of(i * B + half * 128, 128), 128), :] = jnp.concatenate([part] * 8, axis=0).T
        return 0

    lax.fori_loop(0, A // 4, turn, 0)

    group = lax.broadcasted_iota(jnp.int32, (1, 128), 1) // 16

    def gather(step, _):
        for slot in range(SLOTS):
            chunk = step * SLOTS + slot
            fetch(chunk, slot).wait()
            for r in range(128):
                row = None
                for g in range(8):
                    one = ext_ref[pl.ds(slots[slot][g * 128 + r], 1), :]
                    row = one if row is None else jnp.where(group == g, one, row)
                got_ref[chunk, r : r + 1, :] = row

            @pl.when(step < chunks // SLOTS - 1)
            def _():
                fetch(chunk + SLOTS, slot).start()

        return 0

    lax.fori_loop(0, chunks // SLOTS, gather, 0)


def combine_kernel(
    lead_ref, exp_ref, got0_ref, got1_ref, ha_ref, hb_ref, k0_ref, k1_ref, sum_ref, low_ref, spec_ref,
):
    sub = lax.broadcasted_iota(jnp.int32, (8, 128), 0)
    low_half = sub < JS
    base_gain = jnp.where((sub >= JS) & (sub < 2 * JS - 1), 1.0, 0.0).astype(jnp.float32)
    step = pl.program_id(0)
    for part in range(BLOCKS // 2):
        lines = [[[], []], [[], []]]
        for k in range(16):
            blk, g = part * 2 + k // 8, k % 8
            if g == 0:
                turned = [ref[blk].T for ref in (got0_ref, got1_ref)]
            lanes = slice(blk * LINE + g * 128, blk * LINE + g * 128 + 128)
            sums = [None, None]
            for s, k_ref in enumerate((k0_ref, k1_ref)):
                keys = k_ref[:, lanes].astype(jnp.float32)
                upper = turned[s][g * 16 : g * 16 + 8]
                lower = turned[s][g * 16 + 8 : g * 16 + 16]
                tail = keys[8:16]
                diag = jnp.where(low_half, jnp.roll(tail, JS, axis=0), tail)
                for p in range(2):
                    gain = jnp.where(low_half, keys[p * 16 + 8 : p * 16 + 16], base_gain if p == 0 else 0.0)
                    term = diag * (keys[p * 16 : p * 16 + 8] * upper + gain * lower)
                    sums[p] = term if sums[p] is None else sums[p] + term
            folded = [value + jnp.roll(value, JS, axis=0) for value in sums]
            both = jnp.where(low_half, folded[0], folded[1])
            sum_ref[:, lanes] = both
            for p in range(2):
                lines[p][k % 2].append(both[p * JS + JS - 1 : p * JS + JS])
        at = pl.ds(pl.multiple_of(step * (BLOCKS * 4) + part * 8, 8), 8)
        for p in range(2):
            for half in range(2):
                spec_ref[p, at, half * 128 : (half + 1) * 128] = jnp.concatenate(lines[p][half], axis=0)

    @pl.when(step == pl.num_programs(0) - 1)
    def _():
        tw = twiddle(exp_ref[LIMBS * (JS - 1) + lead_ref[0]])
        send_coded([both_sides(ha_ref[...], spec_ref[p], hb_ref[...]) / tw for p in range(2)], low_ref)


def finish_kernel(lead_ref, exp_ref, down_ref, sum_ref, ha_ref, hb_ref, own_ref, *rest):
    arrived, (out_ref, low_ref, returned_ref, rows_ref) = rest[: len(STEPS)], rest[len(STEPS) :]
    lead = lead_ref[0]
    for step, ref in zip(((0, 0),) + STEPS, (own_ref,) + arrived):
        source = partner(lead, step, -1)
        for p in range(2):
            low_ref[source * 2 + p] = received(ref, p)

    def lower(step, _):
        rows = pl.ds(pl.multiple_of(step * CHUNK, CHUNK), CHUNK)
        for p in range(2):
            parts = [low_ref[k * 2 + p, rows, :] for k in range(LIMBS)]
            for j in range(JS - 1):
                total = None
                for k, part in enumerate(parts):
                    term = down_ref[k, lead * (JS - 1) + j] * part
                    total = term if total is None else total + term
                returned_ref[p * (JS - 1) + j, rows, :] = total
        return 0

    lax.fori_loop(0, LIMBS, lower, 0)
    for j in range(JS - 1):
        tw = twiddle(exp_ref[lead * (JS - 1) + j])
        for p in range(2):
            done = both_sides(ha_ref[...], returned_ref[p * (JS - 1) + j] * tw, hb_ref[...])
            rows_ref[0, pl.ds(p * JS + j, A, stride=8), :] = done[:, :128]
            rows_ref[1, pl.ds(p * JS + j, A, stride=8), :] = done[:, 128:]

    def body(i, _):
        for half in range(2):
            lanes = pl.ds(pl.multiple_of(i * B + half * 128, 128), 128)
            left = sum_ref[:, lanes] - rows_ref[half, pl.ds(pl.multiple_of(i * 8, 8), 8), :]
            for j in range(JS - 1):
                out_ref[0, j, :, lanes] = jnp.concatenate([left[j : j + 1], left[JS + j : JS + j + 1]], axis=0)
        return 0

    lax.fori_loop(0, A, body, 0)


def spread_limbs(value):
    return [value] + [
        lax.ppermute(value, "limb", [(source, partner(source, step, 1)) for source in range(LIMBS)])
        for step in STEPS
    ]


def f32(*shape):
    return jax.ShapeDtypeStruct(shape, jnp.float32)


def cost(micros):
    return pl.CostEstimate(flops=int(micros * 1e9), bytes_accessed=1 << 20, transcendentals=0)


def on_device(cipher, key_main, key_special, diag_main, diag_special, perms, tw_exp, up_conv, down_conv):
    lead = lax.axis_index("limb").astype(jnp.int32)[None]
    h_a, h_b = jnp.asarray(hartley(A)), jnp.asarray(hartley(B))
    cipher = cipher.transpose(0, 2, 1, 3)

    coefs = pl.pallas_call(
        inverse_kernel,
        out_shape=jax.ShapeDtypeStruct(((JS - 1) * A + TAIL, B), jnp.int16),
        in_specs=[SMEM, SMEM, VMEM, VMEM, VMEM],
        out_specs=VMEM,
        scratch_shapes=[pltpu.VMEM((JS - 1, A, B), jnp.float32)],
        compiler_params=params(32),
        cost_estimate=cost(2),
        name="coefficients",
    )(lead, tw_exp, cipher, h_a, h_b)
    held = spread_limbs(coefs)

    count = lax.axis_size("key")
    ahead = [((target + 1) % count, target) for target in range(count)]
    key_main, key_special, diag_main, diag_special, perm_own, _ = lax.optimization_barrier(
        (key_main, key_special, diag_main, diag_special, perms[0], coefs)
    )
    both_perms = jnp.concatenate([perm_own, lax.ppermute(perm_own, "key", ahead)])
    lanes = NRING // 4
    packed = pl.pallas_call(
        pack_kernel,
        grid=(4,),
        out_shape=jax.ShapeDtypeStruct((32, NRING), jnp.bfloat16),
        in_specs=[
            pl.BlockSpec((1, 2, DNUM, JS - 1, lanes), lambda step: (0, 0, 0, 0, step)),
            pl.BlockSpec((1, 2, DNUM, 1, lanes), lambda step: (0, 0, 0, 0, step)),
            pl.BlockSpec((1, JS - 1, lanes), lambda step: (0, 0, step)),
            pl.BlockSpec((1, 1, lanes), lambda step: (0, 0, step)),
        ],
        out_specs=pl.BlockSpec((32, lanes), lambda step: (0, step)),
        scratch_shapes=[pltpu.VMEM((32, lanes), jnp.float32)],
        compiler_params=params(32),
        cost_estimate=cost(2),
        name="pack_keys",
    )(key_main, key_special, diag_main, diag_special)
    packed, both_perms, *held = lax.optimization_barrier((packed, both_perms, *held))
    packed_next = lax.ppermute(packed, "key", ahead)

    gathered = pl.pallas_call(
        gather_kernel,
        out_shape=f32(ROTS * NRING // LINE, 128, 128),
        in_specs=[SMEM] * 3 + [pl.BlockSpec(memory_space=pl.ANY)] + [VMEM] * (4 + len(STEPS)),
        out_specs=VMEM,
        scratch_shapes=[
            pltpu.VMEM((LIMBS * (JS - 1), A, B), jnp.float32),
            pltpu.VMEM((DNUM * JS, A, B), jnp.float32),
            pltpu.VMEM((2, A * 16, 128), jnp.float32),
            pltpu.VMEM((NRING, 128), jnp.float32),
        ]
        + [pltpu.SMEM((LINE,), jnp.int32)] * SLOTS
        + [pltpu.SemaphoreType.DMA((SLOTS,))],
        compiler_params=params(56),
        cost_estimate=cost(50),
        name="extend_and_gather",
    )(lead, tw_exp, up_conv, both_perms, cipher, h_a, h_b, *held)

    steps = NRING // LINE // BLOCKS
    lines = (BLOCKS, 128, 128)
    keys = pl.BlockSpec((32, BLOCKS * LINE), lambda step: (0, step))
    low_shape = (2 * A + TAIL, B)
    summed, lowered = pl.pallas_call(
        combine_kernel,
        grid=(steps,),
        out_shape=(f32(2 * JS, NRING), jax.ShapeDtypeStruct(low_shape, jnp.int16)),
        in_specs=[SMEM] * 2
        + [
            pl.BlockSpec(lines, lambda step: (step, 0, 0)),
            pl.BlockSpec(lines, lambda step: (step + steps, 0, 0)),
            pl.BlockSpec((A, A), lambda step: (0, 0)),
            pl.BlockSpec((B, B), lambda step: (0, 0)),
            keys,
            keys,
        ],
        out_specs=(
            pl.BlockSpec((2 * JS, BLOCKS * LINE), lambda step: (0, step)),
            pl.BlockSpec(low_shape, lambda step: (0, 0)),
        ),
        scratch_shapes=[pltpu.VMEM((2, A, B), jnp.float32)],
        compiler_params=params(32),
        cost_estimate=cost(5),
        name="switch_keys",
    )(lead, tw_exp, gathered, gathered, h_a, h_b, packed, packed_next)
    special = spread_limbs(lowered)

    result = pl.pallas_call(
        finish_kernel,
        out_shape=f32(1, JS - 1, 2, NRING),
        in_specs=[SMEM] * 3 + [VMEM] * (4 + len(STEPS)),
        out_specs=VMEM,
        scratch_shapes=[
            pltpu.VMEM((LIMBS * 2, A, B), jnp.float32),
            pltpu.VMEM((2 * (JS - 1), A, B), jnp.float32),
            pltpu.VMEM((2, A * 8, 128), jnp.float32),
        ],
        compiler_params=params(32),
        cost_estimate=cost(4),
        name="finish",
    )(lead, tw_exp, down_conv, summed, h_a, h_b, *special)
    return result.transpose(0, 2, 1, 3)


def solution(mesh):
    placed = (
        P("key", None, "limb", None),
        P("key", None, None, "limb", None),
        P("key", None, None, "limb", None),
        P("key", "limb", None),
        P("key", "limb", None),
        P("key", None),
        P(),
        P(),
        P(),
    )
    return jax.shard_map(
        on_device,
        mesh=mesh,
        in_specs=placed,
        out_specs=P("key", None, "limb", None),
        check_vma=False,
    )
```

time: 185 us -> 124 us (0.67)
  the two profiles are of different devices: /device:TPU:6 before, /device:TPU:0 now
where the time goes in v2:
time: 124 us; the launch traced here: 123 us
  Pallas kernels  67.1 us (54%)
  starting transfers between devices  39.2 us (32%)
  waiting for transfers between devices  8.75 us (7%)
  local copies, waits for them, and re-layouts  7.45 us (6%)
    pallas_call x1, Pallas kernels, on_device(): pl.pallas_call(gather_kernel, out_shape=f32(ROTS * NRING // LINE, 128, 12...  53.4 us
    ppermute x14, starting transfers between devices, spread_limbs(): lax.ppermute(value, 'limb', [(source, partner(source, step, 1)) for sourc...  33.4 us
    ppermute x14, waiting for transfers between devices, spread_limbs(): lax.ppermute(value, 'limb', [(source, partner(source, step, 1)) for sourc...  8.75 us
    pallas_call x1, Pallas kernels, on_device(): pl.pallas_call(finish_kernel, out_shape=f32(1, JS - 1, 2, NRING), in_spec...  5.91 us
    unnamed x44, local copies, waits for them, and re-layouts  5.83 us
    ppermute x1, starting transfers between devices, on_device(): packed_next = lax.ppermute(packed, 'key', ahead)  4.32 us
    pallas_call x1, Pallas kernels, on_device(): pl.pallas_call(combine_kernel, grid=(steps,), out_shape=(f32(2 * JS, NRIN...  4.09 us
  transfers between devices with their start and end apart: 16, of which 4 were waited for; matrix products, arithmetic and copies ran while one was open for 2% of the time, Pallas kernels for 44%

profile of v2, /device:TPU:0, one launch (start us, length us, event | category | flops | bytes accessed | tf_op | source)
XLA Modules:
  0.0 123.4 jit_solution(849065438129343220)
XLA Ops:
  0.0 1.1 copy-done
  1.1 0.7 copy-done.5
  1.8 0.9 copy-done.7
  2.7 0.8 copy-done.9
  3.6 2.3 %coefficients.1.own_ref = s16[400,256]{1,0:T(8,128)(2,1)S(1)} custom-call(s32[1]{0:T(128)} %bitcast.lead_ref, s32[32]{0:T(128)S(1)} %copy-done.5, f32[1,3,2,32768]{3,2,1,0:T(2,128)S(1)} %bitcast.5, f32[128,128]{1,0:T(8,128)S(1)} %copy-done.9, f32[256,256]{1,0:T(8,128)S(1)} %copy-done.7), custom_call_target="tpu_custom_call" | custom-call | flops 2000000000 | bytes 1048576 | tf_op jit(solution)/shard_map/coefficients/pallas_call | solution.py:296
  5.9 0.0 copy-start.2
  5.9 0.0 copy-start.13
  5.9 0.0 copy-start.1
  5.9 0.0 copy-start.3
  5.9 6.7 %collective-permute-start.1 = (s16[400,256]{1,0:T(8,128)(2,1)S(1)}, s16[400,256]{1,0:T(8,128)(2,1)S(1)}, u32[]{:S(2)}, u32[]{:S(2)}) collective-permute-start(s16[400,256]{1,0:T(8,128)(2,1)S(1)} %coefficients.1.own_ref), channel_id=1, source_target_pairs={{0,5},{1,4},{2,7},{3,6},{4,1},{5,0},{6,3},{7,2},{8,13},{9,12},{10,... | collective-permute-start | bytes 614408 | tf_op jit(solution)/shard_map/ppermute | solution.py:278
  12.6 0.8 collective-permute-start.2
  13.4 4.8 %collective-permute-start.3 = (s16[400,256]{1,0:T(8,128)(2,1)S(1)}, s16[400,256]{1,0:T(8,128)(2,1)S(1)}, u32[]{:S(2)}, u32[]{:S(2)}) collective-permute-start(s16[400,256]{1,0:T(8,128)(2,1)S(1)} %coefficients.1.own_ref), channel_id=1, source_target_pairs={{0,7},{1,6},{2,1},{3,0},{4,3},{5,2},{6,5},{7,4},{8,15},{9,14},{10,... | collective-permute-start | bytes 614408 | tf_op jit(solution)/shard_map/ppermute | solution.py:278
  18.3 0.0 collective-permute-start.4
  18.3 0.0 copy-done.14
  18.3 1.5 %collective-permute-start = (s32[32768]{0:T(1024)S(1)}, s32[32768]{0:T(1024)S(1)}, u32[]{:S(2)}, u32[]{:S(2)}) collective-permute-start(s32[32768]{0:T(1024)S(1)} %bitcast.6), channel_id=1, source_target_pairs={{8,0},{16,8},{24,16},{32,24},{40,32},{48,40},{56,48},{64,56},{72,6... | collective-permute-start | bytes 393224 | tf_op jit(solution)/shard_map/ppermute | solution.py:313
  19.7 0.0 copy-done.12
  19.7 1.0 copy.12.km_ref
  20.8 0.0 copy-done.13
  20.8 0.6 copy.13.ks_ref
  21.4 0.0 copy-done.1
  21.4 0.0 copy-done.3
  21.4 1.3 %pack_keys.1.k0_ref = bf16[32,32768]{1,0:T(8,128)(2,1)S(1)} custom-call(bf16[1,2,3,3,32768]{4,3,2,1,0:T(4,128)(2,1)S(1)} %copy.12.km_ref, bf16[1,2,3,1,32768]{4,3,2,1,0:T(2,128)(2,1)S(1)} %copy.13.ks_ref, bf16[1,3,32768]{2,1,0:T(4,128)(2,1)S(1)} %copy-done.1, bf16[1,1,32768]{2,1,0:T(2,128)(2,1)S(1)} %copy-done.3), custom_call_target="tpu_custom_call" | custom-call | flops 2000000000 | bytes 1048576 | tf_op jit(solution)/shard_map/pack_keys/pallas_call | solution.py:315
  22.7 0.0 collective-permute-done
  22.7 1.9 %collective-permute-start.5 = (s16[400,256]{1,0:T(8,128)(2,1)S(1)}, s16[400,256]{1,0:T(8,128)(2,1)S(1)}, u32[]{:S(2)}, u32[]{:S(2)}) collective-permute-start(s16[400,256]{1,0:T(8,128)(2,1)S(1)} %coefficients.1.own_ref), channel_id=1, source_target_pairs={{0,1},{1,0},{2,3},{3,2},{4,5},{5,4},{6,7},{7,6},{8,9},{9,8},{10,11... | collective-permute-start | bytes 614408 | tf_op jit(solution)/shard_map/ppermute | solution.py:278
  24.7 0.0 collective-permute-done.1.rest_0_
  24.7 0.2 collective-permute-start.6
  24.9 0.0 collective-permute-done.2.rest_1_
  24.9 0.0 copy-done.2
  24.9 3.1 %collective-permute-start.7 = (s16[400,256]{1,0:T(8,128)(2,1)S(1)}, s16[400,256]{1,0:T(8,128)(2,1)S(1)}, u32[]{:S(2)}, u32[]{:S(2)}) collective-permute-start(s16[400,256]{1,0:T(8,128)(2,1)S(1)} %coefficients.1.own_ref), channel_id=1, source_target_pairs={{0,6},{1,7},{2,0},{3,1},{4,2},{5,3},{6,4},{7,5},{8,14},{9,15},{10,... | collective-permute-start | bytes 614408 | tf_op jit(solution)/shard_map/ppermute | solution.py:278
  28.0 0.7 pad_add_fusion.idx_ref
  28.7 0.0 collective-permute-done.3.rest_2_
  28.7 0.0 copy-start.17
  28.7 0.0 collective-permute-done.4.rest_3_
  28.7 0.0 copy-start.18
  28.7 2.9 %collective-permute-done.5.rest_4_ = s16[400,256]{1,0:T(8,128)(2,1)S(1)} collective-permute-done((s16[400,256]{1,0:T(8,128)(2,1)S(1)}, s16[400,256]{1,0:T(8,128)(2,1)S(1)}, u32[]{:S(2)}, u32[]{:S(2)}) %collective-permute-start.5) | collective-permute-done | bytes 204832 | tf_op jit(solution)/shard_map/ppermute | solution.py:278
  31.6 0.0 collective-permute-done.6.rest_5_
  31.6 0.3 collective-permute-done.7.rest_6_
  31.9 4.3 %collective-permute-start.8 = (bf16[32,32768]{1,0:T(8,128)(2,1)S(1)}, bf16[32,32768]{1,0:T(8,128)(2,1)S(1)}, u32[]{:S(2)}, u32[]{:S(2)}) collective-permute-start(bf16[32,32768]{1,0:T(8,128)(2,1)S(1)} %pack_keys.1.k0_ref), channel_id=1, source_target_pairs={{8,0},{16,8},{24,16},{32,24},{40,32},{48,40},{56,48},{64,56},{72,6... | collective-permute-start | bytes 6291464 | tf_op jit(solution)/shard_map/ppermute | solution.py:332
  36.2 0.0 copy-done.15
  36.2 0.0 copy-done.16
  36.3 0.0 copy-done.17
  36.3 0.0 copy-done.18
  36.3 0.0 copy-done.19
  36.3 0.0 copy-done.20
  36.3 53.4 %extend_and_gather.1.got0_ref.got1_ref = f32[64,128,128]{2,1,0:T(8,128)} custom-call(s32[1]{0:T(128)} %bitcast.lead_ref, s32[32]{0:T(128)} %exp_ref.7, f32[24,32]{1,0:T(8,128)} %up_ref.1, s32[65536]{0:T(1024)} %pad_add_fusion.idx_ref, f32[1,3,2,32768]{3,2,1,0:T(2,128)} %bitcast.4, f32[128,128]{1,0:T(8,128)} %constant.8.clone.ha_ref, ...), custom_call_target="tpu_custom_call" | custom-call | flops 49999998976 | bytes 1048576 | tf_op jit(solution)/shard_map/extend_and_gather/pallas_call | solution.py:334
  89.7 0.0 copy-start.4
  89.7 0.0 collective-permute-done.8.k1_ref
  89.8 2.2 %copy-done.11 = f32[64,128,128]{2,1,0:T(8,128)S(1)} copy-done((f32[64,128,128]{2,1,0:T(8,128)S(1)}, f32[64,128,128]{2,1,0:T(8,128)}, u32[]{:S(2)}) %copy-start.11) | copy-done | bytes 4194328
  92.0 4.1 %switch_keys.1 = (f32[8,32768]{1,0:T(8,128)S(1)}, s16[272,256]{1,0:T(8,128)(2,1)S(1)}) custom-call(s32[1]{0:T(128)} %bitcast.lead_ref, s32[32]{0:T(128)S(1)} %copy-done.6, f32[64,128,128]{2,1,0:T(8,128)S(1)} %copy-done.11, f32[64,128,128]{2,1,0:T(8,128)S(1)} %copy-done.11, f32[128,128]{1,0:T(8,128)S(1)} %copy-done.10, f32[256,256]{1,0:T(8,128)S(1)} %copy-done.8, ...), custom_call_target="tpu_custom_call" | custom-call | flops 5000000000 | bytes 1048576 | tf_op jit(solution)/shard_map/switch_keys/pallas_call | solution.py:356
  96.1 3.4 %collective-permute-start.10 = (s16[272,256]{1,0:T(8,128)(2,1)S(1)}, s16[272,256]{1,0:T(8,128)(2,1)S(1)}, u32[]{:S(2)}, u32[]{:S(2)}) collective-permute-start(s16[272,256]{1,0:T(8,128)(2,1)S(1)} %get-tuple-element.38.own_ref), channel_id=1, source_target_pairs={{0,3},{1,2},{2,5},{3,4},{4,7},{5,6},{6,1},{7,0},{8,11},{9,10},{10,... | collective-permute-start | bytes 417800 | tf_op jit(solution)/shard_map/ppermute | solution.py:278
  99.5 2.3 %collective-permute-start.11 = (s16[272,256]{1,0:T(8,128)(2,1)S(1)}, s16[272,256]{1,0:T(8,128)(2,1)S(1)}, u32[]{:S(2)}, u32[]{:S(2)}) collective-permute-start(s16[272,256]{1,0:T(8,128)(2,1)S(1)} %get-tuple-element.38.own_ref), channel_id=1, source_target_pairs={{0,7},{1,6},{2,1},{3,0},{4,3},{5,2},{6,5},{7,4},{8,15},{9,14},{10,... | collective-permute-start | bytes 417800 | tf_op jit(solution)/shard_map/ppermute | solution.py:278
  101.8 0.5 collective-permute-start.12
  102.3 3.0 %collective-permute-start.13 = (s16[272,256]{1,0:T(8,128)(2,1)S(1)}, s16[272,256]{1,0:T(8,128)(2,1)S(1)}, u32[]{:S(2)}, u32[]{:S(2)}) collective-permute-start(s16[272,256]{1,0:T(8,128)(2,1)S(1)} %get-tuple-element.38.own_ref), channel_id=1, source_target_pairs={{0,1},{1,0},{2,3},{3,2},{4,5},{5,4},{6,7},{7,6},{8,9},{9,8},{10,11... | collective-permute-start | bytes 417800 | tf_op jit(solution)/shard_map/ppermute | solution.py:278
  105.3 1.1 collective-permute-start.14
  106.4 0.0 collective-permute-done.10.rest_1_
  106.4 2.1 %collective-permute-start.15 = (s16[272,256]{1,0:T(8,128)(2,1)S(1)}, s16[272,256]{1,0:T(8,128)(2,1)S(1)}, u32[]{:S(2)}, u32[]{:S(2)}) collective-permute-start(s16[272,256]{1,0:T(8,128)(2,1)S(1)} %get-tuple-element.38.own_ref), channel_id=1, source_target_pairs={{0,6},{1,7},{2,0},{3,1},{4,2},{5,3},{6,4},{7,5},{8,14},{9,15},{10,... | collective-permute-start | bytes 417800 | tf_op jit(solution)/shard_map/ppermute | solution.py:278
  108.5 0.0 collective-permute-done.11.rest_2_
  108.5 3.4 %collective-permute-start.9 = (s16[272,256]{1,0:T(8,128)(2,1)S(1)}, s16[272,256]{1,0:T(8,128)(2,1)S(1)}, u32[]{:S(2)}, u32[]{:S(2)}) collective-permute-start(s16[272,256]{1,0:T(8,128)(2,1)S(1)} %get-tuple-element.38.own_ref), channel_id=1, source_target_pairs={{0,5},{1,4},{2,7},{3,6},{4,1},{5,0},{6,3},{7,2},{8,13},{9,12},{10,... | collective-permute-start | bytes 417800 | tf_op jit(solution)/shard_map/ppermute | solution.py:278
  112.0 0.0 collective-permute-done.12.rest_3_
  112.0 0.0 collective-permute-done.13.rest_4_
  112.0 1.1 collective-permute-done.14.rest_5_
  113.1 0.0 collective-permute-done.15.rest_6_
  113.1 4.4 %collective-permute-done.9.rest_0_ = s16[272,256]{1,0:T(8,128)(2,1)S(1)} collective-permute-done((s16[272,256]{1,0:T(8,128)(2,1)S(1)}, s16[272,256]{1,0:T(8,128)(2,1)S(1)}, u32[]{:S(2)}, u32[]{:S(2)}) %collective-permute-start.9) | collective-permute-done | bytes 139296 | tf_op jit(solution)/shard_map/ppermute | solution.py:278
  117.5 5.9 %finish.1 = f32[1,3,2,32768]{3,2,1,0:T(2,128)} custom-call(s32[1]{0:T(128)} %bitcast.lead_ref, s32[32]{0:T(128)S(1)} %copy-done.6, f32[8,24]{1,0:T(8,128)S(1)} %copy-done.4, f32[8,32768]{1,0:T(8,128)S(1)} %get-tuple-element.37.sum_ref, f32[128,128]{1,0:T(8,128)S(1)} %copy-done.10, f32[256,256]{1,0:T(8,128)S(1)} %copy-done.8, ...), custom_call_target="tpu_custom_call" | custom-call | flops 4000000000 | bytes 1048576 | tf_op jit(solution)/shard_map/finish/pallas_call | solution.py:380
  (20 shorter events, 0.0 us)
Async XLA Ops:
  0.0 1.1 copy-start
  1.1 0.7 copy-start.5
  1.8 0.9 copy-start.7
  2.7 0.8 copy-start.9
  3.6 14.7 %copy-start.14 = (s32[1,32768]{1,0:T(1,128)S(1)}, s32[1,32768]{1,0:T(1,128)}, u32[]{:S(2)}) copy-start(s32[1,32768]{1,0:T(1,128)} %param.16) | copy-start | bytes 393220
  3.6 16.2 %copy-start.12 = (bf16[1,2,3,3,32768]{4,1,3,2,0:T(2,128)(2,1)S(1)}, bf16[1,2,3,3,32768]{4,1,3,2,0:T(2,128)(2,1)}, u32[]{:S(2)}) copy-start(bf16[1,2,3,3,32768]{4,1,3,2,0:T(2,128)(2,1)} %param.12) | copy-start | bytes 3538948
  5.9 19.0 %copy-start.2 = (s16[400,256]{1,0:T(8,128)(2,1)}, s16[400,256]{1,0:T(8,128)(2,1)S(1)}, u32[]{:S(2)}) copy-start(s16[400,256]{1,0:T(8,128)(2,1)S(1)} %coefficients.1.own_ref) | copy-start | bytes 614404
  5.9 14.8 %copy-start.13 = (bf16[1,2,3,1,32768]{4,1,3,2,0:T(2,128)(2,1)S(1)}, bf16[1,2,3,1,32768]{4,1,3,2,0:T(2,128)(2,1)}, u32[]{:S(2)}) copy-start(bf16[1,2,3,1,32768]{4,1,3,2,0:T(2,128)(2,1)} %param.13) | copy-start | bytes 1179652
  5.9 15.5 %copy-start.1 = (bf16[1,3,32768]{2,1,0:T(4,128)(2,1)S(1)}, bf16[1,3,32768]{2,1,0:T(4,128)(2,1)}, u32[]{:S(2)}) copy-start(bf16[1,3,32768]{2,1,0:T(4,128)(2,1)} %dm_ref) | copy-start | bytes 589828
  5.9 15.5 %copy-start.3 = (bf16[1,1,32768]{2,1,0:T(2,128)(2,1)S(1)}, bf16[1,1,32768]{2,1,0:T(2,128)(2,1)}, u32[]{:S(2)}) copy-start(bf16[1,1,32768]{2,1,0:T(2,128)(2,1)} %ds_ref) | copy-start | bytes 196612
  5.9 18.7 %collective-permute-start.1 = (s16[400,256]{1,0:T(8,128)(2,1)S(1)}, s16[400,256]{1,0:T(8,128)(2,1)S(1)}, u32[]{:S(2)}, u32[]{:S(2)}) collective-permute-start(s16[400,256]{1,0:T(8,128)(2,1)S(1)} %coefficients.1.own_ref), channel_id=1, source_target_pairs={{0,5},{1,4},{2,7},{3,6},{4,1},{5,0},{6,3},{7,2},{8,13},{9,12},{10,... | collective-permute-start | bytes 614408 | tf_op jit(solution)/shard_map/ppermute | solution.py:278
  12.6 12.2 %collective-permute-start.2 = (s16[400,256]{1,0:T(8,128)(2,1)S(1)}, s16[400,256]{1,0:T(8,128)(2,1)S(1)}, u32[]{:S(2)}, u32[]{:S(2)}) collective-permute-start(s16[400,256]{1,0:T(8,128)(2,1)S(1)} %coefficients.1.own_ref), channel_id=1, source_target_pairs={{0,3},{1,2},{2,5},{3,4},{4,7},{5,6},{6,1},{7,0},{8,11},{9,10},{10,... | collective-permute-start | bytes 614408 | tf_op jit(solution)/shard_map/ppermute | solution.py:278
  13.4 15.3 %collective-permute-start.3 = (s16[400,256]{1,0:T(8,128)(2,1)S(1)}, s16[400,256]{1,0:T(8,128)(2,1)S(1)}, u32[]{:S(2)}, u32[]{:S(2)}) collective-permute-start(s16[400,256]{1,0:T(8,128)(2,1)S(1)} %coefficients.1.own_ref), channel_id=1, source_target_pairs={{0,7},{1,6},{2,1},{3,0},{4,3},{5,2},{6,5},{7,4},{8,15},{9,14},{10,... | collective-permute-start | bytes 614408 | tf_op jit(solution)/shard_map/ppermute | solution.py:278
  18.3 10.5 %collective-permute-start.4 = (s16[400,256]{1,0:T(8,128)(2,1)S(1)}, s16[400,256]{1,0:T(8,128)(2,1)S(1)}, u32[]{:S(2)}, u32[]{:S(2)}) collective-permute-start(s16[400,256]{1,0:T(8,128)(2,1)S(1)} %coefficients.1.own_ref), channel_id=1, source_target_pairs={{0,4},{1,5},{2,6},{3,7},{4,0},{5,1},{6,2},{7,3},{8,12},{9,13},{10,... | collective-permute-start | bytes 614408 | tf_op jit(solution)/shard_map/ppermute | solution.py:278
  18.3 4.5 %collective-permute-start = (s32[32768]{0:T(1024)S(1)}, s32[32768]{0:T(1024)S(1)}, u32[]{:S(2)}, u32[]{:S(2)}) collective-permute-start(s32[32768]{0:T(1024)S(1)} %bitcast.6), channel_id=1, source_target_pairs={{8,0},{16,8},{24,16},{32,24},{40,32},{48,40},{56,48},{64,56},{72,6... | collective-permute-start | bytes 393224 | tf_op jit(solution)/shard_map/ppermute | solution.py:313
  22.7 8.9 %collective-permute-start.5 = (s16[400,256]{1,0:T(8,128)(2,1)S(1)}, s16[400,256]{1,0:T(8,128)(2,1)S(1)}, u32[]{:S(2)}, u32[]{:S(2)}) collective-permute-start(s16[400,256]{1,0:T(8,128)(2,1)S(1)} %coefficients.1.own_ref), channel_id=1, source_target_pairs={{0,1},{1,0},{2,3},{3,2},{4,5},{5,4},{6,7},{7,6},{8,9},{9,8},{10,11... | collective-permute-start | bytes 614408 | tf_op jit(solution)/shard_map/ppermute | solution.py:278
  24.7 11.6 %copy-start.15 = (s16[400,256]{1,0:T(8,128)(2,1)}, s16[400,256]{1,0:T(8,128)(2,1)S(1)}, u32[]{:S(2)}) copy-start(s16[400,256]{1,0:T(8,128)(2,1)S(1)} %collective-permute-done.1.rest_0_) | copy-start | bytes 614404
  24.7 7.0 %collective-permute-start.6 = (s16[400,256]{1,0:T(8,128)(2,1)S(1)}, s16[400,256]{1,0:T(8,128)(2,1)S(1)}, u32[]{:S(2)}, u32[]{:S(2)}) collective-permute-start(s16[400,256]{1,0:T(8,128)(2,1)S(1)} %coefficients.1.own_ref), channel_id=1, source_target_pairs={{0,2},{1,3},{2,4},{3,5},{4,6},{5,7},{6,0},{7,1},{8,10},{9,11},{10,... | collective-permute-start | bytes 614408 | tf_op jit(solution)/shard_map/ppermute | solution.py:278
  24.9 11.4 %copy-start.16 = (s16[400,256]{1,0:T(8,128)(2,1)}, s16[400,256]{1,0:T(8,128)(2,1)S(1)}, u32[]{:S(2)}) copy-start(s16[400,256]{1,0:T(8,128)(2,1)S(1)} %collective-permute-done.2.rest_1_) | copy-start | bytes 614404
  24.9 7.1 %collective-permute-start.7 = (s16[400,256]{1,0:T(8,128)(2,1)S(1)}, s16[400,256]{1,0:T(8,128)(2,1)S(1)}, u32[]{:S(2)}, u32[]{:S(2)}) collective-permute-start(s16[400,256]{1,0:T(8,128)(2,1)S(1)} %coefficients.1.own_ref), channel_id=1, source_target_pairs={{0,6},{1,7},{2,0},{3,1},{4,2},{5,3},{6,4},{7,5},{8,14},{9,15},{10,... | collective-permute-start | bytes 614408 | tf_op jit(solution)/shard_map/ppermute | solution.py:278
  28.7 61.1 %copy-start.6 = (s32[32]{0:T(128)S(1)}, s32[32]{0:T(128)}, u32[]{:S(2)}) copy-start(s32[32]{0:T(128)} %exp_ref.7) | copy-start | bytes 388
  28.7 61.1 %copy-start.8 = (f32[256,256]{1,0:T(8,128)S(1)}, f32[256,256]{1,0:T(8,128)}, u32[]{:S(2)}) copy-start(f32[256,256]{1,0:T(8,128)} %constant.9.clone.hb_ref) | copy-start | bytes 786436
  28.7 61.1 %copy-start.10 = (f32[128,128]{1,0:T(8,128)S(1)}, f32[128,128]{1,0:T(8,128)}, u32[]{:S(2)}) copy-start(f32[128,128]{1,0:T(8,128)} %constant.8.clone.ha_ref) | copy-start | bytes 196612
  28.7 7.5 %copy-start.17 = (s16[400,256]{1,0:T(8,128)(2,1)}, s16[400,256]{1,0:T(8,128)(2,1)S(1)}, u32[]{:S(2)}) copy-start(s16[400,256]{1,0:T(8,128)(2,1)S(1)} %collective-permute-done.3.rest_2_) | copy-start | bytes 614404
  28.7 7.5 %copy-start.18 = (s16[400,256]{1,0:T(8,128)(2,1)}, s16[400,256]{1,0:T(8,128)(2,1)S(1)}, u32[]{:S(2)}) copy-start(s16[400,256]{1,0:T(8,128)(2,1)S(1)} %collective-permute-done.4.rest_3_) | copy-start | bytes 614404
  31.6 4.7 %copy-start.19 = (s16[400,256]{1,0:T(8,128)(2,1)}, s16[400,256]{1,0:T(8,128)(2,1)S(1)}, u32[]{:S(2)}) copy-start(s16[400,256]{1,0:T(8,128)(2,1)S(1)} %collective-permute-done.5.rest_4_) | copy-start | bytes 614404
  31.6 4.6 %copy-start.20 = (s16[400,256]{1,0:T(8,128)(2,1)}, s16[400,256]{1,0:T(8,128)(2,1)S(1)}, u32[]{:S(2)}) copy-start(s16[400,256]{1,0:T(8,128)(2,1)S(1)} %collective-permute-done.6.rest_5_) | copy-start | bytes 614404
  31.9 4.4 %copy-start.21 = (s16[400,256]{1,0:T(8,128)(2,1)}, s16[400,256]{1,0:T(8,128)(2,1)S(1)}, u32[]{:S(2)}) copy-start(s16[400,256]{1,0:T(8,128)(2,1)S(1)} %collective-permute-done.7.rest_6_) | copy-start | bytes 614404
  31.9 57.8 %collective-permute-start.8 = (bf16[32,32768]{1,0:T(8,128)(2,1)S(1)}, bf16[32,32768]{1,0:T(8,128)(2,1)S(1)}, u32[]{:S(2)}, u32[]{:S(2)}) collective-permute-start(bf16[32,32768]{1,0:T(8,128)(2,1)S(1)} %pack_keys.1.k0_ref), channel_id=1, source_target_pairs={{8,0},{16,8},{24,16},{32,24},{40,32},{48,40},{56,48},{64,56},{72,6... | collective-permute-start | bytes 6291464 | tf_op jit(solution)/shard_map/ppermute | solution.py:332
  89.7 27.8 %copy-start.4 = (f32[8,24]{1,0:T(8,128)S(1)}, f32[8,24]{1,0:T(8,128)}, u32[]{:S(2)}) copy-start(f32[8,24]{1,0:T(8,128)} %down_ref.1) | copy-start | bytes 2308
  89.8 2.2 %copy-start.11 = (f32[64,128,128]{2,1,0:T(8,128)S(1)}, f32[64,128,128]{2,1,0:T(8,128)}, u32[]{:S(2)}) copy-start(f32[64,128,128]{2,1,0:T(8,128)} %extend_and_gather.1.got0_ref.got1_ref) | copy-start | bytes 12582916
  96.1 10.4 %collective-permute-start.10 = (s16[272,256]{1,0:T(8,128)(2,1)S(1)}, s16[272,256]{1,0:T(8,128)(2,1)S(1)}, u32[]{:S(2)}, u32[]{:S(2)}) collective-permute-start(s16[272,256]{1,0:T(8,128)(2,1)S(1)} %get-tuple-element.38.own_ref), channel_id=1, source_target_pairs={{0,3},{1,2},{2,5},{3,4},{4,7},{5,6},{6,1},{7,0},{8,11},{9,10},{10,... | collective-permute-start | bytes 417800 | tf_op jit(solution)/shard_map/ppermute | solution.py:278
  99.5 9.0 %collective-permute-start.11 = (s16[272,256]{1,0:T(8,128)(2,1)S(1)}, s16[272,256]{1,0:T(8,128)(2,1)S(1)}, u32[]{:S(2)}, u32[]{:S(2)}) collective-permute-start(s16[272,256]{1,0:T(8,128)(2,1)S(1)} %get-tuple-element.38.own_ref), channel_id=1, source_target_pairs={{0,7},{1,6},{2,1},{3,0},{4,3},{5,2},{6,5},{7,4},{8,15},{9,14},{10,... | collective-permute-start | bytes 417800 | tf_op jit(solution)/shard_map/ppermute | solution.py:278
  101.8 10.2 %collective-permute-start.12 = (s16[272,256]{1,0:T(8,128)(2,1)S(1)}, s16[272,256]{1,0:T(8,128)(2,1)S(1)}, u32[]{:S(2)}, u32[]{:S(2)}) collective-permute-start(s16[272,256]{1,0:T(8,128)(2,1)S(1)} %get-tuple-element.38.own_ref), channel_id=1, source_target_pairs={{0,4},{1,5},{2,6},{3,7},{4,0},{5,1},{6,2},{7,3},{8,12},{9,13},{10,... | collective-permute-start | bytes 417800 | tf_op jit(solution)/shard_map/ppermute | solution.py:278
  102.3 9.7 %collective-permute-start.13 = (s16[272,256]{1,0:T(8,128)(2,1)S(1)}, s16[272,256]{1,0:T(8,128)(2,1)S(1)}, u32[]{:S(2)}, u32[]{:S(2)}) collective-permute-start(s16[272,256]{1,0:T(8,128)(2,1)S(1)} %get-tuple-element.38.own_ref), channel_id=1, source_target_pairs={{0,1},{1,0},{2,3},{3,2},{4,5},{5,4},{6,7},{7,6},{8,9},{9,8},{10,11... | collective-permute-start | bytes 417800 | tf_op jit(solution)/shard_map/ppermute | solution.py:278
  105.3 7.8 %collective-permute-start.14 = (s16[272,256]{1,0:T(8,128)(2,1)S(1)}, s16[272,256]{1,0:T(8,128)(2,1)S(1)}, u32[]{:S(2)}, u32[]{:S(2)}) collective-permute-start(s16[272,256]{1,0:T(8,128)(2,1)S(1)} %get-tuple-element.38.own_ref), channel_id=1, source_target_pairs={{0,2},{1,3},{2,4},{3,5},{4,6},{5,7},{6,0},{7,1},{8,10},{9,11},{10,... | collective-permute-start | bytes 417800 | tf_op jit(solution)/shard_map/ppermute | solution.py:278
  106.4 6.6 %collective-permute-start.15 = (s16[272,256]{1,0:T(8,128)(2,1)S(1)}, s16[272,256]{1,0:T(8,128)(2,1)S(1)}, u32[]{:S(2)}, u32[]{:S(2)}) collective-permute-start(s16[272,256]{1,0:T(8,128)(2,1)S(1)} %get-tuple-element.38.own_ref), channel_id=1, source_target_pairs={{0,6},{1,7},{2,0},{3,1},{4,2},{5,3},{6,4},{7,5},{8,14},{9,15},{10,... | collective-permute-start | bytes 417800 | tf_op jit(solution)/shard_map/ppermute | solution.py:278
  108.5 9.0 %collective-permute-start.9 = (s16[272,256]{1,0:T(8,128)(2,1)S(1)}, s16[272,256]{1,0:T(8,128)(2,1)S(1)}, u32[]{:S(2)}, u32[]{:S(2)}) collective-permute-start(s16[272,256]{1,0:T(8,128)(2,1)S(1)} %get-tuple-element.38.own_ref), channel_id=1, source_target_pairs={{0,5},{1,4},{2,7},{3,6},{4,1},{5,0},{6,3},{7,2},{8,13},{9,12},{10,... | collective-permute-start | bytes 417800 | tf_op jit(solution)/shard_map/ppermute | solution.py:278

commit v3 on v2

v3 whole, which is shorter than its diff:
```python
import functools
import math

import jax
import jax.numpy as jnp
import numpy as np
from jax import lax
from jax.experimental import pallas as pl
from jax.experimental.pallas import tpu as pltpu
from jax.sharding import PartitionSpec as P

A = 128
B = 256
NRING = A * B
DNUM = 3
LIMBS = 8
JS = 4
CHUNK = A // LIMBS
HIGHEST = lax.Precision.HIGHEST
MIB = 1 << 20
LN2 = math.log(2.0)
LINE = 1024
SLOTS = 4
CHIPS_Z = 4
BLOCKS = 4
ROTS = 2
TAIL = 16
FINE = 16
CODES = 32767.0

VMEM = pl.BlockSpec(memory_space=pltpu.VMEM)
SMEM = pl.BlockSpec(memory_space=pltpu.SMEM)


def hartley(extent):
    indices = np.arange(extent)
    angles = (indices[:, None] * indices[None, :] % extent) * (2.0 * math.pi / extent)
    return ((np.cos(angles) + np.sin(angles)) / math.sqrt(extent)).astype(np.float32)


def twiddle(exponent):
    product = lax.broadcasted_iota(jnp.int32, (A, B), 0) * lax.broadcasted_iota(jnp.int32, (A, B), 1)
    phase = ((product & (NRING - 1)) * exponent) & (NRING - 1)
    quarter = NRING // 4 - jnp.abs(phase - NRING // 2)
    x = quarter.astype(jnp.float32) * (2.0 * math.pi / NRING)
    y = x * x
    series = 0.0
    for power in (11, 9, 7, 5, 3):
        series = (series + (-1.0) ** (power // 2) / math.factorial(power)) * y
    return 1.0 - 0.5 * (x + x * series)


def params(mib):
    return pltpu.CompilerParams(vmem_limit_bytes=mib * MIB)


def parts(value):
    high = value.astype(jnp.bfloat16)
    return high, (value - high.astype(jnp.float32)).astype(jnp.bfloat16)


def product(left, right):
    terms = [(left[0], right[0]), (left[0], right[1]), (left[1], right[0])]
    done = [jnp.dot(x, y, preferred_element_type=jnp.float32) for x, y in terms]
    return done[0] + (done[1] + done[2])


def both_sides(h_a, block, h_b):
    return product(parts(product(h_a, parts(block))), h_b)


def send_coded(blocks, out_ref, copies):
    top = jnp.max(jnp.abs(blocks[0]))
    for block in blocks[1:]:
        top = jnp.maximum(top, jnp.max(jnp.abs(block)))
    exponent = jnp.ceil(jnp.log(jnp.full((TAIL, B), jnp.maximum(top, 1e-36))) * (FINE / LN2) + 0.125)
    gain = jnp.exp(exponent[:1] * (-LN2 / FINE))
    for at, block in enumerate(blocks):
        root = jnp.sqrt(jnp.sqrt(jnp.abs(block) * gain)) * CODES
        code = jnp.round(jnp.where(block < 0, -root, root)).astype(jnp.int32).astype(jnp.int16)
        for to in range(copies):
            out_ref[to, at * A : (at + 1) * A, :] = code
    scale = exponent.astype(jnp.int32).astype(jnp.int16)
    for to in range(copies):
        out_ref[to, len(blocks) * A :, :] = scale


def received(ref, source, at):
    rows = ref.shape[1]
    tail = ref[source, rows - TAIL : rows, :].astype(jnp.int32).astype(jnp.float32)[:1]
    gain = jnp.exp(tail * (LN2 / FINE))
    root = ref[source, at * A : (at + 1) * A, :].astype(jnp.int32).astype(jnp.float32) * (1.0 / CODES)
    return (root * jnp.abs(root)) * (root * root) * gain


def inverse_kernel(lead_ref, exp_ref, cipher_ref, ha_ref, hb_ref, out_ref, x_ref):
    def spread(step, _):
        for limb in range(JS - 1):
            rows = [cipher_ref[0, limb, 1:2, pl.ds(pl.multiple_of((step * 8 + k) * B, B), B)] for k in range(8)]
            x_ref[limb, pl.ds(pl.multiple_of(step * 8, 8), 8), :] = jnp.concatenate(rows, axis=0)
        return 0

    lax.fori_loop(0, A // 8, spread, 0)
    h_a, h_b = parts(ha_ref[...]), parts(hb_ref[...])
    done = []
    for limb in range(JS - 1):
        tw = twiddle(exp_ref[lead_ref[0] * (JS - 1) + limb])
        done.append(both_sides(h_a, x_ref[limb], h_b) / tw)
    send_coded(done, out_ref, 1)


def pack_kernel(km_ref, ks_ref, dm_ref, ds_ref, out_ref, rows_ref):
    for p in range(2):
        for digit in range(DNUM):
            at = p * 16 + digit * JS
            rows_ref[at : at + JS - 1, :] = km_ref[0, p, digit].astype(jnp.float32)
            rows_ref[at + JS - 1 : at + JS, :] = ks_ref[0, p, digit].astype(jnp.float32)
        at = p * 16 + DNUM * JS
        rows_ref[at : at + JS - 1, :] = dm_ref[0].astype(jnp.float32)
        rows_ref[at + JS - 1 : at + JS, :] = ds_ref[0].astype(jnp.float32)
    out_ref[...] = rows_ref[...].astype(jnp.bfloat16)


def combine(block, keys_ref, lanes_of, before_ref, sum_ref):
    sub = lax.broadcasted_iota(jnp.int32, (8, 128), 0)
    low_half = sub < JS
    base_gain = jnp.where((sub >= JS) & (sub < 2 * JS - 1), 1.0, 0.0).astype(jnp.float32)
    special = [[[], []], [[], []]]
    turned = block.T
    for g in range(8):
        lanes = lanes_of(g)
        keys = keys_ref[:, lanes].astype(jnp.float32)
        upper = turned[g * 16 : g * 16 + 8]
        lower = turned[g * 16 + 8 : g * 16 + 16]
        tail = keys[8:16]
        diag = jnp.where(low_half, jnp.roll(tail, JS, axis=0), tail)
        folded = []
        for p in range(2):
            gain = jnp.where(low_half, keys[p * 16 + 8 : p * 16 + 16], base_gain if p == 0 else 0.0)
            term = diag * (keys[p * 16 : p * 16 + 8] * upper + gain * lower)
            folded.append(term + jnp.roll(term, JS, axis=0))
        both = jnp.where(low_half, folded[0], folded[1])
        if before_ref is not None:
            both = both + before_ref[:, lanes]
        sum_ref[:, lanes] = both
        for p in range(2):
            special[p][g % 2].append(both[p * JS + JS - 1 : p * JS + JS])
    return special


def extend_kernel(
    lead_ref, exp_ref, up_ref, idx_ref, base_ref, ha_ref, hb_ref, keys_ref, held0_ref, held1_ref, held2_ref, held3_ref,
    sum_ref, got_ref, coef_ref, raised_ref, rows_ref, turns_ref, ext_ref, *rest,
):
    slots, got, arrive = rest[:SLOTS], rest[SLOTS : 2 * SLOTS], rest[-1]
    chunks = ROTS * NRING // LINE

    def fetch(chunk, slot):
        place = pl.ds(pl.multiple_of(chunk * LINE, LINE), LINE)
        return pltpu.make_async_copy(idx_ref.at[place], slots[slot], arrive.at[slot])

    for slot in range(SLOTS):
        fetch(slot, slot).start()
    lead = lead_ref[0]
    for step, held_ref in enumerate((held0_ref, held1_ref, held2_ref, held3_ref)):
        for across in range(2):
            source = (lead // 2 + CHIPS_Z - step) % CHIPS_Z * 2 + (lead + across) % 2
            for limb in range(JS - 1):
                coef_ref[source * (JS - 1) + limb] = received(held_ref, across, limb)

    def lift(step, _):
        rows = pl.ds(pl.multiple_of(step * CHUNK, CHUNK), CHUNK)
        for digit in range(DNUM):
            limbs = range(digit * LIMBS, (digit + 1) * LIMBS)
            parts = [coef_ref[limb, rows, :] for limb in limbs]
            for j in range(JS):
                m = lead * (JS - 1) + j if j < JS - 1 else LIMBS * (JS - 1) + lead
                total = None
                for limb, part in zip(limbs, parts):
                    term = up_ref[limb, m] * part
                    total = term if total is None else total + term
                raised_ref[digit * JS + j, rows, :] = total
        return 0

    lax.fori_loop(0, LIMBS, lift, 0)

    h_a, h_b = parts(ha_ref[...]), parts(hb_ref[...])
    for j in range(JS):
        tw = twiddle(exp_ref[lead * (JS - 1) + j if j < JS - 1 else LIMBS * (JS - 1) + lead])
        for digit in range(DNUM):
            ch = digit * JS + j
            done = both_sides(h_a, raised_ref[ch] * tw, h_b)
            rows_ref[0, pl.ds(ch, A, stride=16), :] = done[:, :128]
            rows_ref[1, pl.ds(ch, A, stride=16), :] = done[:, 128:]

    def first(i, _):
        for half in range(2):
            lanes = pl.ds(pl.multiple_of(i * B + half * 128, 128), 128)
            lines = [base_ref[0, limb, 0:1, lanes] for limb in range(JS - 1)] + [jnp.zeros((1, 128), jnp.float32)]
            rows_ref[half, pl.ds(pl.multiple_of(i * 16 + 8, 8) + 4, 4), :] = jnp.concatenate(lines, axis=0)
        return 0

    lax.fori_loop(0, A, first, 0)

    source = lax.broadcasted_iota(jnp.int32, (2 * 128, 128), 0) & 127
    target = lax.broadcasted_iota(jnp.int32, (2 * 128, 128), 1)
    for by in range(8):
        ones = jnp.where(((source + by * 16) & 127) == target, 1.0, 0.0)
        turns_ref[:, by * 128 : (by + 1) * 128] = ones.astype(jnp.bfloat16)

    def turn(step, _):
        for half in range(2):
            block = rows_ref[half, pl.ds(pl.multiple_of(step * 128, 128), 128), :].T
            both = jnp.concatenate(parts(block), axis=1)
            turned = jnp.dot(both, turns_ref[...], preferred_element_type=jnp.float32)
            for by in range(8):
                at = pl.ds(pl.multiple_of(by * (NRING // 8) + step * B + half * 128, 128), 128)
                ext_ref[at, :] = turned[:, by * 128 : (by + 1) * 128]
        return 0

    lax.fori_loop(0, A // 8, turn, 0)


    group = lax.broadcasted_iota(jnp.int32, (1, 128), 1) // 16

    def gather(chunk, slot, store):
        fetch(chunk, slot).wait()
        for r in range(128):
            row = None
            for g in range(8):
                one = ext_ref[pl.ds(slots[slot][g * 128 + r], 1), :]
                row = one if row is None else jnp.where(group == g, one, row)
            store(r, row)

    def own(step, _):
        def product_of(chunk, slot):
            lanes_of = lambda g: pl.ds(pl.multiple_of(chunk * LINE + g * 128, 128), 128)
            combine(got[slot][...], keys_ref, lanes_of, None, sum_ref)

        for slot in range(SLOTS):
            chunk = step * SLOTS + slot

            def store(r, row, slot=slot):
                got[slot][r : r + 1, :] = row

            gather(chunk, slot, store)
            if slot > 0:
                product_of(chunk - 1, slot - 1)
            fetch(chunk + SLOTS, slot).start()
        product_of(step * SLOTS + SLOTS - 1, SLOTS - 1)
        return 0

    lax.fori_loop(0, chunks // 2 // SLOTS, own, 0)

    def other(step, _):
        for slot in range(SLOTS):
            chunk = step * SLOTS + slot

            def store(r, row, chunk=chunk):
                got_ref[chunk - chunks // 2, r : r + 1, :] = row

            gather(chunk, slot, store)
            fetch(jnp.minimum(chunk + SLOTS, chunks - 1), slot).start()
        return 0

    lax.fori_loop(chunks // 2 // SLOTS, chunks // SLOTS, other, 0)
    for slot in range(SLOTS):
        fetch(chunks - 1, slot).wait()


def combine_kernel(
    lead_ref, exp_ref, got_ref, ha_ref, hb_ref, keys_ref, before_ref, sum_ref, low_ref, spec_ref,
):
    step = pl.program_id(0)
    for pair in range(BLOCKS // 2):
        done = []
        for blk in (2 * pair, 2 * pair + 1):
            lanes_of = lambda g: slice(blk * LINE + g * 128, blk * LINE + g * 128 + 128)
            done.append(combine(got_ref[blk], keys_ref, lanes_of, before_ref, sum_ref))
        at = pl.ds(pl.multiple_of(step * (BLOCKS * 4) + pair * 8, 8), 8)
        for p in range(2):
            for half in range(2):
                eight = done[0][p][half] + done[1][p][half]
                spec_ref[p, at, half * 128 : (half + 1) * 128] = jnp.concatenate(eight, axis=0)

    @pl.when(step == pl.num_programs(0) - 1)
    def _():
        tw = twiddle(exp_ref[LIMBS * (JS - 1) + lead_ref[0]])
        h_a, h_b = parts(ha_ref[...]), parts(hb_ref[...])
        send_coded([both_sides(h_a, spec_ref[p], h_b) / tw for p in range(2)], low_ref, LIMBS)


def finish_kernel(lead_ref, exp_ref, down_ref, sum_ref, ha_ref, hb_ref, held_ref, out_ref, low_ref, returned_ref, rows_ref):
    lead = lead_ref[0]
    h_a, h_b = parts(ha_ref[...]), parts(hb_ref[...])
    for source in range(LIMBS):
        for p in range(2):
            low_ref[source * 2 + p] = received(held_ref, source, p)

    def lower(step, _):
        rows = pl.ds(pl.multiple_of(step * CHUNK, CHUNK), CHUNK)
        for p in range(2):
            parts = [low_ref[k * 2 + p, rows, :] for k in range(LIMBS)]
            for j in range(JS - 1):
                total = None
                for k, part in enumerate(parts):
                    term = down_ref[k, lead * (JS - 1) + j] * part
                    total = term if total is None else total + term
                returned_ref[p * (JS - 1) + j, rows, :] = total
        return 0

    lax.fori_loop(0, LIMBS, lower, 0)
    for j in range(JS - 1):
        tw = twiddle(exp_ref[lead * (JS - 1) + j])
        for p in range(2):
            done = both_sides(h_a, returned_ref[p * (JS - 1) + j] * tw, h_b)
            rows_ref[0, pl.ds(p * JS + j, A, stride=8), :] = done[:, :128]
            rows_ref[1, pl.ds(p * JS + j, A, stride=8), :] = done[:, 128:]

    def body(i, _):
        for half in range(2):
            lanes = pl.ds(pl.multiple_of(i * B + half * 128, 128), 128)
            left = sum_ref[:, lanes] - rows_ref[half, pl.ds(pl.multiple_of(i * 8, 8), 8), :]
            for j in range(JS - 1):
                out_ref[0, j, :, lanes] = jnp.concatenate([left[j : j + 1], left[JS + j : JS + j + 1]], axis=0)
        return 0

    lax.fori_loop(0, A, body, 0)


def exchange(value):
    return lax.all_to_all(value, "limb", split_axis=0, concat_axis=0, tiled=True)


def rows_of(perms):
    place = jnp.arange(perms.shape[0], dtype=jnp.int32) >> 7
    by = (place - (perms >> 8)) & 7
    return (by << 12) + ((perms >> 11) << 8) + (perms & (B - 1))


def f32(*shape):
    return jax.ShapeDtypeStruct(shape, jnp.float32)


def cost(micros):
    return pl.CostEstimate(flops=int(micros * 1e9), bytes_accessed=1 << 20, transcendentals=0)


def on_device(cipher, key_main, key_special, diag_main, diag_special, perms, tw_exp, up_conv, down_conv):
    lead = lax.axis_index("limb").astype(jnp.int32)[None]
    h_a, h_b = jnp.asarray(hartley(A)), jnp.asarray(hartley(B))
    cipher = cipher.transpose(0, 2, 1, 3)

    coefs = pl.pallas_call(
        inverse_kernel,
        out_shape=jax.ShapeDtypeStruct((1, (JS - 1) * A + TAIL, B), jnp.int16),
        in_specs=[SMEM, SMEM, VMEM, VMEM, VMEM],
        out_specs=VMEM,
        scratch_shapes=[pltpu.VMEM((JS - 1, A, B), jnp.float32)],
        compiler_params=params(60),
        cost_estimate=cost(2),
        name="coefficients",
    )(lead, tw_exp, cipher, h_a, h_b)
    pair = jnp.concatenate([coefs, lax.ppermute(coefs, "limb", [(source, source ^ 1) for source in range(LIMBS)])])
    held = [pair] + [
        lax.ppermute(pair, "limb", [(source, (source + 2 * step) % LIMBS) for source in range(LIMBS)])
        for step in range(1, CHIPS_Z)
    ]

    count = lax.axis_size("key")
    ahead = [((target + 1) % count, target) for target in range(count)]
    key_main, key_special, diag_main, diag_special, _ = lax.optimization_barrier(
        (key_main, key_special, diag_main, diag_special, coefs)
    )
    lanes = NRING // 4
    packed = pl.pallas_call(
        pack_kernel,
        grid=(4,),
        out_shape=jax.ShapeDtypeStruct((32, NRING), jnp.bfloat16),
        in_specs=[
            pl.BlockSpec((1, 2, DNUM, JS - 1, lanes), lambda step: (0, 0, 0, 0, step)),
            pl.BlockSpec((1, 2, DNUM, 1, lanes), lambda step: (0, 0, 0, 0, step)),
            pl.BlockSpec((1, JS - 1, lanes), lambda step: (0, 0, step)),
            pl.BlockSpec((1, 1, lanes), lambda step: (0, 0, step)),
        ],
        out_specs=pl.BlockSpec((32, lanes), lambda step: (0, step)),
        scratch_shapes=[pltpu.VMEM((32, lanes), jnp.float32)],
        compiler_params=params(32),
        cost_estimate=cost(2),
        name="pack_keys",
    )(key_main, key_special, diag_main, diag_special)
    perm_own, packed = lax.optimization_barrier((perms[0], packed))
    both_rows = rows_of(jnp.concatenate([perm_own, lax.ppermute(perm_own, "key", ahead)]))
    packed, both_rows, *held = lax.optimization_barrier((packed, both_rows, *held))
    packed_next = lax.ppermute(packed, "key", ahead)

    half_lines = NRING // LINE
    first, gathered = pl.pallas_call(
        extend_kernel,
        out_shape=(f32(2 * JS, NRING), f32(half_lines, 128, 128)),
        in_specs=[SMEM] * 3 + [pl.BlockSpec(memory_space=pl.ANY)] + [VMEM] * 8,
        out_specs=(VMEM, VMEM),
        scratch_shapes=[
            pltpu.VMEM((LIMBS * (JS - 1), A, B), jnp.float32),
            pltpu.VMEM((DNUM * JS, A, B), jnp.float32),
            pltpu.VMEM((2, A * 16, 128), jnp.float32),
            pltpu.VMEM((2 * 128, 8 * 128), jnp.bfloat16),
            pltpu.VMEM((NRING, 128), jnp.float32),
        ]
        + [pltpu.SMEM((LINE,), jnp.int32)] * SLOTS
        + [pltpu.VMEM((128, 128), jnp.float32)] * SLOTS
        + [pltpu.SemaphoreType.DMA((SLOTS,))],
        compiler_params=params(40),
        cost_estimate=cost(50),
        name="extend_and_gather",
    )(lead, tw_exp, up_conv, both_rows, cipher, h_a, h_b, packed, *held)

    lines = (BLOCKS, 128, 128)
    columns = pl.BlockSpec((2 * JS, BLOCKS * LINE), lambda step: (0, step))
    low_shape = (LIMBS, 2 * A + TAIL, B)
    summed, lowered = pl.pallas_call(
        combine_kernel,
        grid=(half_lines // BLOCKS,),
        out_shape=(f32(2 * JS, NRING), jax.ShapeDtypeStruct(low_shape, jnp.int16)),
        in_specs=[SMEM] * 2
        + [
            pl.BlockSpec(lines, lambda step: (step, 0, 0)),
            pl.BlockSpec((A, A), lambda step: (0, 0)),
            pl.BlockSpec((B, B), lambda step: (0, 0)),
            pl.BlockSpec((32, BLOCKS * LINE), lambda step: (0, step)),
            columns,
        ],
        out_specs=(columns, pl.BlockSpec(low_shape, lambda step: (0, 0, 0))),
        scratch_shapes=[pltpu.VMEM((2, A, B), jnp.float32)],
        compiler_params=params(32),
        cost_estimate=cost(4),
        name="switch_next",
    )(lead, tw_exp, gathered, h_a, h_b, packed_next, first)
    special = exchange(lowered)

    result = pl.pallas_call(
        finish_kernel,
        out_shape=f32(1, JS - 1, 2, NRING),
        in_specs=[SMEM] * 3 + [VMEM] * 4,
        out_specs=VMEM,
        scratch_shapes=[
            pltpu.VMEM((LIMBS * 2, A, B), jnp.float32),
            pltpu.VMEM((2 * (JS - 1), A, B), jnp.float32),
            pltpu.VMEM((2, A * 8, 128), jnp.float32),
        ],
        compiler_params=params(60),
        cost_estimate=cost(4),
        name="finish",
    )(lead, tw_exp, down_conv, summed, h_a, h_b, special)
    return result.transpose(0, 2, 1, 3)


def solution(mesh):
    placed = (
        P("key", None, "limb", None),
        P("key", None, None, "limb", None),
        P("key", None, None, "limb", None),
        P("key", "limb", None),
        P("key", "limb", None),
        P("key", None),
        P(),
        P(),
        P(),
    )
    return jax.shard_map(
        on_device,
        mesh=mesh,
        in_specs=placed,
        out_specs=P("key", None, "limb", None),
        check_vma=False,
    )
```

time: 124 us -> 120 us (0.968)
  starting transfers between devices: 39.2 us -> 13 us
  blocking collectives: 0 us -> 19.8 us
  waiting for transfers between devices: 8.75 us -> 21.9 us
  local copies, waits for them, and re-layouts: 7.45 us -> 1.71 us
  Pallas kernels: 67.1 us -> 63.1 us
    ppermute x14 -> x4, starting transfers between devices: 33.4 us -> 8.64 us  [the longest x3 5.36 us: on_device(): lax.ppermute(pair, 'limb', [(source, (source + 2 * step) % LIMBS) for sou...]
    all_to_all x0 -> x1, blocking collectives: none -> 19.8 us  [exchange(): lax.all_to_all(value, 'limb', split_axis=0, concat_axis=0, tiled=True)]
    ppermute x14 -> x4, waiting for transfers between devices: 8.75 us -> 19.4 us  [the longest x3 19.4 us: on_device(): lax.ppermute(pair, 'limb', [(source, (source + 2 * step) % LIMBS) for sou...]
    unnamed x44 -> x25, local copies, waits for them, and re-layouts: 5.83 us -> 0.08 us
    pallas_call x3, Pallas kernels: 59.8 us -> 55.8 us  [the longest x1 49.3 us: on_device(): pl.pallas_call(extend_kernel, out_shape=(f32(2 * JS, NRING), f32(half_lin...]
    ppermute x1, waiting for transfers between devices: 0.01 us -> 2.51 us  [on_device(): lax.ppermute(perm_own, 'key', ahead)]
    ppermute x1, starting transfers between devices: 4.32 us -> 2.29 us  [on_device(): packed_next = lax.ppermute(packed, 'key', ahead)]
  transfers between devices with their start and end apart: 16 -> 6, of which waited for: 4 -> 3; matrix products, arithmetic and copies ran while one was open for 2% -> 1% of each run, Pallas kernels for 44% -> 42%
where the time goes in v3:
time: 120 us
  Pallas kernels  63.1 us (53%)
  waiting for transfers between devices  21.9 us (18%)
  blocking collectives  19.8 us (16%)
  starting transfers between devices  13 us (11%)
  local copies, waits for them, and re-layouts  1.71 us (1%)
    pallas_call x1, Pallas kernels, on_device(): pl.pallas_call(extend_kernel, out_shape=(f32(2 * JS, NRING), f32(half_lin...  49.3 us
    all_to_all x1, blocking collectives, exchange(): lax.all_to_all(value, 'limb', split_axis=0, concat_axis=0, tiled=True)  19.8 us
    ppermute x3, waiting for transfers between devices, on_device(): lax.ppermute(pair, 'limb', [(source, (source + 2 * step) % LIMBS) for sou...  19.4 us
    pallas_call x1, Pallas kernels, on_device(): pl.pallas_call(finish_kernel, out_shape=f32(1, JS - 1, 2, NRING), in_spec...  6.02 us
    ppermute x3, starting transfers between devices, on_device(): lax.ppermute(pair, 'limb', [(source, (source + 2 * step) % LIMBS) for sou...  5.36 us
    pallas_call x1, Pallas kernels, on_device(): pl.pallas_call(inverse_kernel, out_shape=jax.ShapeDtypeStruct((1, (JS - 1...  3.36 us
    ppermute x1, starting transfers between devices, on_device(): lax.ppermute(coefs, 'limb', [(source, source ^ 1) for source in range(LIM...  3.28 us
    pallas_call x1, Pallas kernels, on_device(): pl.pallas_call(combine_kernel, grid=(half_lines // BLOCKS,), out_shape=(f...  3.07 us
  transfers between devices with their start and end apart: 6, of which 3 were waited for; matrix products, arithmetic and copies ran while one was open for 1% of the time, Pallas kernels for 42%

profile of v3, /device:TPU:0, one launch (start us, length us, event | category | flops | bytes accessed | tf_op | source)
XLA Modules:
  0.0 119.9 jit_solution(5714373292892453005)
XLA Ops:
  0.0 0.0 copy-start.9
  0.0 3.4 %coefficients.1 = s16[1,400,256]{2,1,0:T(8,128)(2,1)} custom-call(s32[1]{0:T(128)} %bitcast.lead_ref, s32[32]{0:T(128)} %exp_ref.7, f32[1,3,2,32768]{3,2,1,0:T(2,128)} %bitcast.4, f32[128,128]{1,0:T(8,128)} %constant.18.clone.ha_ref, f32[256,256]{1,0:T(8,128)} %constant.19.clone.hb_ref), custom_call_target="tpu_custom_call" | custom-call | flops 2000000000 | bytes 1048576 | tf_op jit(solution)/shard_map/coefficients/pallas_call | solution.py:354
  3.4 0.0 copy-start.8
  3.4 3.3 %collective-permute-start.1 = (s16[1,400,256]{2,1,0:T(8,128)(2,1)}, s16[1,400,256]{2,1,0:T(8,128)(2,1)S(1)}, u32[]{:S(2)}, u32[]{:S(2)}) collective-permute-start(s16[1,400,256]{2,1,0:T(8,128)(2,1)} %coefficients.1), channel_id=1, source_target_pairs={{0,1},{1,0},{2,3},{3,2},{4,5},{5,4},{6,7},{7,6},{8,9},{9,8},{10,11... | collective-permute-start | bytes 614408 | tf_op jit(solution)/shard_map/ppermute | solution.py:364
  6.6 0.0 copy-done.9
  6.6 0.6 copy.13.ks_ref
  7.3 0.0 copy-done.8
  7.3 0.0 copy-start.1
  7.3 0.0 copy-start.2
  7.3 1.0 copy.12.km_ref
  8.3 0.0 copy-done.1
  8.3 0.0 copy-done.2
  8.3 0.0 copy-start.11
  8.3 0.0 copy-start.10
  8.4 1.3 %pack_keys.1.keys_ref = bf16[32,32768]{1,0:T(8,128)(2,1)S(1)} custom-call(bf16[1,2,3,3,32768]{4,3,2,1,0:T(4,128)(2,1)S(1)} %copy.12.km_ref, bf16[1,2,3,1,32768]{4,3,2,1,0:T(2,128)(2,1)S(1)} %copy.13.ks_ref, bf16[1,3,32768]{2,1,0:T(4,128)(2,1)S(1)} %copy-done.1, bf16[1,1,32768]{2,1,0:T(2,128)(2,1)S(1)} %copy-done.2), custom_call_target="tpu_custom_call" | custom-call | flops 2000000000 | bytes 1048576 | tf_op jit(solution)/shard_map/pack_keys/pallas_call | solution.py:376
  9.7 0.0 copy-start
  9.7 0.0 copy-start.3
  9.7 0.0 copy-start.4
  9.7 0.0 copy-start.5
  9.7 0.0 copy-start.6
  9.8 0.0 copy-done.11
  9.8 2.1 %collective-permute-start = (s32[32768]{0:T(1024)S(1)}, s32[32768]{0:T(1024)S(1)}, u32[]{:S(2)}, u32[]{:S(2)}) collective-permute-start(s32[32768]{0:T(1024)S(1)} %bitcast.6), channel_id=1, source_target_pairs={{8,0},{16,8},{24,16},{32,24},{40,32},{48,40},{56,48},{64,56},{72,6... | collective-permute-start | bytes 393224 | tf_op jit(solution)/shard_map/ppermute | solution.py:393
  11.9 2.5 %collective-permute-done = s32[32768]{0:T(1024)S(1)} collective-permute-done((s32[32768]{0:T(1024)S(1)}, s32[32768]{0:T(1024)S(1)}, u32[]{:S(2)}, u32[]{:S(2)}) %collective-permute-start) | collective-permute-done | bytes 131104 | tf_op jit(solution)/shard_map/ppermute | solution.py:393
  14.4 0.0 collective-permute-done.1
  14.4 0.0 copy-done.10
  14.5 4.1 %collective-permute-start.4 = (s16[2,400,256]{2,1,0:T(8,128)(2,1)S(1)}, s16[2,400,256]{2,1,0:T(8,128)(2,1)S(1)}, u32[]{:S(2)}, u32[]{:S(2)}) collective-permute-start(s16[2,400,256]{2,1,0:T(8,128)(2,1)S(1)} %pad_add_fusion.held0_ref), channel_id=1, source_target_pairs={{0,6},{1,7},{2,0},{3,1},{4,2},{5,3},{6,4},{7,5},{8,14},{9,15},{10,... | collective-permute-start | bytes 1228808 | tf_op jit(solution)/shard_map/ppermute | solution.py:366
  18.6 0.0 collective-permute-start.3
  18.6 1.3 %collective-permute-start.2 = (s16[2,400,256]{2,1,0:T(8,128)(2,1)S(1)}, s16[2,400,256]{2,1,0:T(8,128)(2,1)S(1)}, u32[]{:S(2)}, u32[]{:S(2)}) collective-permute-start(s16[2,400,256]{2,1,0:T(8,128)(2,1)S(1)} %pad_add_fusion.held0_ref), channel_id=1, source_target_pairs={{0,2},{1,3},{2,4},{3,5},{4,6},{5,7},{6,0},{7,1},{8,10},{9,11},{10,... | collective-permute-start | bytes 1228808 | tf_op jit(solution)/shard_map/ppermute | solution.py:366
  19.8 0.1 and_add_fusion.idx_ref
  19.9 16.0 %collective-permute-done.4.held3_ref = s16[2,400,256]{2,1,0:T(8,128)(2,1)S(1)} collective-permute-done((s16[2,400,256]{2,1,0:T(8,128)(2,1)S(1)}, s16[2,400,256]{2,1,0:T(8,128)(2,1)S(1)}, u32[]{:S(2)}, u32[]{:S(2)}) %collective-permute-start.4) | collective-permute-done | bytes 409632 | tf_op jit(solution)/shard_map/ppermute | solution.py:366
  35.9 0.0 collective-permute-done.3.held2_ref
  35.9 3.4 %collective-permute-done.2.held1_ref = s16[2,400,256]{2,1,0:T(8,128)(2,1)S(1)} collective-permute-done((s16[2,400,256]{2,1,0:T(8,128)(2,1)S(1)}, s16[2,400,256]{2,1,0:T(8,128)(2,1)S(1)}, u32[]{:S(2)}, u32[]{:S(2)}) %collective-permute-start.2) | collective-permute-done | bytes 409632 | tf_op jit(solution)/shard_map/ppermute | solution.py:366
  39.4 2.3 %collective-permute-start.5 = (bf16[32,32768]{1,0:T(8,128)(2,1)S(1)}, bf16[32,32768]{1,0:T(8,128)(2,1)S(1)}, u32[]{:S(2)}, u32[]{:S(2)}) collective-permute-start(bf16[32,32768]{1,0:T(8,128)(2,1)S(1)} %pack_keys.1.keys_ref), channel_id=1, source_target_pairs={{8,0},{16,8},{24,16},{32,24},{40,32},{48,40},{56,48},{64,56},{72,6... | collective-permute-start | bytes 6291464 | tf_op jit(solution)/shard_map/ppermute | solution.py:395
  41.7 0.0 copy-done
  41.7 0.0 copy-done.3
  41.7 0.0 copy-done.4
  41.7 0.0 copy-done.5
  41.7 0.0 copy-done.6
  41.7 49.3 %extend_and_gather.1 = (f32[8,32768]{1,0:T(8,128)S(1)}, f32[32,128,128]{2,1,0:T(8,128)S(1)}) custom-call(s32[1]{0:T(128)} %bitcast.lead_ref, s32[32]{0:T(128)S(1)} %copy-done.4, f32[24,32]{1,0:T(8,128)S(1)} %copy-done.3, s32[65536]{0:T(1024)S(1)} %and_add_fusion.idx_ref, f32[1,3,2,32768]{3,2,1,0:T(2,128)S(1)} %bitcast.5, f32[128,128]{1,0:T(8,128)S(1)} %copy-done.6, ...), custom_call_target="tpu_custom_call" | custom-call | flops 49999998976 | bytes 1048576 | tf_op jit(solution)/shard_map/extend_and_gather/pallas_call | solution.py:398
  91.0 0.0 collective-permute-done.5.keys_ref
  91.0 3.1 %switch_next.1 = (f32[8,32768]{1,0:T(8,128)S(1)}, s16[8,272,256]{2,1,0:T(8,128)(2,1)S(1)}) custom-call(s32[1]{0:T(128)} %bitcast.lead_ref, s32[32]{0:T(128)S(1)} %copy-done.4, f32[32,128,128]{2,1,0:T(8,128)S(1)} %get-tuple-element.33.got_ref, f32[128,128]{1,0:T(8,128)S(1)} %copy-done.6, f32[256,256]{1,0:T(8,128)S(1)} %copy-done.5, ...), custom_call_target="tpu_custom_call" | custom-call | flops 4000000000 | bytes 1048576 | tf_op jit(solution)/shard_map/switch_next/pallas_call | solution.py:421
  94.1 0.0 copy-start.7
  94.1 19.8 %all_to_all.5.held_ref = s16[8,272,256]{2,1,0:T(8,128)(2,1)} all-to-all(s16[8,272,256]{2,1,0:T(8,128)(2,1)S(1)} %get-tuple-element.36), channel_id=1, replica_groups=mesh['key'=16,'limb'=8] {'limb'}, dimensions={0} | all-to-all | bytes 2228224 | tf_op jit(solution)/shard_map/all_to_all | solution.py:332
  113.9 0.0 copy-done.7
  113.9 6.0 %finish.1 = f32[1,3,2,32768]{3,2,1,0:T(2,128)} custom-call(s32[1]{0:T(128)} %bitcast.lead_ref, s32[32]{0:T(128)} %exp_ref.7, f32[8,24]{1,0:T(8,128)} %down_ref.1, f32[8,32768]{1,0:T(8,128)} %copy-done.7, f32[128,128]{1,0:T(8,128)} %constant.18.clone.ha_ref, f32[256,256]{1,0:T(8,128)} %constant.19.clone.hb_ref, s16[8,272,256]{2,1,0:T(8,128)(2,1)} %all_to_all.5.held_ref), custom_call_target="tpu_custom_call" | custom-call | flops 4000000000 | bytes 1048576 | tf_op jit(solution)/shard_map/finish/pallas_call | solution.py:441
  (3 shorter events, 0.0 us)
Async XLA Ops:
  0.0 6.6 %copy-start.9 = (bf16[1,2,3,1,32768]{4,1,3,2,0:T(2,128)(2,1)S(1)}, bf16[1,2,3,1,32768]{4,1,3,2,0:T(2,128)(2,1)}, u32[]{:S(2)}) copy-start(bf16[1,2,3,1,32768]{4,1,3,2,0:T(2,128)(2,1)} %param.13) | copy-start | bytes 1179652
  3.4 3.9 %copy-start.8 = (bf16[1,2,3,3,32768]{4,1,3,2,0:T(2,128)(2,1)S(1)}, bf16[1,2,3,3,32768]{4,1,3,2,0:T(2,128)(2,1)}, u32[]{:S(2)}) copy-start(bf16[1,2,3,3,32768]{4,1,3,2,0:T(2,128)(2,1)} %param.12) | copy-start | bytes 3538948
  3.4 11.0 %collective-permute-start.1 = (s16[1,400,256]{2,1,0:T(8,128)(2,1)}, s16[1,400,256]{2,1,0:T(8,128)(2,1)S(1)}, u32[]{:S(2)}, u32[]{:S(2)}) collective-permute-start(s16[1,400,256]{2,1,0:T(8,128)(2,1)} %coefficients.1), channel_id=1, source_target_pairs={{0,1},{1,0},{2,3},{3,2},{4,5},{5,4},{6,7},{7,6},{8,9},{9,8},{10,11... | collective-permute-start | bytes 614408 | tf_op jit(solution)/shard_map/ppermute | solution.py:364
  7.3 1.0 copy-start.1
  7.3 1.0 copy-start.2
  8.3 1.4 %copy-start.11 = (s32[1,32768]{1,0:T(1,128)S(1)}, s32[1,32768]{1,0:T(1,128)}, u32[]{:S(2)}) copy-start(s32[1,32768]{1,0:T(1,128)} %param.16) | copy-start | bytes 393220
  8.3 6.1 %copy-start.10 = (s16[1,400,256]{2,1,0:T(8,128)(2,1)S(1)}, s16[1,400,256]{2,1,0:T(8,128)(2,1)}, u32[]{:S(2)}) copy-start(s16[1,400,256]{2,1,0:T(8,128)(2,1)} %coefficients.1) | copy-start | bytes 614404
  9.7 32.0 %copy-start = (f32[1,2,3,32768]{3,1,2,0:T(2,128)S(1)}, f32[1,2,3,32768]{3,1,2,0:T(2,128)}, u32[]{:S(2)}) copy-start(f32[1,2,3,32768]{3,1,2,0:T(2,128)} %param.11) | copy-start | bytes 2359300
  9.7 32.0 %copy-start.3 = (f32[24,32]{1,0:T(8,128)S(1)}, f32[24,32]{1,0:T(8,128)}, u32[]{:S(2)}) copy-start(f32[24,32]{1,0:T(8,128)} %up_ref.1) | copy-start | bytes 9220
  9.7 31.9 %copy-start.4 = (s32[32]{0:T(128)S(1)}, s32[32]{0:T(128)}, u32[]{:S(2)}) copy-start(s32[32]{0:T(128)} %exp_ref.7) | copy-start | bytes 388
  9.7 31.9 %copy-start.5 = (f32[256,256]{1,0:T(8,128)S(1)}, f32[256,256]{1,0:T(8,128)}, u32[]{:S(2)}) copy-start(f32[256,256]{1,0:T(8,128)} %constant.19.clone.hb_ref) | copy-start | bytes 786436
  9.7 31.9 %copy-start.6 = (f32[128,128]{1,0:T(8,128)S(1)}, f32[128,128]{1,0:T(8,128)}, u32[]{:S(2)}) copy-start(f32[128,128]{1,0:T(8,128)} %constant.18.clone.ha_ref) | copy-start | bytes 196612
  9.8 4.6 %collective-permute-start = (s32[32768]{0:T(1024)S(1)}, s32[32768]{0:T(1024)S(1)}, u32[]{:S(2)}, u32[]{:S(2)}) collective-permute-start(s32[32768]{0:T(1024)S(1)} %bitcast.6), channel_id=1, source_target_pairs={{8,0},{16,8},{24,16},{32,24},{40,32},{48,40},{56,48},{64,56},{72,6... | collective-permute-start | bytes 393224 | tf_op jit(solution)/shard_map/ppermute | solution.py:393
  14.5 21.5 %collective-permute-start.4 = (s16[2,400,256]{2,1,0:T(8,128)(2,1)S(1)}, s16[2,400,256]{2,1,0:T(8,128)(2,1)S(1)}, u32[]{:S(2)}, u32[]{:S(2)}) collective-permute-start(s16[2,400,256]{2,1,0:T(8,128)(2,1)S(1)} %pad_add_fusion.held0_ref), channel_id=1, source_target_pairs={{0,6},{1,7},{2,0},{3,1},{4,2},{5,3},{6,4},{7,5},{8,14},{9,15},{10,... | collective-permute-start | bytes 1228808 | tf_op jit(solution)/shard_map/ppermute | solution.py:366
  18.6 17.4 %collective-permute-start.3 = (s16[2,400,256]{2,1,0:T(8,128)(2,1)S(1)}, s16[2,400,256]{2,1,0:T(8,128)(2,1)S(1)}, u32[]{:S(2)}, u32[]{:S(2)}) collective-permute-start(s16[2,400,256]{2,1,0:T(8,128)(2,1)S(1)} %pad_add_fusion.held0_ref), channel_id=1, source_target_pairs={{0,4},{1,5},{2,6},{3,7},{4,0},{5,1},{6,2},{7,3},{8,12},{9,13},{10,... | collective-permute-start | bytes 1228808 | tf_op jit(solution)/shard_map/ppermute | solution.py:366
  18.6 20.8 %collective-permute-start.2 = (s16[2,400,256]{2,1,0:T(8,128)(2,1)S(1)}, s16[2,400,256]{2,1,0:T(8,128)(2,1)S(1)}, u32[]{:S(2)}, u32[]{:S(2)}) collective-permute-start(s16[2,400,256]{2,1,0:T(8,128)(2,1)S(1)} %pad_add_fusion.held0_ref), channel_id=1, source_target_pairs={{0,2},{1,3},{2,4},{3,5},{4,6},{5,7},{6,0},{7,1},{8,10},{9,11},{10,... | collective-permute-start | bytes 1228808 | tf_op jit(solution)/shard_map/ppermute | solution.py:366
  39.4 51.7 %collective-permute-start.5 = (bf16[32,32768]{1,0:T(8,128)(2,1)S(1)}, bf16[32,32768]{1,0:T(8,128)(2,1)S(1)}, u32[]{:S(2)}, u32[]{:S(2)}) collective-permute-start(bf16[32,32768]{1,0:T(8,128)(2,1)S(1)} %pack_keys.1.keys_ref), channel_id=1, source_target_pairs={{8,0},{16,8},{24,16},{32,24},{40,32},{48,40},{56,48},{64,56},{72,6... | collective-permute-start | bytes 6291464 | tf_op jit(solution)/shard_map/ppermute | solution.py:395
  94.1 19.8 %copy-start.7 = (f32[8,32768]{1,0:T(8,128)}, f32[8,32768]{1,0:T(8,128)S(1)}, u32[]{:S(2)}) copy-start(f32[8,32768]{1,0:T(8,128)S(1)} %get-tuple-element.35.sum_ref) | copy-start | bytes 3145732

commit v4 on v3

--- a/solution.py
+++ b/solution.py
@@ -21,7 +21,7 @@
 LN2 = math.log(2.0)
 LINE = 1024
 SLOTS = 4
-CHIPS_Z = 4
+STEPS = ((0, 0), (3, 0), (1, 0), (0, 1), (2, 0), (3, 1), (1, 1), (2, 1))
 BLOCKS = 4
 ROTS = 2
 TAIL = 16
@@ -93,14 +93,20 @@
     return (root * jnp.abs(root)) * (root * root) * gain
 
 
+def partner(lead, step, sign):
+    z = (lead // 2 + LIMBS + sign * step[0]) % (LIMBS // 2)
+    return z * 2 + (lead + step[1]) % 2
+
+
 def inverse_kernel(lead_ref, exp_ref, cipher_ref, ha_ref, hb_ref, out_ref, x_ref):
     def spread(step, _):
-        for limb in range(JS - 1):
-            rows = [cipher_ref[0, limb, 1:2, pl.ds(pl.multiple_of((step * 8 + k) * B, B), B)] for k in range(8)]
-            x_ref[limb, pl.ds(pl.multiple_of(step * 8, 8), 8), :] = jnp.concatenate(rows, axis=0)
-        return 0
-
-    lax.fori_loop(0, A // 8, spread, 0)
+        for at in (step * 16, step * 16 + 8):
+            for limb in range(JS - 1):
+                rows = [cipher_ref[0, limb, 1:2, pl.ds(pl.multiple_of((at + k) * B, B), B)] for k in range(8)]
+                x_ref[limb, pl.ds(pl.multiple_of(at, 8), 8), :] = jnp.concatenate(rows, axis=0)
+        return 0
+
+    lax.fori_loop(0, A // 16, spread, 0)
     h_a, h_b = parts(ha_ref[...]), parts(hb_ref[...])
     done = []
     for limb in range(JS - 1):
@@ -149,9 +155,9 @@
 
 
 def extend_kernel(
-    lead_ref, exp_ref, up_ref, idx_ref, base_ref, ha_ref, hb_ref, keys_ref, held0_ref, held1_ref, held2_ref, held3_ref,
-    sum_ref, got_ref, coef_ref, raised_ref, rows_ref, turns_ref, ext_ref, *rest,
+    lead_ref, exp_ref, up_ref, idx_ref, base_ref, ha_ref, hb_ref, keys_ref, *rest,
 ):
+    held, (sum_ref, got_ref, coef_ref, raised_ref, rows_ref, turns_ref, ext_ref, *rest) = rest[:LIMBS], rest[LIMBS:]
     slots, got, arrive = rest[:SLOTS], rest[SLOTS : 2 * SLOTS], rest[-1]
     chunks = ROTS * NRING // LINE
 
@@ -162,11 +168,10 @@
     for slot in range(SLOTS):
         fetch(slot, slot).start()
     lead = lead_ref[0]
-    for step, held_ref in enumerate((held0_ref, held1_ref, held2_ref, held3_ref)):
-        for across in range(2):
-            source = (lead // 2 + CHIPS_Z - step) % CHIPS_Z * 2 + (lead + across) % 2
-            for limb in range(JS - 1):
-                coef_ref[source * (JS - 1) + limb] = received(held_ref, across, limb)
+    for step, held_ref in zip(STEPS, held):
+        source = partner(lead, step, -1)
+        for limb in range(JS - 1):
+            coef_ref[source * (JS - 1) + limb] = received(held_ref, 0, limb)
 
     def lift(step, _):
         rows = pl.ds(pl.multiple_of(step * CHUNK, CHUNK), CHUNK)
@@ -193,14 +198,15 @@
             rows_ref[0, pl.ds(ch, A, stride=16), :] = done[:, :128]
             rows_ref[1, pl.ds(ch, A, stride=16), :] = done[:, 128:]
 
-    def first(i, _):
-        for half in range(2):
+    def first(step, _):
+        for k in range(8):
+            i, half = step * 4 + k // 2, k % 2
             lanes = pl.ds(pl.multiple_of(i * B + half * 128, 128), 128)
             lines = [base_ref[0, limb, 0:1, lanes] for limb in range(JS - 1)] + [jnp.zeros((1, 128), jnp.float32)]
             rows_ref[half, pl.ds(pl.multiple_of(i * 16 + 8, 8) + 4, 4), :] = jnp.concatenate(lines, axis=0)
         return 0
 
-    lax.fori_loop(0, A, first, 0)
+    lax.fori_loop(0, A // 4, first, 0)
 
     source = lax.broadcasted_iota(jnp.int32, (2 * 128, 128), 0) & 127
     target = lax.broadcasted_iota(jnp.int32, (2 * 128, 128), 1)
@@ -209,16 +215,16 @@
         turns_ref[:, by * 128 : (by + 1) * 128] = ones.astype(jnp.bfloat16)
 
     def turn(step, _):
-        for half in range(2):
-            block = rows_ref[half, pl.ds(pl.multiple_of(step * 128, 128), 128), :].T
-            both = jnp.concatenate(parts(block), axis=1)
+        for k in range(4):
+            at = pl.ds(pl.multiple_of(step * 256 + k // 2 * 128, 128), 128)
+            both = jnp.concatenate(parts(rows_ref[k % 2, at, :].T), axis=1)
             turned = jnp.dot(both, turns_ref[...], preferred_element_type=jnp.float32)
             for by in range(8):
-                at = pl.ds(pl.multiple_of(by * (NRING // 8) + step * B + half * 128, 128), 128)
+                at = pl.ds(pl.multiple_of(by * (NRING // 8) + step * (2 * B) + k * 128, 128), 128)
                 ext_ref[at, :] = turned[:, by * 128 : (by + 1) * 128]
         return 0
 
-    lax.fori_loop(0, A // 8, turn, 0)
+    lax.fori_loop(0, A // 16, turn, 0)
 
 
     group = lax.broadcasted_iota(jnp.int32, (1, 128), 1) // 16
@@ -317,15 +323,16 @@
             rows_ref[0, pl.ds(p * JS + j, A, stride=8), :] = done[:, :128]
             rows_ref[1, pl.ds(p * JS + j, A, stride=8), :] = done[:, 128:]
 
-    def body(i, _):
-        for half in range(2):
+    def body(step, _):
+        for k in range(8):
+            i, half = step * 4 + k // 2, k % 2
             lanes = pl.ds(pl.multiple_of(i * B + half * 128, 128), 128)
             left = sum_ref[:, lanes] - rows_ref[half, pl.ds(pl.multiple_of(i * 8, 8), 8), :]
             for j in range(JS - 1):
                 out_ref[0, j, :, lanes] = jnp.concatenate([left[j : j + 1], left[JS + j : JS + j + 1]], axis=0)
         return 0
 
-    lax.fori_loop(0, A, body, 0)
+    lax.fori_loop(0, A // 4, body, 0)
 
 
 def exchange(value):
@@ -361,16 +368,15 @@
         cost_estimate=cost(2),
         name="coefficients",
     )(lead, tw_exp, cipher, h_a, h_b)
-    pair = jnp.concatenate([coefs, lax.ppermute(coefs, "limb", [(source, source ^ 1) for source in range(LIMBS)])])
-    held = [pair] + [
-        lax.ppermute(pair, "limb", [(source, (source + 2 * step) % LIMBS) for source in range(LIMBS)])
-        for step in range(1, CHIPS_Z)
+    held = [coefs] + [
+        lax.ppermute(coefs, "limb", [(source, partner(source, step, 1)) for source in range(LIMBS)])
+        for step in STEPS[1:]
     ]
 
     count = lax.axis_size("key")
     ahead = [((target + 1) % count, target) for target in range(count)]
-    key_main, key_special, diag_main, diag_special, _ = lax.optimization_barrier(
-        (key_main, key_special, diag_main, diag_special, coefs)
+    key_main, key_special, diag_main, diag_special, perm_own, held[-1] = lax.optimization_barrier(
+        (key_main, key_special, diag_main, diag_special, perms[0], held[-1])
     )
     lanes = NRING // 4
     packed = pl.pallas_call(
@@ -389,7 +395,6 @@
         cost_estimate=cost(2),
         name="pack_keys",
     )(key_main, key_special, diag_main, diag_special)
-    perm_own, packed = lax.optimization_barrier((perms[0], packed))
     both_rows = rows_of(jnp.concatenate([perm_own, lax.ppermute(perm_own, "key", ahead)]))
     packed, both_rows, *held = lax.optimization_barrier((packed, both_rows, *held))
     packed_next = lax.ppermute(packed, "key", ahead)
@@ -398,7 +403,7 @@
     first, gathered = pl.pallas_call(
         extend_kernel,
         out_shape=(f32(2 * JS, NRING), f32(half_lines, 128, 128)),
-        in_specs=[SMEM] * 3 + [pl.BlockSpec(memory_space=pl.ANY)] + [VMEM] * 8,
+        in_specs=[SMEM] * 3 + [pl.BlockSpec(memory_space=pl.ANY)] + [VMEM] * (4 + LIMBS),
         out_specs=(VMEM, VMEM),
         scratch_shapes=[
             pltpu.VMEM((LIMBS * (JS - 1), A, B), jnp.float32),

time: 120 us -> 111 us (0.925)
  waiting for transfers between devices: 21.9 us -> 5.51 us
  starting transfers between devices: 13 us -> 22.1 us
  Pallas kernels: 63.1 us -> 60.3 us
    ppermute x4 -> x7, waiting for transfers between devices: 19.4 us -> 5.51 us  [on_device(): lax.ppermute(coefs, 'limb', [(source, partner(source, step, 1)) for sourc...]
    ppermute x4 -> x7, starting transfers between devices: 8.64 us -> 15.6 us  [on_device(): lax.ppermute(coefs, 'limb', [(source, partner(source, step, 1)) for sourc...]
    ppermute x1, waiting for transfers between devices: 2.51 us -> 0.01 us  [on_device(): lax.ppermute(perm_own, 'key', ahead)]
    pallas_call x1, Pallas kernels: 49.3 us -> 47.1 us  [on_device(): pl.pallas_call(extend_kernel, out_shape=(f32(2 * JS, NRING), f32(half_lin...]
    ppermute x1, starting transfers between devices: 2.29 us -> 4.49 us  [on_device(): packed_next = lax.ppermute(packed, 'key', ahead)]
  transfers between devices with their start and end apart: 6 -> 9, of which waited for: 3 -> 5; matrix products, arithmetic and copies ran while one was open for 1% -> 2% of each run, Pallas kernels for 42% -> 44%
where the time goes in v4:
time: 111 us
  Pallas kernels  60.3 us (54%)
  starting transfers between devices  22.1 us (20%)
  blocking collectives  20.8 us (19%)
  waiting for transfers between devices  5.51 us (5%)
  local copies, waits for them, and re-layouts  1.71 us (2%)
    pallas_call x1, Pallas kernels, on_device(): pl.pallas_call(extend_kernel, out_shape=(f32(2 * JS, NRING), f32(half_lin...  47.1 us
    all_to_all x1, blocking collectives, exchange(): lax.all_to_all(value, 'limb', split_axis=0, concat_axis=0, tiled=True)  20.8 us
    ppermute x7, starting transfers between devices, on_device(): lax.ppermute(coefs, 'limb', [(source, partner(source, step, 1)) for sourc...  15.6 us
    ppermute x7, waiting for transfers between devices, on_device(): lax.ppermute(coefs, 'limb', [(source, partner(source, step, 1)) for sourc...  5.51 us
    pallas_call x1, Pallas kernels, on_device(): pl.pallas_call(finish_kernel, out_shape=f32(1, JS - 1, 2, NRING), in_spec...  5.49 us
    ppermute x1, starting transfers between devices, on_device(): packed_next = lax.ppermute(packed, 'key', ahead)  4.49 us
    pallas_call x1, Pallas kernels, on_device(): pl.pallas_call(inverse_kernel, out_shape=jax.ShapeDtypeStruct((1, (JS - 1...  3.34 us
    pallas_call x1, Pallas kernels, on_device(): pl.pallas_call(combine_kernel, grid=(half_lines // BLOCKS,), out_shape=(f...  3.07 us
  transfers between devices with their start and end apart: 9, of which 5 were waited for; matrix products, arithmetic and copies ran while one was open for 2% of the time, Pallas kernels for 44%

profile of v4, /device:TPU:0, one launch (start us, length us, event | category | flops | bytes accessed | tf_op | source)
XLA Modules:
  0.0 110.7 jit_solution(6972623203872726766)
XLA Ops:
  0.0 0.0 copy-start.11
  0.0 0.0 copy-start.10
  0.0 3.3 %coefficients.1.rest_0_ = s16[1,400,256]{2,1,0:T(8,128)(2,1)} custom-call(s32[1]{0:T(128)} %bitcast.lead_ref, s32[32]{0:T(128)} %exp_ref.7, f32[1,3,2,32768]{3,2,1,0:T(2,128)} %bitcast.4, f32[128,128]{1,0:T(8,128)} %constant.18.clone.ha_ref, f32[256,256]{1,0:T(8,128)} %constant.19.clone.hb_ref), custom_call_target="tpu_custom_call" | custom-call | flops 2000000000 | bytes 1048576 | tf_op jit(solution)/shard_map/coefficients/pallas_call | solution.py:361
  3.3 0.0 copy-start.9
  3.4 6.6 %collective-permute-start = (s16[1,400,256]{2,1,0:T(8,128)(2,1)}, s16[1,400,256]{2,1,0:T(8,128)(2,1)S(1)}, u32[]{:S(2)}, u32[]{:S(2)}) collective-permute-start(s16[1,400,256]{2,1,0:T(8,128)(2,1)} %coefficients.1.rest_0_), channel_id=1, source_target_pairs={{0,5},{1,4},{2,7},{3,6},{4,1},{5,0},{6,3},{7,2},{8,13},{9,12},{10,... | collective-permute-start | bytes 614408 | tf_op jit(solution)/shard_map/ppermute | solution.py:372
  9.9 0.8 collective-permute-start.7
  10.7 4.8 %collective-permute-start.6 = (s16[1,400,256]{2,1,0:T(8,128)(2,1)}, s16[1,400,256]{2,1,0:T(8,128)(2,1)S(1)}, u32[]{:S(2)}, u32[]{:S(2)}) collective-permute-start(s16[1,400,256]{2,1,0:T(8,128)(2,1)} %coefficients.1.rest_0_), channel_id=1, source_target_pairs={{0,7},{1,6},{2,1},{3,0},{4,3},{5,2},{6,5},{7,4},{8,15},{9,14},{10,... | collective-permute-start | bytes 614408 | tf_op jit(solution)/shard_map/ppermute | solution.py:372
  15.6 0.0 collective-permute-start.5
  15.6 0.4 collective-permute-start.4
  16.0 0.0 collective-permute-done.rest_7_
  16.0 0.0 copy-done.11
  16.0 2.0 %collective-permute-start.1 = (s32[32768]{0:T(1024)S(1)}, s32[32768]{0:T(1024)S(1)}, u32[]{:S(2)}, u32[]{:S(2)}) collective-permute-start(s32[32768]{0:T(1024)S(1)} %bitcast.6), channel_id=1, source_target_pairs={{8,0},{16,8},{24,16},{32,24},{40,32},{48,40},{56,48},{64,56},{72,6... | collective-permute-start | bytes 393224 | tf_op jit(solution)/shard_map/ppermute | solution.py:398
  18.0 0.0 copy-done.10
  18.0 0.6 copy.13.ks_ref
  18.7 0.0 copy-done.9
  18.7 0.0 copy-start.1
  18.7 0.0 copy-start.3
  18.7 1.0 copy.12.km_ref
  19.7 0.0 copy-done.1
  19.7 0.0 copy-done.3
  19.7 0.0 copy-start.2
  19.7 0.0 copy-start
  19.8 0.0 copy-start.4
  19.8 0.0 copy-start.5
  19.8 0.0 copy-start.6
  19.8 0.0 copy-start.7
  19.8 1.3 %pack_keys.1.keys_ref = bf16[32,32768]{1,0:T(8,128)(2,1)S(1)} custom-call(bf16[1,2,3,3,32768]{4,3,2,1,0:T(4,128)(2,1)S(1)} %copy.12.km_ref, bf16[1,2,3,1,32768]{4,3,2,1,0:T(2,128)(2,1)S(1)} %copy.13.ks_ref, bf16[1,3,32768]{2,1,0:T(4,128)(2,1)S(1)} %copy-done.1, bf16[1,1,32768]{2,1,0:T(2,128)(2,1)S(1)} %copy-done.3), custom_call_target="tpu_custom_call" | custom-call | flops 2000000000 | bytes 1048576 | tf_op jit(solution)/shard_map/pack_keys/pallas_call | solution.py:382
  21.1 0.0 collective-permute-done.1
  21.2 0.0 copy-done.2
  21.2 0.7 collective-permute-start.3
  21.9 0.4 collective-permute-done.7.rest_6_
  22.3 2.3 %collective-permute-start.2 = (s16[1,400,256]{2,1,0:T(8,128)(2,1)S(1)}, s16[1,400,256]{2,1,0:T(8,128)(2,1)S(1)}, u32[]{:S(2)}, u32[]{:S(2)}) collective-permute-start(s16[1,400,256]{2,1,0:T(8,128)(2,1)S(1)} %copy-done.2), channel_id=1, source_target_pairs={{0,6},{1,7},{2,0},{3,1},{4,2},{5,3},{6,4},{7,5},{8,14},{9,15},{10,... | collective-permute-start | bytes 614408 | tf_op jit(solution)/shard_map/ppermute | solution.py:372
  24.6 0.1 and_add_fusion.idx_ref
  24.7 1.2 %collective-permute-done.6.rest_5_ = s16[1,400,256]{2,1,0:T(8,128)(2,1)S(1)} collective-permute-done((s16[1,400,256]{2,1,0:T(8,128)(2,1)}, s16[1,400,256]{2,1,0:T(8,128)(2,1)S(1)}, u32[]{:S(2)}, u32[]{:S(2)}) %collective-permute-start.6) | collective-permute-done | bytes 204832 | tf_op jit(solution)/shard_map/ppermute | solution.py:372
  25.8 0.0 collective-permute-done.5.rest_4_
  25.9 2.9 %collective-permute-done.4.rest_3_ = s16[1,400,256]{2,1,0:T(8,128)(2,1)S(1)} collective-permute-done((s16[1,400,256]{2,1,0:T(8,128)(2,1)}, s16[1,400,256]{2,1,0:T(8,128)(2,1)S(1)}, u32[]{:S(2)}, u32[]{:S(2)}) %collective-permute-start.4) | collective-permute-done | bytes 204832 | tf_op jit(solution)/shard_map/ppermute | solution.py:372
  28.8 0.6 collective-permute-done.3.rest_2_
  29.4 0.4 collective-permute-done.2.rest_1_
  29.7 4.5 %collective-permute-start.8 = (bf16[32,32768]{1,0:T(8,128)(2,1)S(1)}, bf16[32,32768]{1,0:T(8,128)(2,1)S(1)}, u32[]{:S(2)}, u32[]{:S(2)}) collective-permute-start(bf16[32,32768]{1,0:T(8,128)(2,1)S(1)} %pack_keys.1.keys_ref), channel_id=1, source_target_pairs={{8,0},{16,8},{24,16},{32,24},{40,32},{48,40},{56,48},{64,56},{72,6... | collective-permute-start | bytes 6291464 | tf_op jit(solution)/shard_map/ppermute | solution.py:400
  34.2 0.0 copy-done
  34.2 0.0 copy-done.4
  34.2 0.0 copy-done.5
  34.2 0.0 copy-done.6
  34.2 0.0 copy-done.7
  34.2 47.1 %extend_and_gather.1 = (f32[8,32768]{1,0:T(8,128)S(1)}, f32[32,128,128]{2,1,0:T(8,128)S(1)}) custom-call(s32[1]{0:T(128)} %bitcast.lead_ref, s32[32]{0:T(128)S(1)} %copy-done.5, f32[24,32]{1,0:T(8,128)S(1)} %copy-done.4, s32[65536]{0:T(1024)S(1)} %and_add_fusion.idx_ref, f32[1,3,2,32768]{3,2,1,0:T(2,128)S(1)} %bitcast.5, f32[128,128]{1,0:T(8,128)S(1)} %copy-done.7, ...), custom_call_target="tpu_custom_call" | custom-call | flops 49999998976 | bytes 1048576 | tf_op jit(solution)/shard_map/extend_and_gather/pallas_call | solution.py:403
  81.3 0.0 collective-permute-done.8.keys_ref
  81.3 3.1 %switch_next.1 = (f32[8,32768]{1,0:T(8,128)S(1)}, s16[8,272,256]{2,1,0:T(8,128)(2,1)S(1)}) custom-call(s32[1]{0:T(128)} %bitcast.lead_ref, s32[32]{0:T(128)S(1)} %copy-done.5, f32[32,128,128]{2,1,0:T(8,128)S(1)} %get-tuple-element.41.got_ref, f32[128,128]{1,0:T(8,128)S(1)} %copy-done.7, f32[256,256]{1,0:T(8,128)S(1)} %copy-done.6, ...), custom_call_target="tpu_custom_call" | custom-call | flops 4000000000 | bytes 1048576 | tf_op jit(solution)/shard_map/switch_next/pallas_call | solution.py:426
  84.4 0.0 copy-start.8
  84.4 20.8 %all_to_all.5.held_ref = s16[8,272,256]{2,1,0:T(8,128)(2,1)} all-to-all(s16[8,272,256]{2,1,0:T(8,128)(2,1)S(1)} %get-tuple-element.44), channel_id=1, replica_groups=mesh['key'=16,'limb'=8] {'limb'}, dimensions={0} | all-to-all | bytes 2228224 | tf_op jit(solution)/shard_map/all_to_all | solution.py:339
  105.2 0.0 copy-done.8
  105.2 5.5 %finish.1 = f32[1,3,2,32768]{3,2,1,0:T(2,128)} custom-call(s32[1]{0:T(128)} %bitcast.lead_ref, s32[32]{0:T(128)} %exp_ref.7, f32[8,24]{1,0:T(8,128)} %down_ref.1, f32[8,32768]{1,0:T(8,128)} %copy-done.8, f32[128,128]{1,0:T(8,128)} %constant.18.clone.ha_ref, f32[256,256]{1,0:T(8,128)} %constant.19.clone.hb_ref, s16[8,272,256]{2,1,0:T(8,128)(2,1)} %all_to_all.5.held_ref), custom_call_target="tpu_custom_call" | custom-call | flops 4000000000 | bytes 1048576 | tf_op jit(solution)/shard_map/finish/pallas_call | solution.py:446
  (2 shorter events, 0.0 us)
Async XLA Ops:
  0.0 16.0 %copy-start.11 = (s32[1,32768]{1,0:T(1,128)S(1)}, s32[1,32768]{1,0:T(1,128)}, u32[]{:S(2)}) copy-start(s32[1,32768]{1,0:T(1,128)} %param.16) | copy-start | bytes 393220
  0.0 18.0 %copy-start.10 = (bf16[1,2,3,1,32768]{4,1,3,2,0:T(2,128)(2,1)S(1)}, bf16[1,2,3,1,32768]{4,1,3,2,0:T(2,128)(2,1)}, u32[]{:S(2)}) copy-start(bf16[1,2,3,1,32768]{4,1,3,2,0:T(2,128)(2,1)} %param.13) | copy-start | bytes 1179652
  3.3 15.3 %copy-start.9 = (bf16[1,2,3,3,32768]{4,1,3,2,0:T(2,128)(2,1)S(1)}, bf16[1,2,3,3,32768]{4,1,3,2,0:T(2,128)(2,1)}, u32[]{:S(2)}) copy-start(bf16[1,2,3,3,32768]{4,1,3,2,0:T(2,128)(2,1)} %param.12) | copy-start | bytes 3538948
  3.4 12.7 %collective-permute-start = (s16[1,400,256]{2,1,0:T(8,128)(2,1)}, s16[1,400,256]{2,1,0:T(8,128)(2,1)S(1)}, u32[]{:S(2)}, u32[]{:S(2)}) collective-permute-start(s16[1,400,256]{2,1,0:T(8,128)(2,1)} %coefficients.1.rest_0_), channel_id=1, source_target_pairs={{0,5},{1,4},{2,7},{3,6},{4,1},{5,0},{6,3},{7,2},{8,13},{9,12},{10,... | collective-permute-start | bytes 614408 | tf_op jit(solution)/shard_map/ppermute | solution.py:372
  9.9 12.4 %collective-permute-start.7 = (s16[1,400,256]{2,1,0:T(8,128)(2,1)}, s16[1,400,256]{2,1,0:T(8,128)(2,1)S(1)}, u32[]{:S(2)}, u32[]{:S(2)}) collective-permute-start(s16[1,400,256]{2,1,0:T(8,128)(2,1)} %coefficients.1.rest_0_), channel_id=1, source_target_pairs={{0,3},{1,2},{2,5},{3,4},{4,7},{5,6},{6,1},{7,0},{8,11},{9,10},{10,... | collective-permute-start | bytes 614408 | tf_op jit(solution)/shard_map/ppermute | solution.py:372
  10.7 15.1 %collective-permute-start.6 = (s16[1,400,256]{2,1,0:T(8,128)(2,1)}, s16[1,400,256]{2,1,0:T(8,128)(2,1)S(1)}, u32[]{:S(2)}, u32[]{:S(2)}) collective-permute-start(s16[1,400,256]{2,1,0:T(8,128)(2,1)} %coefficients.1.rest_0_), channel_id=1, source_target_pairs={{0,7},{1,6},{2,1},{3,0},{4,3},{5,2},{6,5},{7,4},{8,15},{9,14},{10,... | collective-permute-start | bytes 614408 | tf_op jit(solution)/shard_map/ppermute | solution.py:372
  15.6 10.3 %collective-permute-start.5 = (s16[1,400,256]{2,1,0:T(8,128)(2,1)}, s16[1,400,256]{2,1,0:T(8,128)(2,1)S(1)}, u32[]{:S(2)}, u32[]{:S(2)}) collective-permute-start(s16[1,400,256]{2,1,0:T(8,128)(2,1)} %coefficients.1.rest_0_), channel_id=1, source_target_pairs={{0,4},{1,5},{2,6},{3,7},{4,0},{5,1},{6,2},{7,3},{8,12},{9,13},{10,... | collective-permute-start | bytes 614408 | tf_op jit(solution)/shard_map/ppermute | solution.py:372
  15.6 13.2 %collective-permute-start.4 = (s16[1,400,256]{2,1,0:T(8,128)(2,1)}, s16[1,400,256]{2,1,0:T(8,128)(2,1)S(1)}, u32[]{:S(2)}, u32[]{:S(2)}) collective-permute-start(s16[1,400,256]{2,1,0:T(8,128)(2,1)} %coefficients.1.rest_0_), channel_id=1, source_target_pairs={{0,1},{1,0},{2,3},{3,2},{4,5},{5,4},{6,7},{7,6},{8,9},{9,8},{10,11... | collective-permute-start | bytes 614408 | tf_op jit(solution)/shard_map/ppermute | solution.py:372
  16.0 5.1 %collective-permute-start.1 = (s32[32768]{0:T(1024)S(1)}, s32[32768]{0:T(1024)S(1)}, u32[]{:S(2)}, u32[]{:S(2)}) collective-permute-start(s32[32768]{0:T(1024)S(1)} %bitcast.6), channel_id=1, source_target_pairs={{8,0},{16,8},{24,16},{32,24},{40,32},{48,40},{56,48},{64,56},{72,6... | collective-permute-start | bytes 393224 | tf_op jit(solution)/shard_map/ppermute | solution.py:398
  18.7 1.0 copy-start.1
  18.7 1.0 copy-start.3
  19.7 1.4 %copy-start.2 = (s16[1,400,256]{2,1,0:T(8,128)(2,1)S(1)}, s16[1,400,256]{2,1,0:T(8,128)(2,1)}, u32[]{:S(2)}) copy-start(s16[1,400,256]{2,1,0:T(8,128)(2,1)} %coefficients.1.rest_0_) | copy-start | bytes 614404
  19.7 14.5 %copy-start = (f32[1,2,3,32768]{3,1,2,0:T(2,128)S(1)}, f32[1,2,3,32768]{3,1,2,0:T(2,128)}, u32[]{:S(2)}) copy-start(f32[1,2,3,32768]{3,1,2,0:T(2,128)} %param.11) | copy-start | bytes 2359300
  19.8 14.5 %copy-start.4 = (f32[24,32]{1,0:T(8,128)S(1)}, f32[24,32]{1,0:T(8,128)}, u32[]{:S(2)}) copy-start(f32[24,32]{1,0:T(8,128)} %up_ref.1) | copy-start | bytes 9220
  19.8 14.5 %copy-start.5 = (s32[32]{0:T(128)S(1)}, s32[32]{0:T(128)}, u32[]{:S(2)}) copy-start(s32[32]{0:T(128)} %exp_ref.7) | copy-start | bytes 388
  19.8 14.5 %copy-start.6 = (f32[256,256]{1,0:T(8,128)S(1)}, f32[256,256]{1,0:T(8,128)}, u32[]{:S(2)}) copy-start(f32[256,256]{1,0:T(8,128)} %constant.19.clone.hb_ref) | copy-start | bytes 786436
  19.8 14.4 %copy-start.7 = (f32[128,128]{1,0:T(8,128)S(1)}, f32[128,128]{1,0:T(8,128)}, u32[]{:S(2)}) copy-start(f32[128,128]{1,0:T(8,128)} %constant.18.clone.ha_ref) | copy-start | bytes 196612
  21.2 8.2 %collective-permute-start.3 = (s16[1,400,256]{2,1,0:T(8,128)(2,1)S(1)}, s16[1,400,256]{2,1,0:T(8,128)(2,1)S(1)}, u32[]{:S(2)}, u32[]{:S(2)}) collective-permute-start(s16[1,400,256]{2,1,0:T(8,128)(2,1)S(1)} %copy-done.2), channel_id=1, source_target_pairs={{0,2},{1,3},{2,4},{3,5},{4,6},{5,7},{6,0},{7,1},{8,10},{9,11},{10,... | collective-permute-start | bytes 614408 | tf_op jit(solution)/shard_map/ppermute | solution.py:372
  22.3 7.4 %collective-permute-start.2 = (s16[1,400,256]{2,1,0:T(8,128)(2,1)S(1)}, s16[1,400,256]{2,1,0:T(8,128)(2,1)S(1)}, u32[]{:S(2)}, u32[]{:S(2)}) collective-permute-start(s16[1,400,256]{2,1,0:T(8,128)(2,1)S(1)} %copy-done.2), channel_id=1, source_target_pairs={{0,6},{1,7},{2,0},{3,1},{4,2},{5,3},{6,4},{7,5},{8,14},{9,15},{10,... | collective-permute-start | bytes 614408 | tf_op jit(solution)/shard_map/ppermute | solution.py:372
  29.7 51.6 %collective-permute-start.8 = (bf16[32,32768]{1,0:T(8,128)(2,1)S(1)}, bf16[32,32768]{1,0:T(8,128)(2,1)S(1)}, u32[]{:S(2)}, u32[]{:S(2)}) collective-permute-start(bf16[32,32768]{1,0:T(8,128)(2,1)S(1)} %pack_keys.1.keys_ref), channel_id=1, source_target_pairs={{8,0},{16,8},{24,16},{32,24},{40,32},{48,40},{56,48},{64,56},{72,6... | collective-permute-start | bytes 6291464 | tf_op jit(solution)/shard_map/ppermute | solution.py:400
  84.4 20.8 %copy-start.8 = (f32[8,32768]{1,0:T(8,128)}, f32[8,32768]{1,0:T(8,128)S(1)}, u32[]{:S(2)}) copy-start(f32[8,32768]{1,0:T(8,128)S(1)} %get-tuple-element.43.sum_ref) | copy-start | bytes 3145732

commit v5 on v4

--- a/solution.py
+++ b/solution.py
@@ -69,7 +69,7 @@
     return product(parts(product(h_a, parts(block))), h_b)
 
 
-def send_coded(blocks, out_ref, copies):
+def send_coded(blocks, out_ref):
     top = jnp.max(jnp.abs(blocks[0]))
     for block in blocks[1:]:
         top = jnp.maximum(top, jnp.max(jnp.abs(block)))
@@ -78,18 +78,15 @@
     for at, block in enumerate(blocks):
         root = jnp.sqrt(jnp.sqrt(jnp.abs(block) * gain)) * CODES
         code = jnp.round(jnp.where(block < 0, -root, root)).astype(jnp.int32).astype(jnp.int16)
-        for to in range(copies):
-            out_ref[to, at * A : (at + 1) * A, :] = code
-    scale = exponent.astype(jnp.int32).astype(jnp.int16)
-    for to in range(copies):
-        out_ref[to, len(blocks) * A :, :] = scale
-
-
-def received(ref, source, at):
-    rows = ref.shape[1]
-    tail = ref[source, rows - TAIL : rows, :].astype(jnp.int32).astype(jnp.float32)[:1]
+        out_ref[at * A : (at + 1) * A, :] = code
+    out_ref[len(blocks) * A :, :] = exponent.astype(jnp.int32).astype(jnp.int16)
+
+
+def received(ref, at):
+    rows = ref.shape[0]
+    tail = ref[rows - TAIL : rows, :].astype(jnp.int32).astype(jnp.float32)[:1]
     gain = jnp.exp(tail * (LN2 / FINE))
-    root = ref[source, at * A : (at + 1) * A, :].astype(jnp.int32).astype(jnp.float32) * (1.0 / CODES)
+    root = ref[at * A : (at + 1) * A, :].astype(jnp.int32).astype(jnp.float32) * (1.0 / CODES)
     return (root * jnp.abs(root)) * (root * root) * gain
 
 
@@ -112,7 +109,7 @@
     for limb in range(JS - 1):
         tw = twiddle(exp_ref[lead_ref[0] * (JS - 1) + limb])
         done.append(both_sides(h_a, x_ref[limb], h_b) / tw)
-    send_coded(done, out_ref, 1)
+    send_coded(done, out_ref)
 
 
 def pack_kernel(km_ref, ks_ref, dm_ref, ds_ref, out_ref, rows_ref):
@@ -171,7 +168,7 @@
     for step, held_ref in zip(STEPS, held):
         source = partner(lead, step, -1)
         for limb in range(JS - 1):
-            coef_ref[source * (JS - 1) + limb] = received(held_ref, 0, limb)
+            coef_ref[source * (JS - 1) + limb] = received(held_ref, limb)
 
     def lift(step, _):
         rows = pl.ds(pl.multiple_of(step * CHUNK, CHUNK), CHUNK)
@@ -215,16 +212,16 @@
         turns_ref[:, by * 128 : (by + 1) * 128] = ones.astype(jnp.bfloat16)
 
     def turn(step, _):
-        for k in range(4):
-            at = pl.ds(pl.multiple_of(step * 256 + k // 2 * 128, 128), 128)
+        for k in range(8):
+            at = pl.ds(pl.multiple_of(step * 512 + k // 2 * 128, 128), 128)
             both = jnp.concatenate(parts(rows_ref[k % 2, at, :].T), axis=1)
             turned = jnp.dot(both, turns_ref[...], preferred_element_type=jnp.float32)
             for by in range(8):
-                at = pl.ds(pl.multiple_of(by * (NRING // 8) + step * (2 * B) + k * 128, 128), 128)
+                at = pl.ds(pl.multiple_of(by * (NRING // 8) + step * (4 * B) + k * 128, 128), 128)
                 ext_ref[at, :] = turned[:, by * 128 : (by + 1) * 128]
         return 0
 
-    lax.fori_loop(0, A // 16, turn, 0)
+    lax.fori_loop(0, A // 32, turn, 0)
 
 
     group = lax.broadcasted_iota(jnp.int32, (1, 128), 1) // 16
@@ -293,15 +290,17 @@
     def _():
         tw = twiddle(exp_ref[LIMBS * (JS - 1) + lead_ref[0]])
         h_a, h_b = parts(ha_ref[...]), parts(hb_ref[...])
-        send_coded([both_sides(h_a, spec_ref[p], h_b) / tw for p in range(2)], low_ref, LIMBS)
-
-
-def finish_kernel(lead_ref, exp_ref, down_ref, sum_ref, ha_ref, hb_ref, held_ref, out_ref, low_ref, returned_ref, rows_ref):
+        send_coded([both_sides(h_a, spec_ref[p], h_b) / tw for p in range(2)], low_ref)
+
+
+def finish_kernel(lead_ref, exp_ref, down_ref, sum_ref, ha_ref, hb_ref, *rest):
+    held, (out_ref, low_ref, returned_ref, rows_ref) = rest[:LIMBS], rest[LIMBS:]
     lead = lead_ref[0]
     h_a, h_b = parts(ha_ref[...]), parts(hb_ref[...])
-    for source in range(LIMBS):
-        for p in range(2):
-            low_ref[source * 2 + p] = received(held_ref, source, p)
+    for step, held_ref in zip(STEPS, held):
+        source = partner(lead, step, -1)
+        for p in range(2):
+            low_ref[source * 2 + p] = received(held_ref, p)
 
     def lower(step, _):
         rows = pl.ds(pl.multiple_of(step * CHUNK, CHUNK), CHUNK)
@@ -335,8 +334,11 @@
     lax.fori_loop(0, A // 4, body, 0)
 
 
-def exchange(value):
-    return lax.all_to_all(value, "limb", split_axis=0, concat_axis=0, tiled=True)
+def spread_limbs(value):
+    return [value] + [
+        lax.ppermute(value, "limb", [(source, partner(source, step, 1)) for source in range(LIMBS)])
+        for step in STEPS[1:]
+    ]
 
 
 def rows_of(perms):
@@ -360,7 +362,7 @@
 
     coefs = pl.pallas_call(
         inverse_kernel,
-        out_shape=jax.ShapeDtypeStruct((1, (JS - 1) * A + TAIL, B), jnp.int16),
+        out_shape=jax.ShapeDtypeStruct(((JS - 1) * A + TAIL, B), jnp.int16),
         in_specs=[SMEM, SMEM, VMEM, VMEM, VMEM],
         out_specs=VMEM,
         scratch_shapes=[pltpu.VMEM((JS - 1, A, B), jnp.float32)],
@@ -368,10 +370,7 @@
         cost_estimate=cost(2),
         name="coefficients",
     )(lead, tw_exp, cipher, h_a, h_b)
-    held = [coefs] + [
-        lax.ppermute(coefs, "limb", [(source, partner(source, step, 1)) for source in range(LIMBS)])
-        for step in STEPS[1:]
-    ]
+    held = spread_limbs(coefs)
 
     count = lax.axis_size("key")
     ahead = [((target + 1) % count, target) for target in range(count)]
@@ -422,7 +421,7 @@
 
     lines = (BLOCKS, 128, 128)
     columns = pl.BlockSpec((2 * JS, BLOCKS * LINE), lambda step: (0, step))
-    low_shape = (LIMBS, 2 * A + TAIL, B)
+    low_shape = (2 * A + TAIL, B)
     summed, lowered = pl.pallas_call(
         combine_kernel,
         grid=(half_lines // BLOCKS,),
@@ -435,18 +434,18 @@
             pl.BlockSpec((32, BLOCKS * LINE), lambda step: (0, step)),
             columns,
         ],
-        out_specs=(columns, pl.BlockSpec(low_shape, lambda step: (0, 0, 0))),
+        out_specs=(columns, pl.BlockSpec(low_shape, lambda step: (0, 0))),
         scratch_shapes=[pltpu.VMEM((2, A, B), jnp.float32)],
         compiler_params=params(32),
         cost_estimate=cost(4),
         name="switch_next",
     )(lead, tw_exp, gathered, h_a, h_b, packed_next, first)
-    special = exchange(lowered)
+    special = spread_limbs(lowered)
 
     result = pl.pallas_call(
         finish_kernel,
         out_shape=f32(1, JS - 1, 2, NRING),
-        in_specs=[SMEM] * 3 + [VMEM] * 4,
+        in_specs=[SMEM] * 3 + [VMEM] * (3 + LIMBS),
         out_specs=VMEM,
         scratch_shapes=[
             pltpu.VMEM((LIMBS * 2, A, B), jnp.float32),
@@ -456,7 +455,7 @@
         compiler_params=params(60),
         cost_estimate=cost(4),
         name="finish",
-    )(lead, tw_exp, down_conv, summed, h_a, h_b, special)
+    )(lead, tw_exp, down_conv, summed, h_a, h_b, *special)
     return result.transpose(0, 2, 1, 3)
 
 

time: 111 us -> 110 us (level)
  blocking collectives: 20.8 us -> 0 us
  starting transfers between devices: 22.1 us -> 34.7 us
  waiting for transfers between devices: 5.51 us -> 11.6 us
  local copies, waits for them, and re-layouts: 1.71 us -> 3.28 us
    all_to_all x1 -> x0, blocking collectives: 20.8 us -> none  [exchange(): lax.all_to_all(value, 'limb', split_axis=0, concat_axis=0, tiled=True)]
    ppermute x7 -> x14, starting transfers between devices: 15.6 us -> 28.2 us  [spread_limbs(): lax.ppermute(value, 'limb', [(source, partner(source, step, 1)) for sourc...]
    ppermute x7 -> x14, waiting for transfers between devices: 5.51 us -> 11.6 us  [spread_limbs(): lax.ppermute(value, 'limb', [(source, partner(source, step, 1)) for sourc...]
    unnamed x25 -> x41, local copies, waits for them, and re-layouts: 0.08 us -> 1.65 us
  transfers between devices with their start and end apart: 9 -> 16, of which waited for: 5 -> 10; matrix products, arithmetic and copies ran while one was open for 2% -> 2% of each run, Pallas kernels for 44% -> 43%
where the time goes in v5:
time: 110 us; the launch traced here: 109 us
  Pallas kernels  59.4 us (54%)
  starting transfers between devices  34.7 us (32%)
  waiting for transfers between devices  11.6 us (11%)
  local copies, waits for them, and re-layouts  3.28 us (3%)
    pallas_call x1, Pallas kernels, on_device(): pl.pallas_call(extend_kernel, out_shape=(f32(2 * JS, NRING), f32(half_lin...  46.2 us
    ppermute x14, starting transfers between devices, spread_limbs(): lax.ppermute(value, 'limb', [(source, partner(source, step, 1)) for sourc...  28.2 us
    ppermute x14, waiting for transfers between devices, spread_limbs(): lax.ppermute(value, 'limb', [(source, partner(source, step, 1)) for sourc...  11.6 us
    pallas_call x1, Pallas kernels, on_device(): pl.pallas_call(finish_kernel, out_shape=f32(1, JS - 1, 2, NRING), in_spec...  5.54 us
    ppermute x1, starting transfers between devices, on_device(): packed_next = lax.ppermute(packed, 'key', ahead)  4.47 us
    pallas_call x1, Pallas kernels, on_device(): pl.pallas_call(inverse_kernel, out_shape=jax.ShapeDtypeStruct(((JS - 1) *...  3.34 us
    pallas_call x1, Pallas kernels, on_device(): pl.pallas_call(combine_kernel, grid=(half_lines // BLOCKS,), out_shape=(f...  3.02 us
  transfers between devices with their start and end apart: 16, of which 10 were waited for; matrix products, arithmetic and copies ran while one was open for 2% of the time, Pallas kernels for 43%

profile of v5, /device:TPU:0, one launch (start us, length us, event | category | flops | bytes accessed | tf_op | source)
XLA Modules:
  0.0 109.4 jit_solution(9481098360509489242)
XLA Ops:
  0.0 3.3 %coefficients.1.rest_0_ = s16[400,256]{1,0:T(8,128)(2,1)} custom-call(s32[1]{0:T(128)} %bitcast.lead_ref, s32[32]{0:T(128)} %exp_ref.7, f32[1,3,2,32768]{3,2,1,0:T(2,128)} %bitcast.4, f32[128,128]{1,0:T(8,128)} %constant.18.clone.ha_ref, f32[256,256]{1,0:T(8,128)} %constant.19.clone.hb_ref), custom_call_target="tpu_custom_call" | custom-call | flops 2000000000 | bytes 1048576 | tf_op jit(solution)/shard_map/coefficients/pallas_call | solution.py:363
  3.4 6.6 %collective-permute-start = (s16[400,256]{1,0:T(8,128)(2,1)}, s16[400,256]{1,0:T(8,128)(2,1)S(1)}, u32[]{:S(2)}, u32[]{:S(2)}) collective-permute-start(s16[400,256]{1,0:T(8,128)(2,1)} %coefficients.1.rest_0_), channel_id=1, source_target_pairs={{0,5},{1,4},{2,7},{3,6},{4,1},{5,0},{6,3},{7,2},{8,13},{9,12},{10,... | collective-permute-start | bytes 614408 | tf_op jit(solution)/shard_map/ppermute | solution.py:339
  9.9 0.8 collective-permute-start.7
  10.7 4.8 %collective-permute-start.6 = (s16[400,256]{1,0:T(8,128)(2,1)}, s16[400,256]{1,0:T(8,128)(2,1)S(1)}, u32[]{:S(2)}, u32[]{:S(2)}) collective-permute-start(s16[400,256]{1,0:T(8,128)(2,1)} %coefficients.1.rest_0_), channel_id=1, source_target_pairs={{0,7},{1,6},{2,1},{3,0},{4,3},{5,2},{6,5},{7,4},{8,15},{9,14},{10,... | collective-permute-start | bytes 614408 | tf_op jit(solution)/shard_map/ppermute | solution.py:339
  15.6 0.0 collective-permute-start.5
  15.6 0.4 collective-permute-start.4
  16.0 0.0 collective-permute-done.rest_7_
  16.0 0.0 copy-done.12
  16.0 2.1 %collective-permute-start.1 = (s32[32768]{0:T(1024)S(1)}, s32[32768]{0:T(1024)S(1)}, u32[]{:S(2)}, u32[]{:S(2)}) collective-permute-start(s32[32768]{0:T(1024)S(1)} %bitcast.6), channel_id=1, source_target_pairs={{8,0},{16,8},{24,16},{32,24},{40,32},{48,40},{56,48},{64,56},{72,6... | collective-permute-start | bytes 393224 | tf_op jit(solution)/shard_map/ppermute | solution.py:397
  18.1 0.0 copy-done.11
  18.1 0.6 copy.13.ks_ref
  18.7 0.0 copy-done.10
  18.7 1.0 copy.12.km_ref
  19.8 0.0 copy-done.1
  19.8 0.0 copy-done.4
  19.8 0.0 copy-start.2
  19.8 0.0 copy-start
  19.8 0.0 copy-start.5
  19.8 0.0 copy-start.6
  19.8 0.0 copy-start.7
  19.8 0.0 copy-start.8
  19.9 1.3 %pack_keys.1.keys_ref = bf16[32,32768]{1,0:T(8,128)(2,1)S(1)} custom-call(bf16[1,2,3,3,32768]{4,3,2,1,0:T(4,128)(2,1)S(1)} %copy.12.km_ref, bf16[1,2,3,1,32768]{4,3,2,1,0:T(2,128)(2,1)S(1)} %copy.13.ks_ref, bf16[1,3,32768]{2,1,0:T(4,128)(2,1)S(1)} %copy-done.1, bf16[1,1,32768]{2,1,0:T(2,128)(2,1)S(1)} %copy-done.4), custom_call_target="tpu_custom_call" | custom-call | flops 2000000000 | bytes 1048576 | tf_op jit(solution)/shard_map/pack_keys/pallas_call | solution.py:381
  21.2 0.0 collective-permute-done.1
  21.2 0.0 copy-done.2
  21.2 0.6 collective-permute-start.3
  21.8 0.5 collective-permute-done.7.rest_6_
  22.3 2.3 %collective-permute-start.2 = (s16[400,256]{1,0:T(8,128)(2,1)S(1)}, s16[400,256]{1,0:T(8,128)(2,1)S(1)}, u32[]{:S(2)}, u32[]{:S(2)}) collective-permute-start(s16[400,256]{1,0:T(8,128)(2,1)S(1)} %copy-done.2), channel_id=1, source_target_pairs={{0,6},{1,7},{2,0},{3,1},{4,2},{5,3},{6,4},{7,5},{8,14},{9,15},{10,... | collective-permute-start | bytes 614408 | tf_op jit(solution)/shard_map/ppermute | solution.py:339
  24.6 0.1 and_add_fusion.idx_ref
  24.7 1.1 %collective-permute-done.6.rest_5_ = s16[400,256]{1,0:T(8,128)(2,1)S(1)} collective-permute-done((s16[400,256]{1,0:T(8,128)(2,1)}, s16[400,256]{1,0:T(8,128)(2,1)S(1)}, u32[]{:S(2)}, u32[]{:S(2)}) %collective-permute-start.6) | collective-permute-done | bytes 204832 | tf_op jit(solution)/shard_map/ppermute | solution.py:339
  25.8 0.0 collective-permute-done.5.rest_4_
  25.9 2.9 %collective-permute-done.4.rest_3_ = s16[400,256]{1,0:T(8,128)(2,1)S(1)} collective-permute-done((s16[400,256]{1,0:T(8,128)(2,1)}, s16[400,256]{1,0:T(8,128)(2,1)S(1)}, u32[]{:S(2)}, u32[]{:S(2)}) %collective-permute-start.4) | collective-permute-done | bytes 204832 | tf_op jit(solution)/shard_map/ppermute | solution.py:339
  28.8 0.6 collective-permute-done.3.rest_2_
  29.4 0.4 collective-permute-done.2.rest_1_
  29.7 4.5 %collective-permute-start.8 = (bf16[32,32768]{1,0:T(8,128)(2,1)S(1)}, bf16[32,32768]{1,0:T(8,128)(2,1)S(1)}, u32[]{:S(2)}, u32[]{:S(2)}) collective-permute-start(bf16[32,32768]{1,0:T(8,128)(2,1)S(1)} %pack_keys.1.keys_ref), channel_id=1, source_target_pairs={{8,0},{16,8},{24,16},{32,24},{40,32},{48,40},{56,48},{64,56},{72,6... | collective-permute-start | bytes 6291464 | tf_op jit(solution)/shard_map/ppermute | solution.py:399
  34.2 0.0 copy-done
  34.2 0.0 copy-done.5
  34.2 0.0 copy-done.6
  34.2 0.0 copy-done.7
  34.2 0.0 copy-done.8
  34.2 46.2 %extend_and_gather.1 = (f32[8,32768]{1,0:T(8,128)S(1)}, f32[32,128,128]{2,1,0:T(8,128)S(1)}) custom-call(s32[1]{0:T(128)} %bitcast.lead_ref, s32[32]{0:T(128)S(1)} %copy-done.6, f32[24,32]{1,0:T(8,128)S(1)} %copy-done.5, s32[65536]{0:T(1024)S(1)} %and_add_fusion.idx_ref, f32[1,3,2,32768]{3,2,1,0:T(2,128)S(1)} %bitcast.5, f32[128,128]{1,0:T(8,128)S(1)} %copy-done.8, ...), custom_call_target="tpu_custom_call" | custom-call | flops 49999998976 | bytes 1048576 | tf_op jit(solution)/shard_map/extend_and_gather/pallas_call | solution.py:402
  80.4 0.0 collective-permute-done.8.keys_ref
  80.4 3.0 %switch_next.1 = (f32[8,32768]{1,0:T(8,128)S(1)}, s16[272,256]{1,0:T(8,128)(2,1)S(1)}) custom-call(s32[1]{0:T(128)} %bitcast.lead_ref, s32[32]{0:T(128)S(1)} %copy-done.6, f32[32,128,128]{2,1,0:T(8,128)S(1)} %get-tuple-element.41.got_ref, f32[128,128]{1,0:T(8,128)S(1)} %copy-done.8, f32[256,256]{1,0:T(8,128)S(1)} %copy-done.7, ...), custom_call_target="tpu_custom_call" | custom-call | flops 4000000000 | bytes 1048576 | tf_op jit(solution)/shard_map/switch_next/pallas_call | solution.py:425
  83.5 1.0 copy-done.9
  84.4 3.5 %collective-permute-start.15 = (s16[272,256]{1,0:T(8,128)(2,1)S(1)}, s16[272,256]{1,0:T(8,128)(2,1)S(1)}, u32[]{:S(2)}, u32[]{:S(2)}) collective-permute-start(s16[272,256]{1,0:T(8,128)(2,1)S(1)} %get-tuple-element.44.rest_0_), channel_id=1, source_target_pairs={{0,5},{1,4},{2,7},{3,6},{4,1},{5,0},{6,3},{7,2},{8,13},{9,12},{10,... | collective-permute-start | bytes 417800 | tf_op jit(solution)/shard_map/ppermute | solution.py:339
  87.9 1.6 %collective-permute-start.14 = (s16[272,256]{1,0:T(8,128)(2,1)S(1)}, s16[272,256]{1,0:T(8,128)(2,1)S(1)}, u32[]{:S(2)}, u32[]{:S(2)}) collective-permute-start(s16[272,256]{1,0:T(8,128)(2,1)S(1)} %get-tuple-element.44.rest_0_), channel_id=1, source_target_pairs={{0,3},{1,2},{2,5},{3,4},{4,7},{5,6},{6,1},{7,0},{8,11},{9,10},{10,... | collective-permute-start | bytes 417800 | tf_op jit(solution)/shard_map/ppermute | solution.py:339
  89.5 4.0 %collective-permute-start.13 = (s16[272,256]{1,0:T(8,128)(2,1)S(1)}, s16[272,256]{1,0:T(8,128)(2,1)S(1)}, u32[]{:S(2)}, u32[]{:S(2)}) collective-permute-start(s16[272,256]{1,0:T(8,128)(2,1)S(1)} %get-tuple-element.44.rest_0_), channel_id=1, source_target_pairs={{0,7},{1,6},{2,1},{3,0},{4,3},{5,2},{6,5},{7,4},{8,15},{9,14},{10,... | collective-permute-start | bytes 417800 | tf_op jit(solution)/shard_map/ppermute | solution.py:339
  93.6 1.0 collective-permute-start.12
  94.6 0.8 collective-permute-start.11
  95.4 0.0 collective-permute-done.15.rest_7_
  95.4 1.2 %collective-permute-start.10 = (s16[272,256]{1,0:T(8,128)(2,1)S(1)}, s16[272,256]{1,0:T(8,128)(2,1)S(1)}, u32[]{:S(2)}, u32[]{:S(2)}) collective-permute-start(s16[272,256]{1,0:T(8,128)(2,1)S(1)} %get-tuple-element.44.rest_0_), channel_id=1, source_target_pairs={{0,2},{1,3},{2,4},{3,5},{4,6},{5,7},{6,0},{7,1},{8,10},{9,11},{10,... | collective-permute-start | bytes 417800 | tf_op jit(solution)/shard_map/ppermute | solution.py:339
  96.6 1.6 %collective-permute-done.14.rest_6_ = s16[272,256]{1,0:T(8,128)(2,1)S(1)} collective-permute-done((s16[272,256]{1,0:T(8,128)(2,1)S(1)}, s16[272,256]{1,0:T(8,128)(2,1)S(1)}, u32[]{:S(2)}, u32[]{:S(2)}) %collective-permute-start.14) | collective-permute-done | bytes 139296 | tf_op jit(solution)/shard_map/ppermute | solution.py:339
  98.1 0.5 collective-permute-start.9
  98.6 0.0 collective-permute-done.13.rest_5_
  98.7 2.1 %collective-permute-done.12.rest_4_ = s16[272,256]{1,0:T(8,128)(2,1)S(1)} collective-permute-done((s16[272,256]{1,0:T(8,128)(2,1)S(1)}, s16[272,256]{1,0:T(8,128)(2,1)S(1)}, u32[]{:S(2)}, u32[]{:S(2)}) %collective-permute-start.12) | collective-permute-done | bytes 139296 | tf_op jit(solution)/shard_map/ppermute | solution.py:339
  100.7 0.4 collective-permute-done.11.rest_3_
  101.1 1.1 collective-permute-done.10.rest_2_
  102.2 1.0 collective-permute-done.9.rest_1_
  103.2 0.0 copy-done.13
  103.2 0.0 copy-done.15
  103.2 0.0 copy-done.16
  103.2 0.0 copy-done.17
  103.2 0.0 copy-done.18
  103.3 0.6 copy-done.19
  103.9 5.5 %finish.1 = f32[1,3,2,32768]{3,2,1,0:T(2,128)} custom-call(s32[1]{0:T(128)} %bitcast.lead_ref, s32[32]{0:T(128)} %exp_ref.7, f32[8,24]{1,0:T(8,128)} %down_ref.1, f32[8,32768]{1,0:T(8,128)} %copy-done.9, f32[128,128]{1,0:T(8,128)} %constant.18.clone.ha_ref, f32[256,256]{1,0:T(8,128)} %constant.19.clone.hb_ref, s16[272,256]{1,0:T(8,128)(2,1)} %copy-done.3, ...), custom_call_target="tpu_custom_call" | custom-call | flops 4000000000 | bytes 1048576 | tf_op jit(solution)/shard_map/finish/pallas_call | solution.py:445
  (18 shorter events, 0.0 us)
Async XLA Ops:
  0.0 16.0 %copy-start.12 = (s32[1,32768]{1,0:T(1,128)S(1)}, s32[1,32768]{1,0:T(1,128)}, u32[]{:S(2)}) copy-start(s32[1,32768]{1,0:T(1,128)} %param.16) | copy-start | bytes 393220
  0.0 18.1 %copy-start.11 = (bf16[1,2,3,1,32768]{4,1,3,2,0:T(2,128)(2,1)S(1)}, bf16[1,2,3,1,32768]{4,1,3,2,0:T(2,128)(2,1)}, u32[]{:S(2)}) copy-start(bf16[1,2,3,1,32768]{4,1,3,2,0:T(2,128)(2,1)} %param.13) | copy-start | bytes 1179652
  3.3 15.4 %copy-start.10 = (bf16[1,2,3,3,32768]{4,1,3,2,0:T(2,128)(2,1)S(1)}, bf16[1,2,3,3,32768]{4,1,3,2,0:T(2,128)(2,1)}, u32[]{:S(2)}) copy-start(bf16[1,2,3,3,32768]{4,1,3,2,0:T(2,128)(2,1)} %param.12) | copy-start | bytes 3538948
  3.4 12.7 %collective-permute-start = (s16[400,256]{1,0:T(8,128)(2,1)}, s16[400,256]{1,0:T(8,128)(2,1)S(1)}, u32[]{:S(2)}, u32[]{:S(2)}) collective-permute-start(s16[400,256]{1,0:T(8,128)(2,1)} %coefficients.1.rest_0_), channel_id=1, source_target_pairs={{0,5},{1,4},{2,7},{3,6},{4,1},{5,0},{6,3},{7,2},{8,13},{9,12},{10,... | collective-permute-start | bytes 614408 | tf_op jit(solution)/shard_map/ppermute | solution.py:339
  9.9 12.4 %collective-permute-start.7 = (s16[400,256]{1,0:T(8,128)(2,1)}, s16[400,256]{1,0:T(8,128)(2,1)S(1)}, u32[]{:S(2)}, u32[]{:S(2)}) collective-permute-start(s16[400,256]{1,0:T(8,128)(2,1)} %coefficients.1.rest_0_), channel_id=1, source_target_pairs={{0,3},{1,2},{2,5},{3,4},{4,7},{5,6},{6,1},{7,0},{8,11},{9,10},{10,... | collective-permute-start | bytes 614408 | tf_op jit(solution)/shard_map/ppermute | solution.py:339
  10.7 15.1 %collective-permute-start.6 = (s16[400,256]{1,0:T(8,128)(2,1)}, s16[400,256]{1,0:T(8,128)(2,1)S(1)}, u32[]{:S(2)}, u32[]{:S(2)}) collective-permute-start(s16[400,256]{1,0:T(8,128)(2,1)} %coefficients.1.rest_0_), channel_id=1, source_target_pairs={{0,7},{1,6},{2,1},{3,0},{4,3},{5,2},{6,5},{7,4},{8,15},{9,14},{10,... | collective-permute-start | bytes 614408 | tf_op jit(solution)/shard_map/ppermute | solution.py:339
  15.6 10.3 %collective-permute-start.5 = (s16[400,256]{1,0:T(8,128)(2,1)}, s16[400,256]{1,0:T(8,128)(2,1)S(1)}, u32[]{:S(2)}, u32[]{:S(2)}) collective-permute-start(s16[400,256]{1,0:T(8,128)(2,1)} %coefficients.1.rest_0_), channel_id=1, source_target_pairs={{0,4},{1,5},{2,6},{3,7},{4,0},{5,1},{6,2},{7,3},{8,12},{9,13},{10,... | collective-permute-start | bytes 614408 | tf_op jit(solution)/shard_map/ppermute | solution.py:339
  15.6 13.2 %collective-permute-start.4 = (s16[400,256]{1,0:T(8,128)(2,1)}, s16[400,256]{1,0:T(8,128)(2,1)S(1)}, u32[]{:S(2)}, u32[]{:S(2)}) collective-permute-start(s16[400,256]{1,0:T(8,128)(2,1)} %coefficients.1.rest_0_), channel_id=1, source_target_pairs={{0,1},{1,0},{2,3},{3,2},{4,5},{5,4},{6,7},{7,6},{8,9},{9,8},{10,11... | collective-permute-start | bytes 614408 | tf_op jit(solution)/shard_map/ppermute | solution.py:339
  16.0 3.8 %copy-start.1 = (bf16[1,3,32768]{2,1,0:T(4,128)(2,1)S(1)}, bf16[1,3,32768]{2,1,0:T(4,128)(2,1)}, u32[]{:S(2)}) copy-start(bf16[1,3,32768]{2,1,0:T(4,128)(2,1)} %dm_ref) | copy-start | bytes 589828
  16.0 3.8 %copy-start.4 = (bf16[1,1,32768]{2,1,0:T(2,128)(2,1)S(1)}, bf16[1,1,32768]{2,1,0:T(2,128)(2,1)}, u32[]{:S(2)}) copy-start(bf16[1,1,32768]{2,1,0:T(2,128)(2,1)} %ds_ref) | copy-start | bytes 196612
  16.0 5.2 %collective-permute-start.1 = (s32[32768]{0:T(1024)S(1)}, s32[32768]{0:T(1024)S(1)}, u32[]{:S(2)}, u32[]{:S(2)}) collective-permute-start(s32[32768]{0:T(1024)S(1)} %bitcast.6), channel_id=1, source_target_pairs={{8,0},{16,8},{24,16},{32,24},{40,32},{48,40},{56,48},{64,56},{72,6... | collective-permute-start | bytes 393224 | tf_op jit(solution)/shard_map/ppermute | solution.py:397
  19.8 1.4 %copy-start.2 = (s16[400,256]{1,0:T(8,128)(2,1)S(1)}, s16[400,256]{1,0:T(8,128)(2,1)}, u32[]{:S(2)}) copy-start(s16[400,256]{1,0:T(8,128)(2,1)} %coefficients.1.rest_0_) | copy-start | bytes 614404
  19.8 14.4 %copy-start = (f32[1,2,3,32768]{3,1,2,0:T(2,128)S(1)}, f32[1,2,3,32768]{3,1,2,0:T(2,128)}, u32[]{:S(2)}) copy-start(f32[1,2,3,32768]{3,1,2,0:T(2,128)} %param.11) | copy-start | bytes 2359300
  19.8 14.4 %copy-start.5 = (f32[24,32]{1,0:T(8,128)S(1)}, f32[24,32]{1,0:T(8,128)}, u32[]{:S(2)}) copy-start(f32[24,32]{1,0:T(8,128)} %up_ref.1) | copy-start | bytes 9220
  19.8 14.4 %copy-start.6 = (s32[32]{0:T(128)S(1)}, s32[32]{0:T(128)}, u32[]{:S(2)}) copy-start(s32[32]{0:T(128)} %exp_ref.7) | copy-start | bytes 388
  19.8 14.4 %copy-start.7 = (f32[256,256]{1,0:T(8,128)S(1)}, f32[256,256]{1,0:T(8,128)}, u32[]{:S(2)}) copy-start(f32[256,256]{1,0:T(8,128)} %constant.19.clone.hb_ref) | copy-start | bytes 786436
  19.8 14.4 %copy-start.8 = (f32[128,128]{1,0:T(8,128)S(1)}, f32[128,128]{1,0:T(8,128)}, u32[]{:S(2)}) copy-start(f32[128,128]{1,0:T(8,128)} %constant.18.clone.ha_ref) | copy-start | bytes 196612
  21.2 8.1 %collective-permute-start.3 = (s16[400,256]{1,0:T(8,128)(2,1)S(1)}, s16[400,256]{1,0:T(8,128)(2,1)S(1)}, u32[]{:S(2)}, u32[]{:S(2)}) collective-permute-start(s16[400,256]{1,0:T(8,128)(2,1)S(1)} %copy-done.2), channel_id=1, source_target_pairs={{0,2},{1,3},{2,4},{3,5},{4,6},{5,7},{6,0},{7,1},{8,10},{9,11},{10,... | collective-permute-start | bytes 614408 | tf_op jit(solution)/shard_map/ppermute | solution.py:339
  22.3 7.4 %collective-permute-start.2 = (s16[400,256]{1,0:T(8,128)(2,1)S(1)}, s16[400,256]{1,0:T(8,128)(2,1)S(1)}, u32[]{:S(2)}, u32[]{:S(2)}) collective-permute-start(s16[400,256]{1,0:T(8,128)(2,1)S(1)} %copy-done.2), channel_id=1, source_target_pairs={{0,6},{1,7},{2,0},{3,1},{4,2},{5,3},{6,4},{7,5},{8,14},{9,15},{10,... | collective-permute-start | bytes 614408 | tf_op jit(solution)/shard_map/ppermute | solution.py:339
  29.7 50.7 %collective-permute-start.8 = (bf16[32,32768]{1,0:T(8,128)(2,1)S(1)}, bf16[32,32768]{1,0:T(8,128)(2,1)S(1)}, u32[]{:S(2)}, u32[]{:S(2)}) collective-permute-start(bf16[32,32768]{1,0:T(8,128)(2,1)S(1)} %pack_keys.1.keys_ref), channel_id=1, source_target_pairs={{8,0},{16,8},{24,16},{32,24},{40,32},{48,40},{56,48},{64,56},{72,6... | collective-permute-start | bytes 6291464 | tf_op jit(solution)/shard_map/ppermute | solution.py:399
  83.5 1.0 copy-start.9
  84.4 18.8 %copy-start.3 = (s16[272,256]{1,0:T(8,128)(2,1)}, s16[272,256]{1,0:T(8,128)(2,1)S(1)}, u32[]{:S(2)}) copy-start(s16[272,256]{1,0:T(8,128)(2,1)S(1)} %get-tuple-element.44.rest_0_) | copy-start | bytes 417796
  84.4 10.9 %collective-permute-start.15 = (s16[272,256]{1,0:T(8,128)(2,1)S(1)}, s16[272,256]{1,0:T(8,128)(2,1)S(1)}, u32[]{:S(2)}, u32[]{:S(2)}) collective-permute-start(s16[272,256]{1,0:T(8,128)(2,1)S(1)} %get-tuple-element.44.rest_0_), channel_id=1, source_target_pairs={{0,5},{1,4},{2,7},{3,6},{4,1},{5,0},{6,3},{7,2},{8,13},{9,12},{10,... | collective-permute-start | bytes 417800 | tf_op jit(solution)/shard_map/ppermute | solution.py:339
  87.9 10.2 %collective-permute-start.14 = (s16[272,256]{1,0:T(8,128)(2,1)S(1)}, s16[272,256]{1,0:T(8,128)(2,1)S(1)}, u32[]{:S(2)}, u32[]{:S(2)}) collective-permute-start(s16[272,256]{1,0:T(8,128)(2,1)S(1)} %get-tuple-element.44.rest_0_), channel_id=1, source_target_pairs={{0,3},{1,2},{2,5},{3,4},{4,7},{5,6},{6,1},{7,0},{8,11},{9,10},{10,... | collective-permute-start | bytes 417800 | tf_op jit(solution)/shard_map/ppermute | solution.py:339
  89.5 9.1 %collective-permute-start.13 = (s16[272,256]{1,0:T(8,128)(2,1)S(1)}, s16[272,256]{1,0:T(8,128)(2,1)S(1)}, u32[]{:S(2)}, u32[]{:S(2)}) collective-permute-start(s16[272,256]{1,0:T(8,128)(2,1)S(1)} %get-tuple-element.44.rest_0_), channel_id=1, source_target_pairs={{0,7},{1,6},{2,1},{3,0},{4,3},{5,2},{6,5},{7,4},{8,15},{9,14},{10,... | collective-permute-start | bytes 417800 | tf_op jit(solution)/shard_map/ppermute | solution.py:339
  93.6 7.2 %collective-permute-start.12 = (s16[272,256]{1,0:T(8,128)(2,1)S(1)}, s16[272,256]{1,0:T(8,128)(2,1)S(1)}, u32[]{:S(2)}, u32[]{:S(2)}) collective-permute-start(s16[272,256]{1,0:T(8,128)(2,1)S(1)} %get-tuple-element.44.rest_0_), channel_id=1, source_target_pairs={{0,4},{1,5},{2,6},{3,7},{4,0},{5,1},{6,2},{7,3},{8,12},{9,13},{10,... | collective-permute-start | bytes 417800 | tf_op jit(solution)/shard_map/ppermute | solution.py:339
  94.6 6.6 %collective-permute-start.11 = (s16[272,256]{1,0:T(8,128)(2,1)S(1)}, s16[272,256]{1,0:T(8,128)(2,1)S(1)}, u32[]{:S(2)}, u32[]{:S(2)}) collective-permute-start(s16[272,256]{1,0:T(8,128)(2,1)S(1)} %get-tuple-element.44.rest_0_), channel_id=1, source_target_pairs={{0,1},{1,0},{2,3},{3,2},{4,5},{5,4},{6,7},{7,6},{8,9},{9,8},{10,11... | collective-permute-start | bytes 417800 | tf_op jit(solution)/shard_map/ppermute | solution.py:339
  95.4 7.8 %copy-start.13 = (s16[272,256]{1,0:T(8,128)(2,1)}, s16[272,256]{1,0:T(8,128)(2,1)S(1)}, u32[]{:S(2)}) copy-start(s16[272,256]{1,0:T(8,128)(2,1)S(1)} %collective-permute-done.15.rest_7_) | copy-start | bytes 417796
  95.4 6.9 %collective-permute-start.10 = (s16[272,256]{1,0:T(8,128)(2,1)S(1)}, s16[272,256]{1,0:T(8,128)(2,1)S(1)}, u32[]{:S(2)}, u32[]{:S(2)}) collective-permute-start(s16[272,256]{1,0:T(8,128)(2,1)S(1)} %get-tuple-element.44.rest_0_), channel_id=1, source_target_pairs={{0,2},{1,3},{2,4},{3,5},{4,6},{5,7},{6,0},{7,1},{8,10},{9,11},{10,... | collective-permute-start | bytes 417800 | tf_op jit(solution)/shard_map/ppermute | solution.py:339
  98.1 5.1 %copy-start.14 = (s16[272,256]{1,0:T(8,128)(2,1)}, s16[272,256]{1,0:T(8,128)(2,1)S(1)}, u32[]{:S(2)}) copy-start(s16[272,256]{1,0:T(8,128)(2,1)S(1)} %collective-permute-done.14.rest_6_) | copy-start | bytes 417796
  98.1 5.1 %collective-permute-start.9 = (s16[272,256]{1,0:T(8,128)(2,1)S(1)}, s16[272,256]{1,0:T(8,128)(2,1)S(1)}, u32[]{:S(2)}, u32[]{:S(2)}) collective-permute-start(s16[272,256]{1,0:T(8,128)(2,1)S(1)} %get-tuple-element.44.rest_0_), channel_id=1, source_target_pairs={{0,6},{1,7},{2,0},{3,1},{4,2},{5,3},{6,4},{7,5},{8,14},{9,15},{10,... | collective-permute-start | bytes 417800 | tf_op jit(solution)/shard_map/ppermute | solution.py:339
  98.7 4.6 %copy-start.15 = (s16[272,256]{1,0:T(8,128)(2,1)}, s16[272,256]{1,0:T(8,128)(2,1)S(1)}, u32[]{:S(2)}) copy-start(s16[272,256]{1,0:T(8,128)(2,1)S(1)} %collective-permute-done.13.rest_5_) | copy-start | bytes 417796
  100.7 2.5 %copy-start.16 = (s16[272,256]{1,0:T(8,128)(2,1)}, s16[272,256]{1,0:T(8,128)(2,1)S(1)}, u32[]{:S(2)}) copy-start(s16[272,256]{1,0:T(8,128)(2,1)S(1)} %collective-permute-done.12.rest_4_) | copy-start | bytes 417796
  101.1 2.1 %copy-start.17 = (s16[272,256]{1,0:T(8,128)(2,1)}, s16[272,256]{1,0:T(8,128)(2,1)S(1)}, u32[]{:S(2)}) copy-start(s16[272,256]{1,0:T(8,128)(2,1)S(1)} %collective-permute-done.11.rest_3_) | copy-start | bytes 417796
  102.2 1.0 copy-start.18
  103.2 0.6 copy-start.19
